TPU v7x, 512 devices: a whole 4x8x8 slice. The times are simulated.
512 devices in a mesh: member: 4 (over x_lo, core), gx: 16 (over x_hi, y), gy: 8 (over z).
Axes of the slice: x: 4 (x_hi: 2, x_lo: 2; x = x_hi * 2 + x_lo), y: 8, z: 8, core: 2. Of those that a mesh axis runs over, the one named last changes fastest.
Arguments:
- forcing: float32 [4, 2, 512, 1024], P('member', None, 'gx', 'gy'), may hold values from -6 to 6
- strength: float32 [64, 128], P('gx', 'gy'), may hold values from 0.3 to 2
- mask: int32 [512, 1024], P('gx', 'gy'), may hold values 0 or 1
- send_cell: int32 [4, 16, 8, 4096], P('member', 'gx', 'gy'), may hold values from 0 to 4095, as said below
- send_code: int32 [4, 16, 8, 4096], P('member', 'gx', 'gy'), may hold values from 0 to 16
- recv_buoy: int32 [4, 16, 8, 4096], P('member', 'gx', 'gy'), may hold values from 0 to 255
- observed: float32 [4, 16, 8, 2, 256], P('member', 'gx', 'gy'), may hold values from -6 to 6
Outputs:
- misfit: float32 [4, 16, 8, 2, 256], P('member', 'gx', 'gy')
- gradient: float32 [64, 128], P('gx', 'gy')
Inputs may be any that keep to these rules, and one draw needn't show every extreme that they name: `send_cell`: a cell index of the sending device's 32 x 128 tile, row-major.
All inputs are finite; a program needn't handle non-finite values. No bound on the sum of `mask` on one device may be relied on, other than what follows from the above.
Results may differ from a plain program's by a relative error of at most 0.0001.
Values sent between devices are 32-bit elements; how exact they have to be, the bound alone decides.
No kernel may reach another device: no remote copies, remote signals or barrier semaphores. Data moves between devices by JAX's collectives and lax.ppermute only.
A program may use at most 64 MiB of HBM per device.

v0:
```python
import jax
import jax.numpy as jnp
from jax import lax
from jax.sharding import PartitionSpec as P

SUBCYCLES = 8
BUOYS = 256


visc_scale = 0.2
relax = 0.6
step_size = 0.2
damping = 0.7


def from_behind(x, axis, by):
    count = lax.axis_size(axis)
    pairs = [(i, i + by) for i in range(count) if 0 <= i + by < count]
    return lax.ppermute(x, axis, pairs)


def split_step(velocity, stress, visc, cover, tau):
    upper_x = from_behind(velocity[:, :1, :], "gx", -1)
    upper_y = from_behind(velocity[:, :, :1], "gy", -1)
    next_x = jnp.concatenate([velocity[:, 1:, :], upper_x], axis=1)
    next_y = jnp.concatenate([velocity[:, :, 1:], upper_y], axis=2)
    strain_x = next_x[0] - velocity[0]
    strain_y = next_y[1] - velocity[1]
    shear_rate = next_y[0] - velocity[0] + (next_x[1] - velocity[1])
    first = relax * stress[0] + visc * (strain_x + strain_y)
    second = relax * stress[1] + 0.25 * visc * (strain_x - strain_y)
    third = relax * stress[2] + 0.25 * visc * shear_rate
    combos = jnp.stack([0.5 * (first + second), 0.5 * (first - second), third])
    lower_x = from_behind(combos[:, -1:, :], "gx", 1)
    lower_y = from_behind(combos[:, :, -1:], "gy", 1)
    prev_x = jnp.concatenate([lower_x, combos[:, :-1, :]], axis=1)
    prev_y = jnp.concatenate([lower_y, combos[:, :, :-1]], axis=2)
    force_x = combos[0] - prev_x[0] + combos[2] - prev_y[2]
    force_y = combos[1] - prev_y[1] + combos[2] - prev_x[2]
    forces = jnp.stack([force_x, force_y])
    velocity = cover * (damping * velocity + step_size * (forces + tau))
    return (
        velocity,
        jnp.stack([first, second, third]),
        jnp.stack([strain_x, strain_y, shear_rate]),
    )


def adjoint_step(adj_vel, adj_stress, rates, visc, cover):
    scaled = cover * step_size * adj_vel
    upper_x = from_behind(scaled[:, :1, :], "gx", -1)
    upper_y = from_behind(scaled[:, :, :1], "gy", -1)
    next_x = jnp.concatenate([scaled[:, 1:, :], upper_x], axis=1)
    next_y = jnp.concatenate([scaled[:, :, 1:], upper_y], axis=2)
    adj_nx = scaled[0] - next_x[0]
    adj_ny = scaled[1] - next_y[1]
    adj_third = scaled[0] - next_y[0] + scaled[1] - next_x[1]
    total_one = adj_stress[0] + 0.5 * (adj_nx + adj_ny)
    total_two = adj_stress[1] + 0.5 * (adj_nx - adj_ny)
    total_three = adj_stress[2] + adj_third
    dvisc = (
        total_one * (rates[0] + rates[1])
        + 0.25 * total_two * (rates[0] - rates[1])
        + 0.25 * total_three * rates[2]
    )
    adj_rates = jnp.stack(
        [
            visc * (total_one + 0.25 * total_two),
            visc * (total_one - 0.25 * total_two),
            0.25 * visc * total_three,
        ]
    )
    lower_x = from_behind(adj_rates[:, -1:, :], "gx", 1)
    lower_y = from_behind(adj_rates[:, :, -1:], "gy", 1)
    prev_x = jnp.concatenate([lower_x, adj_rates[:, :-1, :]], axis=1)
    prev_y = jnp.concatenate([lower_y, adj_rates[:, :, :-1]], axis=2)
    adj_east = (
        cover * damping * adj_vel[0] + (prev_x[0] - adj_rates[0]) + (prev_y[2] - adj_rates[2])
    )
    adj_north = (
        cover * damping * adj_vel[1] + (prev_y[1] - adj_rates[1]) + (prev_x[2] - adj_rates[2])
    )
    return (
        jnp.stack([adj_east, adj_north]),
        relax * jnp.stack([total_one, total_two, total_three]),
        dvisc,
    )


def per_device(forcing, strength, mask, send_cell, send_code, recv_buoy, observed):
    tau = forcing[0]
    rows_x = tau.shape[1]
    rows_y = tau.shape[2]
    owners = lax.axis_size("gy")
    cover = mask.astype(jnp.float32)
    fine = jnp.repeat(jnp.repeat(strength, 8, axis=0), 8, axis=1)
    visc = visc_scale * fine * cover
    velocity = jnp.zeros((2, rows_x, rows_y), jnp.float32)
    stress = jnp.zeros((3, rows_x, rows_y), jnp.float32)
    kept = []
    for step in range(SUBCYCLES):
        velocity, stress, rates = split_step(velocity, stress, visc, cover, tau)
        kept.append(rates)
    cells = send_cell[0, 0, 0]
    weights = send_code[0, 0, 0].astype(jnp.float32) / 16.0
    slots = recv_buoy[0, 0, 0]
    entries = cells.shape[0]
    flat = velocity.reshape(2, rows_x * rows_y)
    partial_value = (flat[:, cells] * weights[None, :]).reshape(2, owners, entries // owners)
    received = lax.all_to_all(partial_value, "gy", split_axis=1, concat_axis=1, tiled=True).reshape(
        2, entries
    )
    summed = jax.ops.segment_sum(received.T, slots, num_segments=BUOYS).T
    misfit = summed - observed[0, 0, 0]
    back = misfit[:, slots].reshape(2, owners, entries // owners)
    returned = lax.all_to_all(back, "gy", split_axis=1, concat_axis=1, tiled=True).reshape(
        2, entries
    )
    adj_flat = jax.ops.segment_sum(
        (returned * weights[None, :]).T, cells, num_segments=rows_x * rows_y
    ).T
    adj_vel = adj_flat.reshape(2, rows_x, rows_y)
    adj_stress = jnp.zeros((3, rows_x, rows_y), jnp.float32)
    fine_grad = jnp.zeros((rows_x, rows_y), jnp.float32)
    for step in range(SUBCYCLES - 1, -1, -1):
        adj_vel, adj_stress, dvisc = adjoint_step(adj_vel, adj_stress, kept[step], visc, cover)
        fine_grad = fine_grad + dvisc
    fine_grad = visc_scale * cover * fine_grad
    coarse = fine_grad.reshape(rows_x // 8, 8, rows_y // 8, 8).sum(axis=(1, 3))
    gradient = lax.psum(coarse, "member")
    return (misfit[None, None, None], gradient)


def solution(mesh):
    return jax.shard_map(
        per_device,
        mesh=mesh,
        in_specs=(
            P("member", None, "gx", "gy"),
            P("gx", "gy"),
            P("gx", "gy"),
            P("member", "gx", "gy", None),
            P("member", "gx", "gy", None),
            P("member", "gx", "gy", None),
            P("member", "gx", "gy", None, None),
        ),
        out_specs=(P("member", "gx", "gy", None, None), P("gx", "gy")),
        check_vma=False,
    )
```

profile of v0, /device:TPU:7, one launch (start us, length us, event | category | flops | bytes accessed | tf_op | source)
XLA Modules:
  0.0 436.9 jit_solution(3924389111148507190)
XLA Ops:
  2.0 5.9 %collective-permute-start = (f32[2,1,128]{2,1,0:T(1,128)S(1)}, f32[2,1,128]{2,1,0:T(1,128)S(1)}, u32[]{:S(2)}, u32[]{:S(2)}) collective-permute-start(f32[2,1,128]{2,1,0:T(1,128)S(1)} %slice.931), channel_id=1, source_target_pairs={{8,0},{16,8},{24,16},{32,24},{40,32},{48,40},{56,48},{64,56},{72,6... | collective-permute-start | bytes 3080 | tf_op jit(solution)/shard_map/ppermute | solution.py:19
  11.7 4.6 %collective-permute-start.3 = (f32[3,32,1]{2,1,0:T(8,128)S(1)}, f32[3,32,1]{2,1,0:T(8,128)S(1)}, u32[]{:S(2)}, u32[]{:S(2)}) collective-permute-start(f32[3,32,1]{2,1,0:T(8,128)S(1)} %slice.1235), channel_id=1, source_target_pairs={{0,1},{1,2},{2,3},{3,4},{4,5},{5,6},{6,7},{8,9},{9,10},{10,11},{11... | collective-permute-start | bytes 1160 | tf_op jit(solution)/shard_map/ppermute | solution.py:19
  18.5 6.8 %collective-permute-start.4 = (f32[2,1,128]{2,1,0:T(1,128)S(1)}, f32[2,1,128]{2,1,0:T(1,128)S(1)}, u32[]{:S(2)}, u32[]{:S(2)}) collective-permute-start(f32[2,1,128]{2,1,0:T(1,128)S(1)} %slice.1238), channel_id=1, source_target_pairs={{8,0},{16,8},{24,16},{32,24},{40,32},{48,40},{56,48},{64,56},{72,6... | collective-permute-start | bytes 3080 | tf_op jit(solution)/shard_map/ppermute | solution.py:19
  26.8 3.9 collective-permute-done.5
  30.8 1.9 collective-permute-start.6
  32.8 4.0 collective-permute-start.7
  38.9 6.2 %collective-permute-start.8 = (f32[2,1,128]{2,1,0:T(1,128)S(1)}, f32[2,1,128]{2,1,0:T(1,128)S(1)}, u32[]{:S(2)}, u32[]{:S(2)}) collective-permute-start(f32[2,1,128]{2,1,0:T(1,128)S(1)} %slice.1251), channel_id=1, source_target_pairs={{8,0},{16,8},{24,16},{32,24},{40,32},{48,40},{56,48},{64,56},{72,6... | collective-permute-start | bytes 3080 | tf_op jit(solution)/shard_map/ppermute | solution.py:19
  46.5 5.1 %collective-permute-done.9 = f32[2,32,1]{2,1,0:T(8,128)S(1)} collective-permute-done((f32[2,32,1]{2,1,0:T(8,128)S(1)}, f32[2,32,1]{2,1,0:T(8,128)S(1)}, u32[]{:S(2)}, u32[]{:S(2)}) %collective-permute-start.9) | collective-permute-done | bytes 288 | tf_op jit(solution)/shard_map/ppermute | solution.py:19
  53.7 4.9 %collective-permute-start.11 = (f32[3,32,1]{2,1,0:T(8,128)S(1)}, f32[3,32,1]{2,1,0:T(8,128)S(1)}, u32[]{:S(2)}, u32[]{:S(2)}) collective-permute-start(f32[3,32,1]{2,1,0:T(8,128)S(1)} %slice.1261), channel_id=1, source_target_pairs={{0,1},{1,2},{2,3},{3,4},{4,5},{5,6},{6,7},{8,9},{9,10},{10,11},{11... | collective-permute-start | bytes 1160 | tf_op jit(solution)/shard_map/ppermute | solution.py:19
  59.9 7.0 %collective-permute-start.12 = (f32[2,1,128]{2,1,0:T(1,128)S(1)}, f32[2,1,128]{2,1,0:T(1,128)S(1)}, u32[]{:S(2)}, u32[]{:S(2)}) collective-permute-start(f32[2,1,128]{2,1,0:T(1,128)S(1)} %slice.1264), channel_id=1, source_target_pairs={{8,0},{16,8},{24,16},{32,24},{40,32},{48,40},{56,48},{64,56},{72,6... | collective-permute-start | bytes 3080 | tf_op jit(solution)/shard_map/ppermute | solution.py:19
  68.3 3.6 collective-permute-done.13
  74.0 4.6 %collective-permute-start.15 = (f32[3,32,1]{2,1,0:T(8,128)S(1)}, f32[3,32,1]{2,1,0:T(8,128)S(1)}, u32[]{:S(2)}, u32[]{:S(2)}) collective-permute-start(f32[3,32,1]{2,1,0:T(8,128)S(1)} %slice.1274), channel_id=1, source_target_pairs={{0,1},{1,2},{2,3},{3,4},{4,5},{5,6},{6,7},{8,9},{9,10},{10,11},{11... | collective-permute-start | bytes 1160 | tf_op jit(solution)/shard_map/ppermute | solution.py:19
  80.0 6.8 %collective-permute-start.16 = (f32[2,1,128]{2,1,0:T(1,128)S(1)}, f32[2,1,128]{2,1,0:T(1,128)S(1)}, u32[]{:S(2)}, u32[]{:S(2)}) collective-permute-start(f32[2,1,128]{2,1,0:T(1,128)S(1)} %slice.1277), channel_id=1, source_target_pairs={{8,0},{16,8},{24,16},{32,24},{40,32},{48,40},{56,48},{64,56},{72,6... | collective-permute-start | bytes 3080 | tf_op jit(solution)/shard_map/ppermute | solution.py:19
  88.2 3.6 collective-permute-done.17
  93.9 4.6 %collective-permute-start.19 = (f32[3,32,1]{2,1,0:T(8,128)S(1)}, f32[3,32,1]{2,1,0:T(8,128)S(1)}, u32[]{:S(2)}, u32[]{:S(2)}) collective-permute-start(f32[3,32,1]{2,1,0:T(8,128)S(1)} %slice.1287), channel_id=1, source_target_pairs={{0,1},{1,2},{2,3},{3,4},{4,5},{5,6},{6,7},{8,9},{9,10},{10,11},{11... | collective-permute-start | bytes 1160 | tf_op jit(solution)/shard_map/ppermute | solution.py:19
  100.0 6.8 %collective-permute-start.20 = (f32[2,1,128]{2,1,0:T(1,128)S(1)}, f32[2,1,128]{2,1,0:T(1,128)S(1)}, u32[]{:S(2)}, u32[]{:S(2)}) collective-permute-start(f32[2,1,128]{2,1,0:T(1,128)S(1)} %slice.1290), channel_id=1, source_target_pairs={{8,0},{16,8},{24,16},{32,24},{40,32},{48,40},{56,48},{64,56},{72,6... | collective-permute-start | bytes 3080 | tf_op jit(solution)/shard_map/ppermute | solution.py:19
  108.2 3.9 collective-permute-done.21
  114.2 4.6 %collective-permute-start.23 = (f32[3,32,1]{2,1,0:T(8,128)S(1)}, f32[3,32,1]{2,1,0:T(8,128)S(1)}, u32[]{:S(2)}, u32[]{:S(2)}) collective-permute-start(f32[3,32,1]{2,1,0:T(8,128)S(1)} %slice.1300), channel_id=1, source_target_pairs={{0,1},{1,2},{2,3},{3,4},{4,5},{5,6},{6,7},{8,9},{9,10},{10,11},{11... | collective-permute-start | bytes 1160 | tf_op jit(solution)/shard_map/ppermute | solution.py:19
  121.5 6.8 %collective-permute-start.24 = (f32[2,1,128]{2,1,0:T(1,128)S(1)}, f32[2,1,128]{2,1,0:T(1,128)S(1)}, u32[]{:S(2)}, u32[]{:S(2)}) collective-permute-start(f32[2,1,128]{2,1,0:T(1,128)S(1)} %slice.1303), channel_id=1, source_target_pairs={{8,0},{16,8},{24,16},{32,24},{40,32},{48,40},{56,48},{64,56},{72,6... | collective-permute-start | bytes 3080 | tf_op jit(solution)/shard_map/ppermute | solution.py:19
  131.2 4.4 %collective-permute-start.27 = (f32[3,32,1]{2,1,0:T(8,128)S(1)}, f32[3,32,1]{2,1,0:T(8,128)S(1)}, u32[]{:S(2)}, u32[]{:S(2)}) collective-permute-start(f32[3,32,1]{2,1,0:T(8,128)S(1)} %slice.1313), channel_id=1, source_target_pairs={{0,1},{1,2},{2,3},{3,4},{4,5},{5,6},{6,7},{8,9},{9,10},{10,11},{11... | collective-permute-start | bytes 1160 | tf_op jit(solution)/shard_map/ppermute | solution.py:19
  138.7 6.6 %collective-permute-start.28 = (f32[2,1,128]{2,1,0:T(1,128)S(1)}, f32[2,1,128]{2,1,0:T(1,128)S(1)}, u32[]{:S(2)}, u32[]{:S(2)}) collective-permute-start(f32[2,1,128]{2,1,0:T(1,128)S(1)} %slice.1316), channel_id=1, source_target_pairs={{8,0},{16,8},{24,16},{32,24},{40,32},{48,40},{56,48},{64,56},{72,6... | collective-permute-start | bytes 3080 | tf_op jit(solution)/shard_map/ppermute | solution.py:19
  148.2 5.4 %collective-permute-start.31 = (f32[3,32,1]{2,1,0:T(8,128)S(1)}, f32[3,32,1]{2,1,0:T(8,128)S(1)}, u32[]{:S(2)}, u32[]{:S(2)}) collective-permute-start(f32[3,32,1]{2,1,0:T(8,128)S(1)} %slice.1326), channel_id=1, source_target_pairs={{0,1},{1,2},{2,3},{3,4},{4,5},{5,6},{6,7},{8,9},{9,10},{10,11},{11... | collective-permute-start | bytes 1160 | tf_op jit(solution)/shard_map/ppermute | solution.py:19
  155.8 14.1 %gather_fusion = f32[4096,2]{1,0:T(8,128)} fusion(f32[2,4096]{0,1:T(8,128)S(1)} %copy.113, s32[4096]{0:T(1024)S(1)} %broadcast_clamp_fusion.1), kind=kCustom, calls=%fused_computation | custom fusion | bytes 81920 | tf_op jit(solution)/shard_map/gather | solution.py:109
  169.9 2.2 copy.114
  172.8 11.5 %all-to-all-start = ((f32[2,8,512]{2,0,1:T(2,128)}), f32[2,8,512]{2,0,1:T(2,128)S(1)}, u32[]{:S(2)}, u32[]{:S(2)}) async-start(f32[2,8,512]{2,0,1:T(2,128)} %broadcast_multiply_fusion), calls=%async_computation | async-start | bytes 65536 | tf_op jit(solution)/shard_map/all_to_all | solution.py:110
  184.5 6.7 %all-to-all-done = f32[2,8,512]{2,0,1:T(2,128)S(1)} async-done(((f32[2,8,512]{2,0,1:T(2,128)}), f32[2,8,512]{2,0,1:T(2,128)S(1)}, u32[]{:S(2)}, u32[]{:S(2)}) %all-to-all-start) | async-done | bytes 32800 | tf_op jit(solution)/shard_map/all_to_all | solution.py:110
  191.8 22.4 %scatter_custom_fusion = f32[256,2]{1,0:T(8,128)S(1)} fusion(s32[4096]{0:T(1024)S(1)} %bitcast.1306, f32[4096,2]{1,0:T(8,128)S(1)} %copy.115, f32[]{:T(128)} %constant.11.clone.1), kind=kCustom, calls=%fused_computation.11 | custom fusion | flops 8192 | bytes 2052 | tf_op jit(solution)/shard_map/scatter-add | solution.py:113
  214.3 10.8 %gather_fusion.1 = f32[4096,2]{1,0:T(8,128)S(1)} fusion(f32[2,256]{0,1:T(8,128)S(1)} %bitcast_subtract_fusion, s32[4096]{0:T(1024)S(1)} %broadcast_clamp_fusion), kind=kCustom, calls=%fused_computation.1 | custom fusion | bytes 81920 | tf_op jit(solution)/shard_map/gather | solution.py:115
  225.7 9.2 %all_to_all.10 = f32[2,8,512]{2,0,1:T(2,128)S(1)} all-to-all(f32[2,8,512]{2,0,1:T(2,128)S(1)} %copy.117), channel_id=1, replica_groups=mesh['member'=4,'gx'=16,'gy'=8] {'gy'}, dimensions={1} | all-to-all | bytes 65536 | tf_op jit(solution)/shard_map/all_to_all | solution.py:116
  234.9 2.0 copy.118
  236.9 23.2 %scatter_custom_fusion.1 = f32[4096,2]{1,0:T(8,128)S(1)} fusion(s32[4096]{0:T(1024)S(1)} %bitcast.1307, f32[4096,2]{1,0:T(8,128)} %copy.118, f32[]{:T(128)} %constant.11.clone.1), kind=kCustom, calls=%fused_computation.6 | custom fusion | flops 8192 | bytes 33280 | tf_op jit(solution)/shard_map/scatter-add | solution.py:119
  260.7 7.0 %collective-permute-start.32 = (f32[2,1,128]{2,1,0:T(1,128)S(1)}, f32[2,1,128]{2,1,0:T(1,128)S(1)}, u32[]{:S(2)}, u32[]{:S(2)}) collective-permute-start(f32[2,1,128]{2,1,0:T(1,128)S(1)} %slice.1330), channel_id=1, source_target_pairs={{8,0},{16,8},{24,16},{32,24},{40,32},{48,40},{56,48},{64,56},{72,6... | collective-permute-start | bytes 3080 | tf_op jit(solution)/shard_map/ppermute | solution.py:19
  269.1 3.3 collective-permute-done.33
  274.6 2.4 collective-permute-start.35
  282.0 5.2 %collective-permute-start.36 = (f32[2,1,128]{2,1,0:T(1,128)S(1)}, f32[2,1,128]{2,1,0:T(1,128)S(1)}, u32[]{:S(2)}, u32[]{:S(2)}) collective-permute-start(f32[2,1,128]{2,1,0:T(1,128)S(1)} %slice.1346), channel_id=1, source_target_pairs={{8,0},{16,8},{24,16},{32,24},{40,32},{48,40},{56,48},{64,56},{72,6... | collective-permute-start | bytes 3080 | tf_op jit(solution)/shard_map/ppermute | solution.py:19
  290.1 4.0 collective-permute-start.39
  297.6 6.2 %collective-permute-start.40 = (f32[2,1,128]{2,1,0:T(1,128)S(1)}, f32[2,1,128]{2,1,0:T(1,128)S(1)}, u32[]{:S(2)}, u32[]{:S(2)}) collective-permute-start(f32[2,1,128]{2,1,0:T(1,128)S(1)} %slice.1362), channel_id=1, source_target_pairs={{8,0},{16,8},{24,16},{32,24},{40,32},{48,40},{56,48},{64,56},{72,6... | collective-permute-start | bytes 3080 | tf_op jit(solution)/shard_map/ppermute | solution.py:19
  306.8 4.3 collective-permute-start.43
  314.3 6.5 %collective-permute-start.44 = (f32[2,1,128]{2,1,0:T(1,128)S(1)}, f32[2,1,128]{2,1,0:T(1,128)S(1)}, u32[]{:S(2)}, u32[]{:S(2)}) collective-permute-start(f32[2,1,128]{2,1,0:T(1,128)S(1)} %slice.1378), channel_id=1, source_target_pairs={{8,0},{16,8},{24,16},{32,24},{40,32},{48,40},{56,48},{64,56},{72,6... | collective-permute-start | bytes 3080 | tf_op jit(solution)/shard_map/ppermute | solution.py:19
  323.7 4.3 collective-permute-start.47
  331.3 6.5 %collective-permute-start.48 = (f32[2,1,128]{2,1,0:T(1,128)S(1)}, f32[2,1,128]{2,1,0:T(1,128)S(1)}, u32[]{:S(2)}, u32[]{:S(2)}) collective-permute-start(f32[2,1,128]{2,1,0:T(1,128)S(1)} %slice.1394), channel_id=1, source_target_pairs={{8,0},{16,8},{24,16},{32,24},{40,32},{48,40},{56,48},{64,56},{72,6... | collective-permute-start | bytes 3080 | tf_op jit(solution)/shard_map/ppermute | solution.py:19
  340.7 4.3 collective-permute-start.51
  348.3 6.5 %collective-permute-start.52 = (f32[2,1,128]{2,1,0:T(1,128)S(1)}, f32[2,1,128]{2,1,0:T(1,128)S(1)}, u32[]{:S(2)}, u32[]{:S(2)}) collective-permute-start(f32[2,1,128]{2,1,0:T(1,128)S(1)} %slice.1410), channel_id=1, source_target_pairs={{8,0},{16,8},{24,16},{32,24},{40,32},{48,40},{56,48},{64,56},{72,6... | collective-permute-start | bytes 3080 | tf_op jit(solution)/shard_map/ppermute | solution.py:19
  357.7 4.3 collective-permute-start.55
  365.3 6.5 %collective-permute-start.56 = (f32[2,1,128]{2,1,0:T(1,128)S(1)}, f32[2,1,128]{2,1,0:T(1,128)S(1)}, u32[]{:S(2)}, u32[]{:S(2)}) collective-permute-start(f32[2,1,128]{2,1,0:T(1,128)S(1)} %slice.1426), channel_id=1, source_target_pairs={{8,0},{16,8},{24,16},{32,24},{40,32},{48,40},{56,48},{64,56},{72,6... | collective-permute-start | bytes 3080 | tf_op jit(solution)/shard_map/ppermute | solution.py:19
  374.7 5.7 %collective-permute-start.59 = (f32[3,32,1]{2,1,0:T(8,128)S(1)}, f32[3,32,1]{2,1,0:T(8,128)S(1)}, u32[]{:S(2)}, u32[]{:S(2)}) collective-permute-start(f32[3,32,1]{2,1,0:T(8,128)S(1)} %slice.1438), channel_id=1, source_target_pairs={{0,1},{1,2},{2,3},{3,4},{4,5},{5,6},{6,7},{8,9},{9,10},{10,11},{11... | collective-permute-start | bytes 1160 | tf_op jit(solution)/shard_map/ppermute | solution.py:19
  383.0 7.2 %collective-permute-start.60 = (f32[2,1,128]{2,1,0:T(1,128)S(1)}, f32[2,1,128]{2,1,0:T(1,128)S(1)}, u32[]{:S(2)}, u32[]{:S(2)}) collective-permute-start(f32[2,1,128]{2,1,0:T(1,128)S(1)} %slice.1442), channel_id=1, source_target_pairs={{8,0},{16,8},{24,16},{32,24},{40,32},{48,40},{56,48},{64,56},{72,6... | collective-permute-start | bytes 3080 | tf_op jit(solution)/shard_map/ppermute | solution.py:19
  391.3 45.5 %psum.7 = f32[4,16]{1,0:T(4,128)} all-reduce(f32[4,16]{1,0:T(4,128)S(1)} %reduce_sum.9), channel_id=1, replica_groups=mesh['member'=4,'gx'=16,'gy'=8] {'member'}, use_global_device_ids=true, to_apply=%region_3.0 | all-reduce | flops 64 | bytes 512 | tf_op jit(solution)/shard_map/psum | solution.py:130
  (285 shorter events, 91.1 us)
Async XLA Ops:
  0.7 8.1 %collective-permute-start.1 = (f32[2,32,1]{2,1,0:T(8,128)S(1)}, f32[2,32,1]{2,1,0:T(8,128)S(1)}, u32[]{:S(2)}, u32[]{:S(2)}) collective-permute-start(f32[2,32,1]{2,1,0:T(8,128)S(1)} %slice.933), channel_id=1, source_target_pairs={{1,0},{2,1},{3,2},{4,3},{5,4},{6,5},{7,6},{9,8},{10,9},{11,10},{12... | collective-permute-start | bytes 776 | tf_op jit(solution)/shard_map/ppermute | solution.py:19
  2.0 6.8 %collective-permute-start = (f32[2,1,128]{2,1,0:T(1,128)S(1)}, f32[2,1,128]{2,1,0:T(1,128)S(1)}, u32[]{:S(2)}, u32[]{:S(2)}) collective-permute-start(f32[2,1,128]{2,1,0:T(1,128)S(1)} %slice.931), channel_id=1, source_target_pairs={{8,0},{16,8},{24,16},{32,24},{40,32},{48,40},{56,48},{64,56},{72,6... | collective-permute-start | bytes 3080 | tf_op jit(solution)/shard_map/ppermute | solution.py:19
  9.7 8.0 %collective-permute-start.2 = (f32[3,1,128]{2,1,0:T(1,128)S(1)}, f32[3,1,128]{2,1,0:T(1,128)S(1)}, u32[]{:S(2)}, u32[]{:S(2)}) collective-permute-start(f32[3,1,128]{2,1,0:T(1,128)S(1)} %pad_maximum_fusion.89), channel_id=1, source_target_pairs={{0,8},{8,16},{16,24},{24,32},{32,40},{40,48},{48,56},{56,64},{64,7... | collective-permute-start | bytes 4616 | tf_op jit(solution)/shard_map/ppermute | solution.py:19
  11.7 5.8 %collective-permute-start.3 = (f32[3,32,1]{2,1,0:T(8,128)S(1)}, f32[3,32,1]{2,1,0:T(8,128)S(1)}, u32[]{:S(2)}, u32[]{:S(2)}) collective-permute-start(f32[3,32,1]{2,1,0:T(8,128)S(1)} %slice.1235), channel_id=1, source_target_pairs={{0,1},{1,2},{2,3},{3,4},{4,5},{5,6},{6,7},{8,9},{9,10},{10,11},{11... | collective-permute-start | bytes 1160 | tf_op jit(solution)/shard_map/ppermute | solution.py:19
  18.5 12.2 %collective-permute-start.4 = (f32[2,1,128]{2,1,0:T(1,128)S(1)}, f32[2,1,128]{2,1,0:T(1,128)S(1)}, u32[]{:S(2)}, u32[]{:S(2)}) collective-permute-start(f32[2,1,128]{2,1,0:T(1,128)S(1)} %slice.1238), channel_id=1, source_target_pairs={{8,0},{16,8},{24,16},{32,24},{40,32},{48,40},{56,48},{64,56},{72,6... | collective-permute-start | bytes 3080 | tf_op jit(solution)/shard_map/ppermute | solution.py:19
  30.8 7.9 %collective-permute-start.6 = (f32[3,1,128]{2,1,0:T(1,128)S(1)}, f32[3,1,128]{2,1,0:T(1,128)S(1)}, u32[]{:S(2)}, u32[]{:S(2)}) collective-permute-start(f32[3,1,128]{2,1,0:T(1,128)S(1)} %pad_maximum_fusion.88), channel_id=1, source_target_pairs={{0,8},{8,16},{16,24},{24,32},{32,40},{40,48},{48,56},{56,64},{64,7... | collective-permute-start | bytes 4616 | tf_op jit(solution)/shard_map/ppermute | solution.py:19
  38.9 12.7 %collective-permute-start.8 = (f32[2,1,128]{2,1,0:T(1,128)S(1)}, f32[2,1,128]{2,1,0:T(1,128)S(1)}, u32[]{:S(2)}, u32[]{:S(2)}) collective-permute-start(f32[2,1,128]{2,1,0:T(1,128)S(1)} %slice.1251), channel_id=1, source_target_pairs={{8,0},{16,8},{24,16},{32,24},{40,32},{48,40},{56,48},{64,56},{72,6... | collective-permute-start | bytes 3080 | tf_op jit(solution)/shard_map/ppermute | solution.py:19
  45.1 6.5 %collective-permute-start.9 = (f32[2,32,1]{2,1,0:T(8,128)S(1)}, f32[2,32,1]{2,1,0:T(8,128)S(1)}, u32[]{:S(2)}, u32[]{:S(2)}) collective-permute-start(f32[2,32,1]{2,1,0:T(8,128)S(1)} %bitcast.1196), channel_id=1, source_target_pairs={{1,0},{2,1},{3,2},{4,3},{5,4},{6,5},{7,6},{9,8},{10,9},{11,10},{12... | collective-permute-start | bytes 776 | tf_op jit(solution)/shard_map/ppermute | solution.py:19
  51.7 8.1 %collective-permute-start.10 = (f32[3,1,128]{2,1,0:T(1,128)S(1)}, f32[3,1,128]{2,1,0:T(1,128)S(1)}, u32[]{:S(2)}, u32[]{:S(2)}) collective-permute-start(f32[3,1,128]{2,1,0:T(1,128)S(1)} %pad_maximum_fusion.87), channel_id=1, source_target_pairs={{0,8},{8,16},{16,24},{24,32},{32,40},{40,48},{48,56},{56,64},{64,7... | collective-permute-start | bytes 4616 | tf_op jit(solution)/shard_map/ppermute | solution.py:19
  53.7 6.0 %collective-permute-start.11 = (f32[3,32,1]{2,1,0:T(8,128)S(1)}, f32[3,32,1]{2,1,0:T(8,128)S(1)}, u32[]{:S(2)}, u32[]{:S(2)}) collective-permute-start(f32[3,32,1]{2,1,0:T(8,128)S(1)} %slice.1261), channel_id=1, source_target_pairs={{0,1},{1,2},{2,3},{3,4},{4,5},{5,6},{6,7},{8,9},{9,10},{10,11},{11... | collective-permute-start | bytes 1160 | tf_op jit(solution)/shard_map/ppermute | solution.py:19
  59.9 12.0 %collective-permute-start.12 = (f32[2,1,128]{2,1,0:T(1,128)S(1)}, f32[2,1,128]{2,1,0:T(1,128)S(1)}, u32[]{:S(2)}, u32[]{:S(2)}) collective-permute-start(f32[2,1,128]{2,1,0:T(1,128)S(1)} %slice.1264), channel_id=1, source_target_pairs={{8,0},{16,8},{24,16},{32,24},{40,32},{48,40},{56,48},{64,56},{72,6... | collective-permute-start | bytes 3080 | tf_op jit(solution)/shard_map/ppermute | solution.py:19
  72.0 7.9 %collective-permute-start.14 = (f32[3,1,128]{2,1,0:T(1,128)S(1)}, f32[3,1,128]{2,1,0:T(1,128)S(1)}, u32[]{:S(2)}, u32[]{:S(2)}) collective-permute-start(f32[3,1,128]{2,1,0:T(1,128)S(1)} %pad_maximum_fusion.86), channel_id=1, source_target_pairs={{0,8},{8,16},{16,24},{24,32},{32,40},{40,48},{48,56},{56,64},{64,7... | collective-permute-start | bytes 4616 | tf_op jit(solution)/shard_map/ppermute | solution.py:19
  74.0 5.7 %collective-permute-start.15 = (f32[3,32,1]{2,1,0:T(8,128)S(1)}, f32[3,32,1]{2,1,0:T(8,128)S(1)}, u32[]{:S(2)}, u32[]{:S(2)}) collective-permute-start(f32[3,32,1]{2,1,0:T(8,128)S(1)} %slice.1274), channel_id=1, source_target_pairs={{0,1},{1,2},{2,3},{3,4},{4,5},{5,6},{6,7},{8,9},{9,10},{10,11},{11... | collective-permute-start | bytes 1160 | tf_op jit(solution)/shard_map/ppermute | solution.py:19
  80.0 11.8 %collective-permute-start.16 = (f32[2,1,128]{2,1,0:T(1,128)S(1)}, f32[2,1,128]{2,1,0:T(1,128)S(1)}, u32[]{:S(2)}, u32[]{:S(2)}) collective-permute-start(f32[2,1,128]{2,1,0:T(1,128)S(1)} %slice.1277), channel_id=1, source_target_pairs={{8,0},{16,8},{24,16},{32,24},{40,32},{48,40},{56,48},{64,56},{72,6... | collective-permute-start | bytes 3080 | tf_op jit(solution)/shard_map/ppermute | solution.py:19
  91.9 7.9 %collective-permute-start.18 = (f32[3,1,128]{2,1,0:T(1,128)S(1)}, f32[3,1,128]{2,1,0:T(1,128)S(1)}, u32[]{:S(2)}, u32[]{:S(2)}) collective-permute-start(f32[3,1,128]{2,1,0:T(1,128)S(1)} %pad_maximum_fusion.85), channel_id=1, source_target_pairs={{0,8},{8,16},{16,24},{24,32},{32,40},{40,48},{48,56},{56,64},{64,7... | collective-permute-start | bytes 4616 | tf_op jit(solution)/shard_map/ppermute | solution.py:19
  100.0 12.1 %collective-permute-start.20 = (f32[2,1,128]{2,1,0:T(1,128)S(1)}, f32[2,1,128]{2,1,0:T(1,128)S(1)}, u32[]{:S(2)}, u32[]{:S(2)}) collective-permute-start(f32[2,1,128]{2,1,0:T(1,128)S(1)} %slice.1290), channel_id=1, source_target_pairs={{8,0},{16,8},{24,16},{32,24},{40,32},{48,40},{56,48},{64,56},{72,6... | collective-permute-start | bytes 3080 | tf_op jit(solution)/shard_map/ppermute | solution.py:19
  112.2 7.9 %collective-permute-start.22 = (f32[3,1,128]{2,1,0:T(1,128)S(1)}, f32[3,1,128]{2,1,0:T(1,128)S(1)}, u32[]{:S(2)}, u32[]{:S(2)}) collective-permute-start(f32[3,1,128]{2,1,0:T(1,128)S(1)} %pad_maximum_fusion.84), channel_id=1, source_target_pairs={{0,8},{8,16},{16,24},{24,32},{32,40},{40,48},{48,56},{56,64},{64,7... | collective-permute-start | bytes 4616 | tf_op jit(solution)/shard_map/ppermute | solution.py:19
  120.2 8.2 %collective-permute-start.25 = (f32[2,32,1]{2,1,0:T(8,128)S(1)}, f32[2,32,1]{2,1,0:T(8,128)S(1)}, u32[]{:S(2)}, u32[]{:S(2)}) collective-permute-start(f32[2,32,1]{2,1,0:T(8,128)S(1)} %bitcast.1204), channel_id=1, source_target_pairs={{1,0},{2,1},{3,2},{4,3},{5,4},{6,5},{7,6},{9,8},{10,9},{11,10},{12... | collective-permute-start | bytes 776 | tf_op jit(solution)/shard_map/ppermute | solution.py:19
  121.5 7.5 %collective-permute-start.24 = (f32[2,1,128]{2,1,0:T(1,128)S(1)}, f32[2,1,128]{2,1,0:T(1,128)S(1)}, u32[]{:S(2)}, u32[]{:S(2)}) collective-permute-start(f32[2,1,128]{2,1,0:T(1,128)S(1)} %slice.1303), channel_id=1, source_target_pairs={{8,0},{16,8},{24,16},{32,24},{40,32},{48,40},{56,48},{64,56},{72,6... | collective-permute-start | bytes 3080 | tf_op jit(solution)/shard_map/ppermute | solution.py:19
  129.1 8.2 %collective-permute-start.26 = (f32[3,1,128]{2,1,0:T(1,128)S(1)}, f32[3,1,128]{2,1,0:T(1,128)S(1)}, u32[]{:S(2)}, u32[]{:S(2)}) collective-permute-start(f32[3,1,128]{2,1,0:T(1,128)S(1)} %pad_maximum_fusion.83), channel_id=1, source_target_pairs={{0,8},{8,16},{16,24},{24,32},{32,40},{40,48},{48,56},{56,64},{64,7... | collective-permute-start | bytes 4616 | tf_op jit(solution)/shard_map/ppermute | solution.py:19
  137.4 8.0 %collective-permute-start.29 = (f32[2,32,1]{2,1,0:T(8,128)S(1)}, f32[2,32,1]{2,1,0:T(8,128)S(1)}, u32[]{:S(2)}, u32[]{:S(2)}) collective-permute-start(f32[2,32,1]{2,1,0:T(8,128)S(1)} %bitcast.1240), channel_id=1, source_target_pairs={{1,0},{2,1},{3,2},{4,3},{5,4},{6,5},{7,6},{9,8},{10,9},{11,10},{12... | collective-permute-start | bytes 776 | tf_op jit(solution)/shard_map/ppermute | solution.py:19
  138.7 7.3 %collective-permute-start.28 = (f32[2,1,128]{2,1,0:T(1,128)S(1)}, f32[2,1,128]{2,1,0:T(1,128)S(1)}, u32[]{:S(2)}, u32[]{:S(2)}) collective-permute-start(f32[2,1,128]{2,1,0:T(1,128)S(1)} %slice.1316), channel_id=1, source_target_pairs={{8,0},{16,8},{24,16},{32,24},{40,32},{48,40},{56,48},{64,56},{72,6... | collective-permute-start | bytes 3080 | tf_op jit(solution)/shard_map/ppermute | solution.py:19
  146.2 8.5 %collective-permute-start.30 = (f32[3,1,128]{2,1,0:T(1,128)S(1)}, f32[3,1,128]{2,1,0:T(1,128)S(1)}, u32[]{:S(2)}, u32[]{:S(2)}) collective-permute-start(f32[3,1,128]{2,1,0:T(1,128)S(1)} %pad_maximum_fusion.82), channel_id=1, source_target_pairs={{0,8},{8,16},{16,24},{24,32},{32,40},{40,48},{48,56},{56,64},{64,7... | collective-permute-start | bytes 4616 | tf_op jit(solution)/shard_map/ppermute | solution.py:19
  148.2 6.5 %collective-permute-start.31 = (f32[3,32,1]{2,1,0:T(8,128)S(1)}, f32[3,32,1]{2,1,0:T(8,128)S(1)}, u32[]{:S(2)}, u32[]{:S(2)}) collective-permute-start(f32[3,32,1]{2,1,0:T(8,128)S(1)} %slice.1326), channel_id=1, source_target_pairs={{0,1},{1,2},{2,3},{3,4},{4,5},{5,6},{6,7},{8,9},{9,10},{10,11},{11... | collective-permute-start | bytes 1160 | tf_op jit(solution)/shard_map/ppermute | solution.py:19
  172.8 18.4 %all-to-all-start = ((f32[2,8,512]{2,0,1:T(2,128)}), f32[2,8,512]{2,0,1:T(2,128)S(1)}, u32[]{:S(2)}, u32[]{:S(2)}) async-start(f32[2,8,512]{2,0,1:T(2,128)} %broadcast_multiply_fusion), calls=%async_computation | async-start | bytes 65536 | tf_op jit(solution)/shard_map/all_to_all | solution.py:110
  260.7 11.7 %collective-permute-start.32 = (f32[2,1,128]{2,1,0:T(1,128)S(1)}, f32[2,1,128]{2,1,0:T(1,128)S(1)}, u32[]{:S(2)}, u32[]{:S(2)}) collective-permute-start(f32[2,1,128]{2,1,0:T(1,128)S(1)} %slice.1330), channel_id=1, source_target_pairs={{8,0},{16,8},{24,16},{32,24},{40,32},{48,40},{56,48},{64,56},{72,6... | collective-permute-start | bytes 3080 | tf_op jit(solution)/shard_map/ppermute | solution.py:19
  272.6 7.9 %collective-permute-start.34 = (f32[3,1,128]{2,1,0:T(1,128)S(1)}, f32[3,1,128]{2,1,0:T(1,128)S(1)}, u32[]{:S(2)}, u32[]{:S(2)}) collective-permute-start(f32[3,1,128]{2,1,0:T(1,128)S(1)} %pad_maximum_fusion.81), channel_id=1, source_target_pairs={{0,8},{8,16},{16,24},{24,32},{32,40},{40,48},{48,56},{56,64},{64,7... | collective-permute-start | bytes 4616 | tf_op jit(solution)/shard_map/ppermute | solution.py:19
  280.7 6.6 %collective-permute-start.37 = (f32[2,32,1]{2,1,0:T(8,128)S(1)}, f32[2,32,1]{2,1,0:T(8,128)S(1)}, u32[]{:S(2)}, u32[]{:S(2)}) collective-permute-start(f32[2,32,1]{2,1,0:T(8,128)S(1)} %bitcast.1197), channel_id=1, source_target_pairs={{1,0},{2,1},{3,2},{4,3},{5,4},{6,5},{7,6},{9,8},{10,9},{11,10},{12... | collective-permute-start | bytes 776 | tf_op jit(solution)/shard_map/ppermute | solution.py:19
  282.0 5.9 %collective-permute-start.36 = (f32[2,1,128]{2,1,0:T(1,128)S(1)}, f32[2,1,128]{2,1,0:T(1,128)S(1)}, u32[]{:S(2)}, u32[]{:S(2)}) collective-permute-start(f32[2,1,128]{2,1,0:T(1,128)S(1)} %slice.1346), channel_id=1, source_target_pairs={{8,0},{16,8},{24,16},{32,24},{40,32},{48,40},{56,48},{64,56},{72,6... | collective-permute-start | bytes 3080 | tf_op jit(solution)/shard_map/ppermute | solution.py:19
  288.0 8.2 %collective-permute-start.38 = (f32[3,1,128]{2,1,0:T(1,128)S(1)}, f32[3,1,128]{2,1,0:T(1,128)S(1)}, u32[]{:S(2)}, u32[]{:S(2)}) collective-permute-start(f32[3,1,128]{2,1,0:T(1,128)S(1)} %pad_maximum_fusion.80), channel_id=1, source_target_pairs={{0,8},{8,16},{16,24},{24,32},{32,40},{40,48},{48,56},{56,64},{64,7... | collective-permute-start | bytes 4616 | tf_op jit(solution)/shard_map/ppermute | solution.py:19
  296.3 7.6 %collective-permute-start.41 = (f32[2,32,1]{2,1,0:T(8,128)S(1)}, f32[2,32,1]{2,1,0:T(8,128)S(1)}, u32[]{:S(2)}, u32[]{:S(2)}) collective-permute-start(f32[2,32,1]{2,1,0:T(8,128)S(1)} %bitcast.1199), channel_id=1, source_target_pairs={{1,0},{2,1},{3,2},{4,3},{5,4},{6,5},{7,6},{9,8},{10,9},{11,10},{12... | collective-permute-start | bytes 776 | tf_op jit(solution)/shard_map/ppermute | solution.py:19
  297.6 6.9 %collective-permute-start.40 = (f32[2,1,128]{2,1,0:T(1,128)S(1)}, f32[2,1,128]{2,1,0:T(1,128)S(1)}, u32[]{:S(2)}, u32[]{:S(2)}) collective-permute-start(f32[2,1,128]{2,1,0:T(1,128)S(1)} %slice.1362), channel_id=1, source_target_pairs={{8,0},{16,8},{24,16},{32,24},{40,32},{48,40},{56,48},{64,56},{72,6... | collective-permute-start | bytes 3080 | tf_op jit(solution)/shard_map/ppermute | solution.py:19
  304.7 8.2 %collective-permute-start.42 = (f32[3,1,128]{2,1,0:T(1,128)S(1)}, f32[3,1,128]{2,1,0:T(1,128)S(1)}, u32[]{:S(2)}, u32[]{:S(2)}) collective-permute-start(f32[3,1,128]{2,1,0:T(1,128)S(1)} %pad_maximum_fusion.79), channel_id=1, source_target_pairs={{0,8},{8,16},{16,24},{24,32},{32,40},{40,48},{48,56},{56,64},{64,7... | collective-permute-start | bytes 4616 | tf_op jit(solution)/shard_map/ppermute | solution.py:19
  313.0 7.9 %collective-permute-start.45 = (f32[2,32,1]{2,1,0:T(8,128)S(1)}, f32[2,32,1]{2,1,0:T(8,128)S(1)}, u32[]{:S(2)}, u32[]{:S(2)}) collective-permute-start(f32[2,32,1]{2,1,0:T(8,128)S(1)} %bitcast.1200), channel_id=1, source_target_pairs={{1,0},{2,1},{3,2},{4,3},{5,4},{6,5},{7,6},{9,8},{10,9},{11,10},{12... | collective-permute-start | bytes 776 | tf_op jit(solution)/shard_map/ppermute | solution.py:19
  314.3 7.2 %collective-permute-start.44 = (f32[2,1,128]{2,1,0:T(1,128)S(1)}, f32[2,1,128]{2,1,0:T(1,128)S(1)}, u32[]{:S(2)}, u32[]{:S(2)}) collective-permute-start(f32[2,1,128]{2,1,0:T(1,128)S(1)} %slice.1378), channel_id=1, source_target_pairs={{8,0},{16,8},{24,16},{32,24},{40,32},{48,40},{56,48},{64,56},{72,6... | collective-permute-start | bytes 3080 | tf_op jit(solution)/shard_map/ppermute | solution.py:19
  321.7 8.2 %collective-permute-start.46 = (f32[3,1,128]{2,1,0:T(1,128)S(1)}, f32[3,1,128]{2,1,0:T(1,128)S(1)}, u32[]{:S(2)}, u32[]{:S(2)}) collective-permute-start(f32[3,1,128]{2,1,0:T(1,128)S(1)} %pad_maximum_fusion.78), channel_id=1, source_target_pairs={{0,8},{8,16},{16,24},{24,32},{32,40},{40,48},{48,56},{56,64},{64,7... | collective-permute-start | bytes 4616 | tf_op jit(solution)/shard_map/ppermute | solution.py:19
  330.0 7.9 %collective-permute-start.49 = (f32[2,32,1]{2,1,0:T(8,128)S(1)}, f32[2,32,1]{2,1,0:T(8,128)S(1)}, u32[]{:S(2)}, u32[]{:S(2)}) collective-permute-start(f32[2,32,1]{2,1,0:T(8,128)S(1)} %bitcast.1201), channel_id=1, source_target_pairs={{1,0},{2,1},{3,2},{4,3},{5,4},{6,5},{7,6},{9,8},{10,9},{11,10},{12... | collective-permute-start | bytes 776 | tf_op jit(solution)/shard_map/ppermute | solution.py:19
  331.3 7.2 %collective-permute-start.48 = (f32[2,1,128]{2,1,0:T(1,128)S(1)}, f32[2,1,128]{2,1,0:T(1,128)S(1)}, u32[]{:S(2)}, u32[]{:S(2)}) collective-permute-start(f32[2,1,128]{2,1,0:T(1,128)S(1)} %slice.1394), channel_id=1, source_target_pairs={{8,0},{16,8},{24,16},{32,24},{40,32},{48,40},{56,48},{64,56},{72,6... | collective-permute-start | bytes 3080 | tf_op jit(solution)/shard_map/ppermute | solution.py:19
  338.7 8.2 %collective-permute-start.50 = (f32[3,1,128]{2,1,0:T(1,128)S(1)}, f32[3,1,128]{2,1,0:T(1,128)S(1)}, u32[]{:S(2)}, u32[]{:S(2)}) collective-permute-start(f32[3,1,128]{2,1,0:T(1,128)S(1)} %pad_maximum_fusion.77), channel_id=1, source_target_pairs={{0,8},{8,16},{16,24},{24,32},{32,40},{40,48},{48,56},{56,64},{64,7... | collective-permute-start | bytes 4616 | tf_op jit(solution)/shard_map/ppermute | solution.py:19
  347.0 7.9 %collective-permute-start.53 = (f32[2,32,1]{2,1,0:T(8,128)S(1)}, f32[2,32,1]{2,1,0:T(8,128)S(1)}, u32[]{:S(2)}, u32[]{:S(2)}) collective-permute-start(f32[2,32,1]{2,1,0:T(8,128)S(1)} %bitcast.1202), channel_id=1, source_target_pairs={{1,0},{2,1},{3,2},{4,3},{5,4},{6,5},{7,6},{9,8},{10,9},{11,10},{12... | collective-permute-start | bytes 776 | tf_op jit(solution)/shard_map/ppermute | solution.py:19
  348.3 7.2 %collective-permute-start.52 = (f32[2,1,128]{2,1,0:T(1,128)S(1)}, f32[2,1,128]{2,1,0:T(1,128)S(1)}, u32[]{:S(2)}, u32[]{:S(2)}) collective-permute-start(f32[2,1,128]{2,1,0:T(1,128)S(1)} %slice.1410), channel_id=1, source_target_pairs={{8,0},{16,8},{24,16},{32,24},{40,32},{48,40},{56,48},{64,56},{72,6... | collective-permute-start | bytes 3080 | tf_op jit(solution)/shard_map/ppermute | solution.py:19
  355.7 8.2 %collective-permute-start.54 = (f32[3,1,128]{2,1,0:T(1,128)S(1)}, f32[3,1,128]{2,1,0:T(1,128)S(1)}, u32[]{:S(2)}, u32[]{:S(2)}) collective-permute-start(f32[3,1,128]{2,1,0:T(1,128)S(1)} %pad_maximum_fusion.76), channel_id=1, source_target_pairs={{0,8},{8,16},{16,24},{24,32},{32,40},{40,48},{48,56},{56,64},{64,7... | collective-permute-start | bytes 4616 | tf_op jit(solution)/shard_map/ppermute | solution.py:19
  364.0 7.9 %collective-permute-start.57 = (f32[2,32,1]{2,1,0:T(8,128)S(1)}, f32[2,32,1]{2,1,0:T(8,128)S(1)}, u32[]{:S(2)}, u32[]{:S(2)}) collective-permute-start(f32[2,32,1]{2,1,0:T(8,128)S(1)} %bitcast.1203), channel_id=1, source_target_pairs={{1,0},{2,1},{3,2},{4,3},{5,4},{6,5},{7,6},{9,8},{10,9},{11,10},{12... | collective-permute-start | bytes 776 | tf_op jit(solution)/shard_map/ppermute | solution.py:19
  365.3 7.2 %collective-permute-start.56 = (f32[2,1,128]{2,1,0:T(1,128)S(1)}, f32[2,1,128]{2,1,0:T(1,128)S(1)}, u32[]{:S(2)}, u32[]{:S(2)}) collective-permute-start(f32[2,1,128]{2,1,0:T(1,128)S(1)} %slice.1426), channel_id=1, source_target_pairs={{8,0},{16,8},{24,16},{32,24},{40,32},{48,40},{56,48},{64,56},{72,6... | collective-permute-start | bytes 3080 | tf_op jit(solution)/shard_map/ppermute | solution.py:19
  372.7 8.9 %collective-permute-start.58 = (f32[3,1,128]{2,1,0:T(1,128)S(1)}, f32[3,1,128]{2,1,0:T(1,128)S(1)}, u32[]{:S(2)}, u32[]{:S(2)}) collective-permute-start(f32[3,1,128]{2,1,0:T(1,128)S(1)} %pad_maximum_fusion.75), channel_id=1, source_target_pairs={{0,8},{8,16},{16,24},{24,32},{32,40},{40,48},{48,56},{56,64},{64,7... | collective-permute-start | bytes 4616 | tf_op jit(solution)/shard_map/ppermute | solution.py:19
  374.7 6.9 %collective-permute-start.59 = (f32[3,32,1]{2,1,0:T(8,128)S(1)}, f32[3,32,1]{2,1,0:T(8,128)S(1)}, u32[]{:S(2)}, u32[]{:S(2)}) collective-permute-start(f32[3,32,1]{2,1,0:T(8,128)S(1)} %slice.1438), channel_id=1, source_target_pairs={{0,1},{1,2},{2,3},{3,4},{4,5},{5,6},{6,7},{8,9},{9,10},{10,11},{11... | collective-permute-start | bytes 1160 | tf_op jit(solution)/shard_map/ppermute | solution.py:19
  381.7 8.6 %collective-permute-start.61 = (f32[2,32,1]{2,1,0:T(8,128)S(1)}, f32[2,32,1]{2,1,0:T(8,128)S(1)}, u32[]{:S(2)}, u32[]{:S(2)}) collective-permute-start(f32[2,32,1]{2,1,0:T(8,128)S(1)} %bitcast.1238), channel_id=1, source_target_pairs={{1,0},{2,1},{3,2},{4,3},{5,4},{6,5},{7,6},{9,8},{10,9},{11,10},{12... | collective-permute-start | bytes 776 | tf_op jit(solution)/shard_map/ppermute | solution.py:19
  383.0 7.9 %collective-permute-start.60 = (f32[2,1,128]{2,1,0:T(1,128)S(1)}, f32[2,1,128]{2,1,0:T(1,128)S(1)}, u32[]{:S(2)}, u32[]{:S(2)}) collective-permute-start(f32[2,1,128]{2,1,0:T(1,128)S(1)} %slice.1442), channel_id=1, source_target_pairs={{8,0},{16,8},{24,16},{32,24},{40,32},{48,40},{56,48},{64,56},{72,6... | collective-permute-start | bytes 3080 | tf_op jit(solution)/shard_map/ppermute | solution.py:19
  (21 other events, 360.1 us)
where the time goes:
time: 446 us; the launch traced here: 437 us
  starting transfers between devices  232 us (52%)
  waiting for transfers between devices  57.9 us (13%)
  blocking collectives  54.8 us (12%)
  other arithmetic  53.4 us (12%)
  local copies, waits for them, and re-layouts  36.8 us (8%)
    ppermute x62, starting transfers between devices, from_behind(): return lax.ppermute(x, axis, pairs)  220 us
    ppermute x62, waiting for transfers between devices, from_behind(): return lax.ppermute(x, axis, pairs)  51.2 us
    psum x1, blocking collectives, per_device(): gradient = lax.psum(coarse, 'member')  45.5 us
    scatter-add x1, other arithmetic, per_device(): jax.ops.segment_sum((returned * weights[None, :]).T, cells, num_segments=...  23.2 us
    scatter-add x1, other arithmetic, per_device(): summed = jax.ops.segment_sum(received.T, slots, num_segments=BUOYS).T  22.4 us
    gather x2, local copies, waits for them, and re-layouts, per_device(): flat[:, cells] * weights[None, :]  16.3 us
    all_to_all x1, starting transfers between devices, per_device(): lax.all_to_all(partial_value, 'gy', split_axis=1, concat_axis=1, tiled=True)  11.5 us
    gather x1, local copies, waits for them, and re-layouts, per_device(): back = misfit[:, slots].reshape(2, owners, entries // owners)  10.8 us
  transfers between devices with their start and end apart: 63, of which 42 were waited for; matrix products, arithmetic and copies ran while one was open for 2% of the time, Pallas kernels for 0%

commit v1 on v0

v1 whole, which is shorter than its diff:
```python
import jax
import jax.numpy as jnp
from jax import lax
from jax.experimental import pallas as pl
from jax.experimental.pallas import tpu as pltpu
from jax.sharding import PartitionSpec as P

SUBCYCLES = 8
BUOYS = 256
HALO = 8
ROWS = 32
COLS = 128
WIN = ROWS + 2 * HALO
OWNERS = 8

visc_scale = 0.2
relax = 0.6
step_size = 0.2
damping = 0.7

f32 = jnp.float32
bf16 = jnp.bfloat16


def from_behind(x, axis, by):
    count = lax.axis_size(axis)
    pairs = [(i, i + by) for i in range(count) if 0 <= i + by < count]
    return lax.ppermute(x, axis, pairs)


def iota(shape, dim):
    return lax.broadcasted_iota(jnp.int32, shape, dim)


def split3(x):
    hi = x.astype(bf16).astype(f32)
    rest = x - hi
    mid = rest.astype(bf16).astype(f32)
    return hi, mid, rest - mid


def contract_last(a, b):
    return lax.dot_general(a, b, (((1,), (1,)), ((), ())), preferred_element_type=f32)


def tile_fields(forcing, strength, mask):
    cover = mask.astype(f32)
    spread = (iota((16, COLS), 1) // 8 == iota((16, COLS), 0)).astype(f32)
    wide = jnp.dot(strength, spread, precision=lax.Precision.HIGHEST, preferred_element_type=f32)
    fine = jnp.concatenate([jnp.broadcast_to(wide[i : i + 1], (8, COLS)) for i in range(ROWS // 8)], axis=0)
    return forcing[0], forcing[1], cover, visc_scale * fine * cover


def pack_kernel(forcing, strength, mask, recv, out):
    b = lax.axis_index("gy")
    fields = tile_fields(forcing[...], strength[...], mask[...])
    lane = iota((8, COLS), 1)
    left = jnp.zeros((8, COLS), f32)
    right = jnp.zeros((8, COLS), f32)
    for g in range(4):
        for f in range(4):
            at = 32 * g + 8 * f
            piece = fields[f][8 * g : 8 * g + 8]
            here = (lane >= at) & (lane < at + 8)
            left = jnp.where(here, pltpu.roll(piece, at, 1) if at else piece, left)
            right = jnp.where(here, pltpu.roll(piece, at + 8, 1), right)
    slots = recv[...].astype(f32)
    for d in range(OWNERS):
        out[d, 0:8, :] = jnp.where(d < b, left, right)
        for k, s in enumerate((max(d - 1, 0), d, min(d + 1, OWNERS - 1))):
            out[d, 8 + 4 * k : 12 + 4 * k, :] = slots[4 * s : 4 * s + 4]
        out[d, 20:24, :] = jnp.zeros((4, COLS), f32)


def widen_kernel(received, forcing, strength, mask, ext, first, last):
    b = lax.axis_index("gy")
    fields = tile_fields(forcing[...], strength[...], mask[...])
    lane = iota((8, COLS), 1)
    from_left = received[jnp.maximum(b - 1, 0), 0:8, :] * (b > 0).astype(f32)
    from_right = received[jnp.minimum(b + 1, OWNERS - 1), 0:8, :] * (b < OWNERS - 1).astype(f32)
    for f in range(4):
        ext[f, :, 0:COLS] = fields[f]
        for g in range(4):
            at = 32 * g + 8 * f
            low = pltpu.roll(from_right, (COLS - at) % COLS, 1) if at else from_right
            high = pltpu.roll(from_left, (120 - at) % COLS, 1)
            ext[f, 8 * g : 8 * g + 8, COLS:] = jnp.where(lane < 8, low, jnp.where(lane >= 120, high, 0.0))
    first[...] = ext[:, 0:8, :]
    last[...] = ext[:, ROWS - 8 : ROWS, :]


def next_row(x):
    return pltpu.roll(x, x.shape[0] - 1, 0)


def prev_row(x):
    return pltpu.roll(x, 1, 0)


def next_col(x):
    return pltpu.roll(x, x.shape[1] - 1, 1)


def prev_col(x):
    return pltpu.roll(x, 1, 1)


def forward_kernel(ext, above, below, cells, codes, received, observed, sums, rates, window, vel):
    b = lax.axis_index("gy")
    force_x, force_y, cover, visc = (
        jnp.concatenate([above[f], ext[f], below[f]], axis=0) for f in range(4)
    )
    window[0] = cover
    window[1] = visc
    tau_x = step_size * cover * force_x
    tau_y = step_size * cover * force_y
    big = (0.625 * step_size) * visc
    small = (0.375 * step_size) * visc
    quarter = (0.25 * step_size) * visc
    u, v = tau_x, tau_y
    nx = ny = s3 = None
    own = slice(HALO, HALO + ROWS)
    for step in range(SUBCYCLES - 1):
        ex = next_row(u) - u
        ey = next_col(v) - v
        sh = (next_col(u) - u) + (next_row(v) - v)
        rates[step, 0] = ex[own, :COLS]
        rates[step, 1] = ey[own, :COLS]
        rates[step, 2] = sh[own, :COLS]
        dx = big * ex + small * ey
        dy = small * ex + big * ey
        ds = quarter * sh
        nx = dx if nx is None else relax * nx + dx
        ny = dy if ny is None else relax * ny + dy
        s3 = ds if s3 is None else relax * s3 + ds
        fx = (nx - prev_row(nx)) + (s3 - prev_col(s3))
        fy = (ny - prev_col(ny)) + (s3 - prev_row(s3))
        u = damping * u + cover * fx + tau_x
        v = damping * v + cover * fy + tau_y
    vel[0] = u[own, :COLS]
    vel[1] = v[own, :COLS]

    cell = cells[...]
    row, col = cell // COLS, cell % COLS
    got_u = jnp.zeros((ROWS, COLS), f32)
    got_v = jnp.zeros((ROWS, COLS), f32)
    for r in range(ROWS):
        hit = row == r
        line_u = jnp.broadcast_to(vel[0, r : r + 1, :], (ROWS, COLS))
        line_v = jnp.broadcast_to(vel[1, r : r + 1, :], (ROWS, COLS))
        got_u = jnp.where(hit, jnp.take_along_axis(line_u, col, axis=1), got_u)
        got_v = jnp.where(hit, jnp.take_along_axis(line_v, col, axis=1), got_v)
    weight = codes[...].astype(f32) * (1.0 / 16.0)
    parts = split3(got_u * weight) + split3(got_v * weight)
    sub = iota((8, COLS), 0)
    slot_ids = iota((BUOYS, COLS), 0)
    blocks = []
    for d in range(OWNERS):
        lines = received[d, 12:16, :].astype(jnp.int32)
        base = 8 * (d // 2)
        left, right = [], []
        for i in range(4):
            keep = sub == 4 * (d % 2) + i
            left.append(
                jnp.concatenate([jnp.where(keep, p[base : base + 8], 0.0) for p in parts], axis=0).astype(bf16)
            )
            right.append((slot_ids == lines[i : i + 1, :]).astype(f32).astype(bf16))
        prod = contract_last(jnp.concatenate(left, axis=1), jnp.concatenate(right, axis=1))
        mine = (b == d).astype(f32)
        blocks.append(jnp.sum(prod[0:24], axis=0, keepdims=True) - mine * observed[0:1, :])
        blocks.append(jnp.sum(prod[24:48], axis=0, keepdims=True) - mine * observed[1:2, :])
    total = jnp.concatenate(blocks, axis=0)
    for d in range(OWNERS):
        sums[d] = total


def scatter_kernel(sums, tables, received, misfit, adj, first, last, total, lhs, rhs):
    b = lax.axis_index("gy")
    acc = sums[0]
    for j in range(1, OWNERS):
        acc = acc + sums[j]
    total[...] = acc
    mine = acc[0:2]
    for d in range(1, OWNERS):
        mine = jnp.where(b == d, acc[2 * d : 2 * d + 2], mine)
    misfit[...] = mine
    sub = iota((8, COLS), 0)
    lane = iota((ROWS, COLS), 1)
    row_ids = iota((ROWS, COLS), 0)
    col_ids = iota((COLS, COLS), 0)
    results = []
    for k, s in enumerate((jnp.maximum(b - 1, 0), b, jnp.minimum(b + 1, OWNERS - 1))):
        cell = tables[s, 0]
        weight = tables[s, 1].astype(f32) * (1.0 / 16.0)
        row, col = cell // COLS, cell % COLS
        values = [[], []]
        for q in range(4):
            slot = jnp.concatenate(
                [received[2 * q + o, 8 + 4 * k : 12 + 4 * k, :] for o in range(2)], axis=0
            ).astype(jnp.int32)
            near = slot % COLS
            for c in range(2):
                table = [
                    jnp.where(
                        sub < 4,
                        jnp.broadcast_to(total[4 * q + c : 4 * q + c + 1, h : h + COLS], (8, COLS)),
                        jnp.broadcast_to(total[4 * q + 2 + c : 4 * q + 3 + c, h : h + COLS], (8, COLS)),
                    )
                    for h in (0, COLS)
                ]
                values[c].append(
                    jnp.where(
                        slot < COLS,
                        jnp.take_along_axis(table[0], near, axis=1),
                        jnp.take_along_axis(table[1], near, axis=1),
                    )
                )
        parts = []
        for c in range(2):
            parts += split3(jnp.concatenate(values[c], axis=0) * weight)
        for i in range(ROWS):
            at = slice(COLS * i, COLS * i + COLS)
            hit = row_ids == row[i : i + 1, :]
            for p, part in enumerate(parts):
                lhs[ROWS * p : ROWS * p + ROWS, at] = jnp.where(hit, part[i : i + 1, :], 0.0).astype(bf16)
            rhs[:, at] = (col_ids == col[i : i + 1, :]).astype(f32).astype(bf16)
        prod = contract_last(lhs[...], rhs[...])
        results.append(
            [prod[96 * c : 96 * c + 32] + prod[96 * c + 32 : 96 * c + 64] + prod[96 * c + 64 : 96 * c + 96] for c in range(2)]
        )
    for c in range(2):
        adj[c, :, 0:COLS] = results[1][c]
        adj[c, :, COLS:] = jnp.where(lane < 8, results[2][c], jnp.where(lane >= 120, results[0][c], 0.0))
    first[...] = adj[:, 0:8, :]
    last[...] = adj[:, ROWS - 8 : ROWS, :]


def adjoint_kernel(adj, above, below, window, rates, out):
    cover = window[0]
    visc = window[1]
    scaled = step_size * cover
    third = 0.25 * visc
    w0, w1 = (scaled * jnp.concatenate([above[c], adj[c], below[c]], axis=0) for c in range(2))
    own = slice(HALO, HALO + ROWS)
    a = h = t = None
    grad = None
    for step in range(SUBCYCLES - 2, -1, -1):
        ax = w0 - next_row(w0)
        ay = w1 - next_col(w1)
        at = (w0 - next_col(w0)) + (w1 - next_row(w1))
        da = 0.625 * ax + 0.375 * ay
        dh = 0.375 * ax + 0.625 * ay
        a = da if a is None else relax * a + da
        h = dh if h is None else relax * h + dh
        t = at if t is None else relax * t + at
        term = (
            a[own, :COLS] * rates[step, 0]
            + h[own, :COLS] * rates[step, 1]
            + 0.25 * (t[own, :COLS] * rates[step, 2])
        )
        grad = term if grad is None else grad + term
        if step:
            ra, rh, rt = visc * a, visc * h, third * t
            w0 = damping * w0 + scaled * ((prev_row(ra) - ra) + (prev_col(rt) - rt))
            w1 = damping * w1 + scaled * ((prev_col(rh) - rh) + (prev_row(rt) - rt))
    grad = visc_scale * cover[own, :COLS] * grad
    rows = jnp.concatenate(
        [jnp.sum(grad[8 * i : 8 * i + 8], axis=0, keepdims=True) for i in range(ROWS // 8)], axis=0
    )
    gather = (iota((COLS, 16), 0) // 8 == iota((COLS, 16), 1)).astype(f32)
    out[...] = jnp.dot(rows, gather, precision=lax.Precision.HIGHEST, preferred_element_type=f32)


def call(kernel, outs, args, scratch=()):
    vmem = pl.BlockSpec(memory_space=pltpu.VMEM)
    return pl.pallas_call(
        kernel,
        out_shape=tuple(jax.ShapeDtypeStruct(s, f32) for s in outs),
        in_specs=[vmem] * len(args),
        out_specs=(vmem,) * len(outs),
        scratch_shapes=list(scratch),
        compiler_params=pltpu.CompilerParams(vmem_limit_bytes=24 * 1024 * 1024),
    )(*args)


def per_device(forcing, strength, mask, send_cell, send_code, recv_buoy, observed):
    forcing = forcing[0]
    cells = send_cell.reshape(ROWS, COLS)
    codes = send_code.reshape(ROWS, COLS)
    recv = recv_buoy.reshape(ROWS, COLS)
    observed = observed.reshape(2, BUOYS)
    tables = lax.all_gather(jnp.stack([cells, codes]), "gy")
    (packed,) = call(pack_kernel, [(OWNERS, 24, COLS)], (forcing, strength, mask, recv))
    received = lax.all_to_all(packed, "gy", 0, 0, tiled=True)
    ext, first, last = call(
        widen_kernel,
        [(4, ROWS, 2 * COLS), (4, 8, 2 * COLS), (4, 8, 2 * COLS)],
        (received, forcing, strength, mask),
    )
    above = from_behind(last, "gx", 1)
    below = from_behind(first, "gx", -1)
    sums, rates, window = call(
        forward_kernel,
        [(OWNERS, 2 * OWNERS, BUOYS), (SUBCYCLES - 1, 3, ROWS, COLS), (2, WIN, 2 * COLS)],
        (ext, above, below, cells, codes, received, observed),
        [pltpu.VMEM((2, ROWS, COLS), f32)],
    )
    sums = lax.all_to_all(sums, "gy", 0, 0, tiled=True)
    misfit, adj, first, last = call(
        scatter_kernel,
        [(2, BUOYS), (2, ROWS, 2 * COLS), (2, 8, 2 * COLS), (2, 8, 2 * COLS)],
        (sums, tables, received),
        [
            pltpu.VMEM((2 * OWNERS, BUOYS), f32),
            pltpu.VMEM((6 * ROWS, ROWS * COLS), bf16),
            pltpu.VMEM((COLS, ROWS * COLS), bf16),
        ],
    )
    above = from_behind(last, "gx", 1)
    below = from_behind(first, "gx", -1)
    (coarse,) = call(adjoint_kernel, [(ROWS // 8, COLS // 8)], (adj, above, below, window, rates))
    gradient = lax.psum(coarse, "member")
    return (misfit[None, None, None], gradient)


def solution(mesh):
    return jax.shard_map(
        per_device,
        mesh=mesh,
        in_specs=(
            P("member", None, "gx", "gy"),
            P("gx", "gy"),
            P("gx", "gy"),
            P("member", "gx", "gy", None),
            P("member", "gx", "gy", None),
            P("member", "gx", "gy", None),
            P("member", "gx", "gy", None, None),
        ),
        out_specs=(P("member", "gx", "gy", None, None), P("gx", "gy")),
        check_vma=False,
    )
```

time: 446 us -> 92.5 us (0.21)
  the two profiles are of different devices: /device:TPU:7 before, /device:TPU:56 now
where the time goes in v1:
time: 92.5 us; the launch traced here: 91.9 us
  blocking collectives  51.7 us (56%)
  starting transfers between devices  15.3 us (17%)
  waiting for transfers between devices  12.8 us (14%)
  Pallas kernels  7.91 us (9%)
  local copies, waits for them, and re-layouts  3.55 us (4%)
    all_gather x1, blocking collectives, per_device(): tables = lax.all_gather(jnp.stack([cells, codes]), 'gy')  26.3 us
    all_to_all x1, blocking collectives, per_device(): received = lax.all_to_all(packed, 'gy', 0, 0, tiled=True)  18.8 us
    ppermute x4, waiting for transfers between devices, from_behind(): return lax.ppermute(x, axis, pairs)  12.8 us
    ppermute x4, starting transfers between devices, from_behind(): return lax.ppermute(x, axis, pairs)  11.9 us
    pallas_call x5, Pallas kernels, call(): pl.pallas_call(kernel, out_shape=tuple((jax.ShapeDtypeStruct(s, f32) for...  7.91 us
    psum x1, blocking collectives, per_device(): gradient = lax.psum(coarse, 'member')  6.54 us
    unnamed x14, local copies, waits for them, and re-layouts  3.55 us
    all_to_all x1, starting transfers between devices, per_device(): sums = lax.all_to_all(sums, 'gy', 0, 0, tiled=True)  3.37 us
  transfers between devices with their start and end apart: 5, of which 2 were waited for; matrix products, arithmetic and copies ran while one was open for 0% of the time, Pallas kernels for 0%

profile of v1, /device:TPU:56, one launch (start us, length us, event | category | flops | bytes accessed | tf_op | source)
XLA Modules:
  0.0 91.9 jit_solution(10921832129376083891)
XLA Ops:
  0.6 0.0 copy-start.5
  0.6 0.7 copy-done.5
  1.3 0.0 copy-start
  1.3 0.8 copy-done
  2.1 0.0 copy-start.3
  2.1 0.7 copy-done.3
  2.8 0.0 copy-start.4
  2.8 0.7 copy-done.4
  3.5 0.2 shard_map.86
  3.7 18.8 %all_to_all.10.received = f32[8,24,128]{2,1,0:T(8,128)S(1)} all-to-all(f32[8,24,128]{2,1,0:T(8,128)S(1)} %shard_map.86), channel_id=1, replica_groups=mesh['member'=4,'gx'=16,'gy'=8] {'gy'}, dimensions={0} | all-to-all | bytes 196608 | tf_op jit(solution)/shard_map/all_to_all | solution.py:294
  22.6 0.0 copy-start.1
  22.6 0.0 copy-start.2
  22.6 0.1 shard_map.87
  22.7 4.1 %collective-permute-start = (f32[4,8,256]{2,1,0:T(8,128)S(1)}, f32[4,8,256]{2,1,0:T(8,128)S(1)}, u32[]{:S(2)}, u32[]{:S(2)}) collective-permute-start(f32[4,8,256]{2,1,0:T(8,128)S(1)} %get-tuple-element.13), channel_id=1, source_target_pairs={{0,8},{8,16},{16,24},{24,32},{32,40},{40,48},{48,56},{56,64},{64,7... | collective-permute-start | bytes 98312 | tf_op jit(solution)/shard_map/ppermute | solution.py:28
  26.8 1.9 %collective-permute-start.1 = (f32[4,8,256]{2,1,0:T(8,128)S(1)}, f32[4,8,256]{2,1,0:T(8,128)S(1)}, u32[]{:S(2)}, u32[]{:S(2)}) collective-permute-start(f32[4,8,256]{2,1,0:T(8,128)S(1)} %get-tuple-element.14), channel_id=1, source_target_pairs={{8,0},{16,8},{24,16},{32,24},{40,32},{48,40},{56,48},{64,56},{72,6... | collective-permute-start | bytes 98312 | tf_op jit(solution)/shard_map/ppermute | solution.py:28
  28.8 0.0 collective-permute-done.above
  28.8 7.5 %collective-permute-done.1.below = f32[4,8,256]{2,1,0:T(8,128)S(1)} collective-permute-done((f32[4,8,256]{2,1,0:T(8,128)S(1)}, f32[4,8,256]{2,1,0:T(8,128)S(1)}, u32[]{:S(2)}, u32[]{:S(2)}) %collective-permute-start.1) | collective-permute-done | bytes 32800 | tf_op jit(solution)/shard_map/ppermute | solution.py:28
  36.3 0.0 copy-start.6
  36.3 0.0 copy-done.1
  36.3 0.0 copy-done.2
  36.3 0.7 copy-done.6
  37.0 2.7 %shard_map.88 = (f32[8,16,256]{2,1,0:T(8,128)}, f32[7,3,32,128]{3,2,1,0:T(8,128)S(1)}, f32[2,48,256]{2,1,0:T(8,128)S(1)}) custom-call(f32[4,32,256]{2,1,0:T(8,128)S(1)} %get-tuple-element.12.ext, f32[4,8,256]{2,1,0:T(8,128)S(1)} %collective-permute-done.above, f32[4,8,256]{2,1,0:T(8,128)S(1)} %collective-permute-done.1.below, s32[32,128]{1,0:T(8,128)S(1)} %bitcast.12, ...), custom_call_target="tpu_custom_call" | custom-call | tf_op jit(solution)/shard_map/pallas_call | solution.py:276
  39.7 3.4 %all-to-all-start.1 = ((f32[8,16,256]{2,1,0:T(8,128)}), f32[8,16,256]{2,1,0:T(8,128)S(1)}, u32[]{:S(2)}, u32[]{:S(2)}) async-start(f32[8,16,256]{2,1,0:T(8,128)} %get-tuple-element.15), calls=%async_computation.1 | async-start | bytes 262144 | tf_op jit(solution)/shard_map/all_to_all | solution.py:308
  43.1 26.3 %all-gather = s32[16,32,128]{2,1,0:T(8,128)S(1)} all-gather(s32[2,32,128]{2,1,0:T(8,128)S(1)} %pad_add_fusion), channel_id=2, replica_groups=mesh['member'=4,'gx'=16,'gy'=8] {'gy'}, dimensions={0}, use_global_device_ids=true | all-gather | bytes 294912 | tf_op jit(solution)/shard_map/all_gather | solution.py:292
  69.3 0.0 all-to-all-done.1.sums
  69.3 3.6 %shard_map.89 = (f32[2,256]{1,0:T(2,128)}, f32[2,32,256]{2,1,0:T(8,128)S(1)}, f32[2,8,256]{2,1,0:T(8,128)S(1)}, f32[2,8,256]{2,1,0:T(8,128)S(1)}) custom-call(f32[8,16,256]{2,1,0:T(8,128)S(1)} %all-to-all-done.1.sums, s32[8,2,32,128]{3,2,1,0:T(8,128)S(1)} %bitcast.9, f32[8,24,128]{2,1,0:T(8,128)S(1)} %all_to_all.10.received), custom_call_target="tpu_custom_call" | custom-call | tf_op jit(solution)/shard_map/pallas_call | solution.py:276
  72.9 1.9 %collective-permute-start.2 = (f32[2,8,256]{2,1,0:T(8,128)S(1)}, f32[2,8,256]{2,1,0:T(8,128)S(1)}, u32[]{:S(2)}, u32[]{:S(2)}) collective-permute-start(f32[2,8,256]{2,1,0:T(8,128)S(1)} %get-tuple-element.18), channel_id=1, source_target_pairs={{0,8},{8,16},{16,24},{24,32},{32,40},{40,48},{48,56},{56,64},{64,7... | collective-permute-start | bytes 49160 | tf_op jit(solution)/shard_map/ppermute | solution.py:28
  74.9 3.9 %collective-permute-start.3 = (f32[2,8,256]{2,1,0:T(8,128)S(1)}, f32[2,8,256]{2,1,0:T(8,128)S(1)}, u32[]{:S(2)}, u32[]{:S(2)}) collective-permute-start(f32[2,8,256]{2,1,0:T(8,128)S(1)} %get-tuple-element.19), channel_id=1, source_target_pairs={{8,0},{16,8},{24,16},{32,24},{40,32},{48,40},{56,48},{64,56},{72,6... | collective-permute-start | bytes 49160 | tf_op jit(solution)/shard_map/ppermute | solution.py:28
  78.8 0.0 collective-permute-done.2.above
  78.8 5.3 %collective-permute-done.3.below = f32[2,8,256]{2,1,0:T(8,128)S(1)} collective-permute-done((f32[2,8,256]{2,1,0:T(8,128)S(1)}, f32[2,8,256]{2,1,0:T(8,128)S(1)}, u32[]{:S(2)}, u32[]{:S(2)}) %collective-permute-start.3) | collective-permute-done | bytes 16416 | tf_op jit(solution)/shard_map/ppermute | solution.py:28
  84.1 1.2 %shard_map.90 = f32[4,16]{1,0:T(4,128)S(1)} custom-call(f32[2,32,256]{2,1,0:T(8,128)S(1)} %get-tuple-element.17.adj, f32[2,8,256]{2,1,0:T(8,128)S(1)} %collective-permute-done.2.above, f32[2,8,256]{2,1,0:T(8,128)S(1)} %collective-permute-done.3.below, f32[2,48,256]{2,1,0:T(8,128)S(1)} %get-tuple-element.20.window, f32[7,3,32,128]{3,2,1,0:T(8,128)S(1)} %get-tuple-element.21.rates), custom_call_target="tpu_custom_call" | custom-call | tf_op jit(solution)/shard_map/pallas_call | solution.py:276
  85.4 6.5 %psum.7 = f32[4,16]{1,0:T(4,128)} all-reduce(f32[4,16]{1,0:T(4,128)S(1)} %shard_map.90), channel_id=1, replica_groups=mesh['member'=4,'gx'=16,'gy'=8] {'member'}, use_global_device_ids=true, to_apply=%region_0.0 | all-reduce | flops 64 | bytes 512 | tf_op jit(solution)/shard_map/psum | solution.py:322
  (1 shorter events, 0.0 us)
Async XLA Ops:
  0.6 0.7 copy-start.5
  1.3 0.8 copy-start
  2.1 0.7 copy-start.3
  2.8 0.7 copy-start.4
  22.6 13.7 %copy-start.1 = (s32[1,1,1,4096]{3,2,1,0:T(1,128)S(1)}, s32[1,1,1,4096]{3,2,1,0:T(1,128)}, u32[]{:S(2)}) copy-start(s32[1,1,1,4096]{3,2,1,0:T(1,128)} %param.10) | copy-start | bytes 49156
  22.6 13.7 %copy-start.2 = (s32[1,1,1,4096]{3,2,1,0:T(1,128)S(1)}, s32[1,1,1,4096]{3,2,1,0:T(1,128)}, u32[]{:S(2)}) copy-start(s32[1,1,1,4096]{3,2,1,0:T(1,128)} %param.11) | copy-start | bytes 49156
  22.7 6.1 %collective-permute-start = (f32[4,8,256]{2,1,0:T(8,128)S(1)}, f32[4,8,256]{2,1,0:T(8,128)S(1)}, u32[]{:S(2)}, u32[]{:S(2)}) collective-permute-start(f32[4,8,256]{2,1,0:T(8,128)S(1)} %get-tuple-element.13), channel_id=1, source_target_pairs={{0,8},{8,16},{16,24},{24,32},{32,40},{40,48},{48,56},{56,64},{64,7... | collective-permute-start | bytes 98312 | tf_op jit(solution)/shard_map/ppermute | solution.py:28
  26.8 9.4 %collective-permute-start.1 = (f32[4,8,256]{2,1,0:T(8,128)S(1)}, f32[4,8,256]{2,1,0:T(8,128)S(1)}, u32[]{:S(2)}, u32[]{:S(2)}) collective-permute-start(f32[4,8,256]{2,1,0:T(8,128)S(1)} %get-tuple-element.14), channel_id=1, source_target_pairs={{8,0},{16,8},{24,16},{32,24},{40,32},{48,40},{56,48},{64,56},{72,6... | collective-permute-start | bytes 98312 | tf_op jit(solution)/shard_map/ppermute | solution.py:28
  36.3 0.7 copy-start.6
  39.7 29.7 %all-to-all-start.1 = ((f32[8,16,256]{2,1,0:T(8,128)}), f32[8,16,256]{2,1,0:T(8,128)S(1)}, u32[]{:S(2)}, u32[]{:S(2)}) async-start(f32[8,16,256]{2,1,0:T(8,128)} %get-tuple-element.15), calls=%async_computation.1 | async-start | bytes 262144 | tf_op jit(solution)/shard_map/all_to_all | solution.py:308
  72.9 5.8 %collective-permute-start.2 = (f32[2,8,256]{2,1,0:T(8,128)S(1)}, f32[2,8,256]{2,1,0:T(8,128)S(1)}, u32[]{:S(2)}, u32[]{:S(2)}) collective-permute-start(f32[2,8,256]{2,1,0:T(8,128)S(1)} %get-tuple-element.18), channel_id=1, source_target_pairs={{0,8},{8,16},{16,24},{24,32},{32,40},{40,48},{48,56},{56,64},{64,7... | collective-permute-start | bytes 49160 | tf_op jit(solution)/shard_map/ppermute | solution.py:28
  74.9 9.2 %collective-permute-start.3 = (f32[2,8,256]{2,1,0:T(8,128)S(1)}, f32[2,8,256]{2,1,0:T(8,128)S(1)}, u32[]{:S(2)}, u32[]{:S(2)}) collective-permute-start(f32[2,8,256]{2,1,0:T(8,128)S(1)} %get-tuple-element.19), channel_id=1, source_target_pairs={{8,0},{16,8},{24,16},{32,24},{40,32},{48,40},{56,48},{64,56},{72,6... | collective-permute-start | bytes 49160 | tf_op jit(solution)/shard_map/ppermute | solution.py:28

commit v2 on v1

--- a/solution.py
+++ b/solution.py
@@ -12,6 +12,7 @@
 COLS = 128
 WIN = ROWS + 2 * HALO
 OWNERS = 8
+SPAN = 8
 
 visc_scale = 0.2
 relax = 0.6
@@ -51,9 +52,22 @@
     return forcing[0], forcing[1], cover, visc_scale * fine * cover
 
 
-def pack_kernel(forcing, strength, mask, recv, out):
+def pack_kernel(
+    forcing_in, strength_in, mask_in, recv_in, cells_in, codes_in, observed_in,
+    out, own, table, observed,
+    forcing, strength, mask, recv, sems,
+):
     b = lax.axis_index("gy")
+    sources = (forcing_in, strength_in, mask_in, recv_in, cells_in, codes_in, observed_in)
+    targets = (forcing, strength, mask, recv, table.at[0], table.at[1], observed)
+    copies = [pltpu.make_async_copy(a, t, sems.at[i]) for i, (a, t) in enumerate(zip(sources, targets))]
+    for copy in copies:
+        copy.start()
+    for copy in copies:
+        copy.wait()
     fields = tile_fields(forcing[...], strength[...], mask[...])
+    for f in range(4):
+        own[f] = fields[f]
     lane = iota((8, COLS), 1)
     left = jnp.zeros((8, COLS), f32)
     right = jnp.zeros((8, COLS), f32)
@@ -67,19 +81,16 @@
     slots = recv[...].astype(f32)
     for d in range(OWNERS):
         out[d, 0:8, :] = jnp.where(d < b, left, right)
-        for k, s in enumerate((max(d - 1, 0), d, min(d + 1, OWNERS - 1))):
-            out[d, 8 + 4 * k : 12 + 4 * k, :] = slots[4 * s : 4 * s + 4]
-        out[d, 20:24, :] = jnp.zeros((4, COLS), f32)
-
-
-def widen_kernel(received, forcing, strength, mask, ext, first, last):
+        out[d, 8:12, :] = slots[4 * d : 4 * d + 4]
+
+
+def widen_kernel(received, own, ext, first, last):
     b = lax.axis_index("gy")
-    fields = tile_fields(forcing[...], strength[...], mask[...])
     lane = iota((8, COLS), 1)
     from_left = received[jnp.maximum(b - 1, 0), 0:8, :] * (b > 0).astype(f32)
     from_right = received[jnp.minimum(b + 1, OWNERS - 1), 0:8, :] * (b < OWNERS - 1).astype(f32)
     for f in range(4):
-        ext[f, :, 0:COLS] = fields[f]
+        ext[f, :, 0:COLS] = own[f]
         for g in range(4):
             at = 32 * g + 8 * f
             low = pltpu.roll(from_right, (COLS - at) % COLS, 1) if at else from_right
@@ -105,7 +116,23 @@
     return pltpu.roll(x, 1, 1)
 
 
-def forward_kernel(ext, above, below, cells, codes, received, observed, sums, rates, window, vel):
+def own_kernel(received, table, table_out, slot_hot, col_hot):
+    slot_ids = iota((BUOYS, COLS), 0)
+    col_ids = iota((COLS, COLS), 0)
+    slots = jnp.concatenate([received[d, 8:12, :] for d in range(OWNERS)], axis=0).astype(jnp.int32)
+    cell = table[0]
+    weight = table[1].astype(f32) * (1.0 / 16.0)
+    col = cell % COLS
+    table_out[0] = cell
+    table_out[1] = table[1]
+    table_out[2] = slots
+    for i in range(ROWS):
+        at = slice(COLS * i, COLS * i + COLS)
+        slot_hot[:, at] = (slot_ids == slots[i : i + 1, :]).astype(f32).astype(bf16)
+        col_hot[:, at] = jnp.where(col_ids == col[i : i + 1, :], weight[i : i + 1, :], 0.0).astype(bf16)
+
+
+def forward_kernel(ext, above, below, hot, table, observed, sums, rates, window, vel):
     b = lax.axis_index("gy")
     force_x, force_y, cover, visc = (
         jnp.concatenate([above[f], ext[f], below[f]], axis=0) for f in range(4)
@@ -140,7 +167,7 @@
     vel[0] = u[own, :COLS]
     vel[1] = v[own, :COLS]
 
-    cell = cells[...]
+    cell = table[0]
     row, col = cell // COLS, cell % COLS
     got_u = jnp.zeros((ROWS, COLS), f32)
     got_v = jnp.zeros((ROWS, COLS), f32)
@@ -150,22 +177,19 @@
         line_v = jnp.broadcast_to(vel[1, r : r + 1, :], (ROWS, COLS))
         got_u = jnp.where(hit, jnp.take_along_axis(line_u, col, axis=1), got_u)
         got_v = jnp.where(hit, jnp.take_along_axis(line_v, col, axis=1), got_v)
-    weight = codes[...].astype(f32) * (1.0 / 16.0)
+    weight = table[1].astype(f32) * (1.0 / 16.0)
     parts = split3(got_u * weight) + split3(got_v * weight)
     sub = iota((8, COLS), 0)
-    slot_ids = iota((BUOYS, COLS), 0)
     blocks = []
     for d in range(OWNERS):
-        lines = received[d, 12:16, :].astype(jnp.int32)
         base = 8 * (d // 2)
-        left, right = [], []
+        left = []
         for i in range(4):
             keep = sub == 4 * (d % 2) + i
             left.append(
                 jnp.concatenate([jnp.where(keep, p[base : base + 8], 0.0) for p in parts], axis=0).astype(bf16)
             )
-            right.append((slot_ids == lines[i : i + 1, :]).astype(f32).astype(bf16))
-        prod = contract_last(jnp.concatenate(left, axis=1), jnp.concatenate(right, axis=1))
+        prod = contract_last(jnp.concatenate(left, axis=1), hot[:, 4 * COLS * d : 4 * COLS * d + 4 * COLS])
         mine = (b == d).astype(f32)
         blocks.append(jnp.sum(prod[0:24], axis=0, keepdims=True) - mine * observed[0:1, :])
         blocks.append(jnp.sum(prod[24:48], axis=0, keepdims=True) - mine * observed[1:2, :])
@@ -174,7 +198,23 @@
         sums[d] = total
 
 
-def scatter_kernel(sums, tables, received, misfit, adj, first, last, total, lhs, rhs):
+def edge_kernel(left_table, right_table, left_hot, right_hot):
+    edge_ids = iota((8 * SPAN, COLS), 0)
+    for table, hot, first_col in ((left_table, left_hot, COLS - 8), (right_table, right_hot, 0)):
+        cell = table[0]
+        weight = table[1].astype(f32) * (1.0 / 16.0)
+        row, col = cell // COLS, cell % COLS
+        place = jnp.where((col >= first_col) & (col < first_col + 8), row % SPAN * 8 + col % 8, -1)
+        for i in range(ROWS):
+            at = slice(COLS * i, COLS * i + COLS)
+            hot[:, at] = jnp.where(edge_ids == place[i : i + 1, :], weight[i : i + 1, :], 0.0).astype(bf16)
+
+
+def scatter_kernel(
+    sums, left_table, own_table, right_table, col_hot, left_hot, right_hot,
+    misfit, adj, first, last,
+    total, lhs, edge_lhs,
+):
     b = lax.axis_index("gy")
     acc = sums[0]
     for j in range(1, OWNERS):
@@ -185,52 +225,75 @@
         mine = jnp.where(b == d, acc[2 * d : 2 * d + 2], mine)
     misfit[...] = mine
     sub = iota((8, COLS), 0)
-    lane = iota((ROWS, COLS), 1)
+    lane = iota((8, COLS), 1)
+    tables = [
+        [
+            [
+                jnp.where(
+                    sub < 4,
+                    jnp.broadcast_to(total[4 * q + c : 4 * q + c + 1, h : h + COLS], (8, COLS)),
+                    jnp.broadcast_to(total[4 * q + 2 + c : 4 * q + 3 + c, h : h + COLS], (8, COLS)),
+                )
+                for h in (0, COLS)
+            ]
+            for c in range(2)
+        ]
+        for q in range(4)
+    ]
     row_ids = iota((ROWS, COLS), 0)
-    col_ids = iota((COLS, COLS), 0)
-    results = []
-    for k, s in enumerate((jnp.maximum(b - 1, 0), b, jnp.minimum(b + 1, OWNERS - 1))):
-        cell = tables[s, 0]
-        weight = tables[s, 1].astype(f32) * (1.0 / 16.0)
-        row, col = cell // COLS, cell % COLS
+    halo = [None, None, None]
+    for k in (0, 2, 1):
+        row = (left_table, own_table, right_table)[k][0] // COLS
         values = [[], []]
         for q in range(4):
-            slot = jnp.concatenate(
-                [received[2 * q + o, 8 + 4 * k : 12 + 4 * k, :] for o in range(2)], axis=0
-            ).astype(jnp.int32)
+            slot = (left_table, own_table, right_table)[k][2, 8 * q : 8 * q + 8, :]
             near = slot % COLS
             for c in range(2):
-                table = [
-                    jnp.where(
-                        sub < 4,
-                        jnp.broadcast_to(total[4 * q + c : 4 * q + c + 1, h : h + COLS], (8, COLS)),
-                        jnp.broadcast_to(total[4 * q + 2 + c : 4 * q + 3 + c, h : h + COLS], (8, COLS)),
-                    )
-                    for h in (0, COLS)
-                ]
                 values[c].append(
                     jnp.where(
                         slot < COLS,
-                        jnp.take_along_axis(table[0], near, axis=1),
-                        jnp.take_along_axis(table[1], near, axis=1),
+                        jnp.take_along_axis(tables[q][c][0], near, axis=1),
+                        jnp.take_along_axis(tables[q][c][1], near, axis=1),
                     )
                 )
         parts = []
         for c in range(2):
-            parts += split3(jnp.concatenate(values[c], axis=0) * weight)
-        for i in range(ROWS):
-            at = slice(COLS * i, COLS * i + COLS)
-            hit = row_ids == row[i : i + 1, :]
-            for p, part in enumerate(parts):
-                lhs[ROWS * p : ROWS * p + ROWS, at] = jnp.where(hit, part[i : i + 1, :], 0.0).astype(bf16)
-            rhs[:, at] = (col_ids == col[i : i + 1, :]).astype(f32).astype(bf16)
-        prod = contract_last(lhs[...], rhs[...])
-        results.append(
-            [prod[96 * c : 96 * c + 32] + prod[96 * c + 32 : 96 * c + 64] + prod[96 * c + 64 : 96 * c + 96] for c in range(2)]
-        )
+            parts += split3(jnp.concatenate(values[c], axis=0))
+        if k == 1:
+            for i in range(ROWS):
+                at = slice(COLS * i, COLS * i + COLS)
+                hit = row_ids == row[i : i + 1, :]
+                for p, part in enumerate(parts):
+                    lhs[ROWS * p : ROWS * p + ROWS, at] = jnp.where(hit, part[i : i + 1, :], 0.0).astype(bf16)
+            prod = contract_last(lhs[...], col_hot[...])
+            for c in range(2):
+                at = 3 * ROWS * c
+                adj[c, :, 0:COLS] = prod[at : at + 32] + prod[at + 32 : at + 64] + prod[at + 64 : at + 96]
+        else:
+            group = row // SPAN
+            for i in range(ROWS):
+                base = slice(8 * (i // 8), 8 * (i // 8) + 8)
+                keep = [(sub == i % 8) & (group[base] == g) for g in range(ROWS // SPAN)]
+                edge_lhs[:, COLS * i : COLS * i + COLS] = jnp.concatenate(
+                    [jnp.where(m, p[base], 0.0) for m in keep for p in parts], axis=0
+                ).astype(bf16)
+            prod = contract_last(edge_lhs[...], (right_hot if k else left_hot)[...])
+            halo[k] = [
+                [jnp.sum(prod[at : at + 24], axis=0, keepdims=True) for at in (48 * g, 48 * g + 24)]
+                for g in range(ROWS // SPAN)
+            ]
     for c in range(2):
-        adj[c, :, 0:COLS] = results[1][c]
-        adj[c, :, COLS:] = jnp.where(lane < 8, results[2][c], jnp.where(lane >= 120, results[0][c], 0.0))
+        for q in range(4):
+            first_row = 8 * q % SPAN
+            where = ((first_row % 16 + sub) * 8 + lane % 8) % COLS
+            sides = []
+            for k in (2, 0):
+                line = halo[k][8 * q // SPAN][c]
+                line = line[:, 8 * (first_row - first_row % 16) :][:, :COLS]
+                if line.shape[1] < COLS:
+                    line = jnp.concatenate([line, line], axis=1)
+                sides.append(jnp.take_along_axis(jnp.broadcast_to(line, (8, COLS)), where, axis=1))
+            adj[c, 8 * q : 8 * q + 8, COLS:] = jnp.where(lane < 8, sides[0], jnp.where(lane >= 120, sides[1], 0.0))
     first[...] = adj[:, 0:8, :]
     last[...] = adj[:, ROWS - 8 : ROWS, :]
 
@@ -271,16 +334,22 @@
     out[...] = jnp.dot(rows, gather, precision=lax.Precision.HIGHEST, preferred_element_type=f32)
 
 
-def call(kernel, outs, args, scratch=()):
-    vmem = pl.BlockSpec(memory_space=pltpu.VMEM)
+def call(kernel, outs, args, far=(), scratch=(), cost=0, limit=8):
+    far = [pltpu.with_memory_space_constraint(x, pltpu.HBM) for x in far]
+    near = pl.BlockSpec(memory_space=pltpu.VMEM)
     return pl.pallas_call(
         kernel,
-        out_shape=tuple(jax.ShapeDtypeStruct(s, f32) for s in outs),
-        in_specs=[vmem] * len(args),
-        out_specs=(vmem,) * len(outs),
+        out_shape=tuple(outs),
+        in_specs=[near] * len(args) + [pl.BlockSpec(memory_space=pltpu.HBM)] * len(far),
+        out_specs=(near,) * len(outs),
         scratch_shapes=list(scratch),
-        compiler_params=pltpu.CompilerParams(vmem_limit_bytes=24 * 1024 * 1024),
-    )(*args)
+        cost_estimate=pl.CostEstimate(flops=cost, bytes_accessed=0, transcendentals=0) if cost else None,
+        compiler_params=pltpu.CompilerParams(vmem_limit_bytes=limit * 1024 * 1024),
+    )(*args, *far)
+
+
+def near(*shape, dtype=f32):
+    return pltpu.VMEM(shape, dtype)
 
 
 def per_device(forcing, strength, mask, send_cell, send_code, recv_buoy, observed):
@@ -289,37 +358,70 @@
     codes = send_code.reshape(ROWS, COLS)
     recv = recv_buoy.reshape(ROWS, COLS)
     observed = observed.reshape(2, BUOYS)
-    tables = lax.all_gather(jnp.stack([cells, codes]), "gy")
-    (packed,) = call(pack_kernel, [(OWNERS, 24, COLS)], (forcing, strength, mask, recv))
+    entries = ROWS * COLS
+    packed, own, table, observed = call(
+        pack_kernel,
+        [near(OWNERS, 12, COLS), near(4, ROWS, COLS), near(2, ROWS, COLS, dtype=jnp.int32), near(2, BUOYS)],
+        (),
+        (forcing, strength, mask, recv, cells, codes, observed),
+        [
+            near(2, ROWS, COLS),
+            near(ROWS // 8, COLS // 8),
+            near(ROWS, COLS, dtype=jnp.int32),
+            near(ROWS, COLS, dtype=jnp.int32),
+            pltpu.SemaphoreType.DMA((7,)),
+        ],
+    )
     received = lax.all_to_all(packed, "gy", 0, 0, tiled=True)
     ext, first, last = call(
         widen_kernel,
-        [(4, ROWS, 2 * COLS), (4, 8, 2 * COLS), (4, 8, 2 * COLS)],
-        (received, forcing, strength, mask),
+        [near(4, ROWS, 2 * COLS), near(4, 8, 2 * COLS), near(4, 8, 2 * COLS)],
+        (received, own),
     )
     above = from_behind(last, "gx", 1)
     below = from_behind(first, "gx", -1)
+    table, slot_hot, col_hot = call(
+        own_kernel,
+        [
+            near(3, ROWS, COLS, dtype=jnp.int32),
+            near(BUOYS, entries, dtype=bf16),
+            near(COLS, entries, dtype=bf16),
+        ],
+        (received, table),
+        cost=10**9,
+    )
     sums, rates, window = call(
         forward_kernel,
-        [(OWNERS, 2 * OWNERS, BUOYS), (SUBCYCLES - 1, 3, ROWS, COLS), (2, WIN, 2 * COLS)],
-        (ext, above, below, cells, codes, received, observed),
-        [pltpu.VMEM((2, ROWS, COLS), f32)],
+        [near(OWNERS, 2 * OWNERS, BUOYS), near(SUBCYCLES - 1, 3, ROWS, COLS), near(2, WIN, 2 * COLS)],
+        (ext, above, below, slot_hot, table, observed),
+        (),
+        [near(2, ROWS, COLS)],
     )
     sums = lax.all_to_all(sums, "gy", 0, 0, tiled=True)
+    left_table = from_behind(table, "gy", 1)
+    right_table = from_behind(table, "gy", -1)
+    left_hot, right_hot = call(
+        edge_kernel,
+        [near(8 * SPAN, entries, dtype=bf16), near(8 * SPAN, entries, dtype=bf16)],
+        (left_table, right_table),
+        cost=10**9,
+    )
     misfit, adj, first, last = call(
         scatter_kernel,
-        [(2, BUOYS), (2, ROWS, 2 * COLS), (2, 8, 2 * COLS), (2, 8, 2 * COLS)],
-        (sums, tables, received),
         [
-            pltpu.VMEM((2 * OWNERS, BUOYS), f32),
-            pltpu.VMEM((6 * ROWS, ROWS * COLS), bf16),
-            pltpu.VMEM((COLS, ROWS * COLS), bf16),
+            jax.ShapeDtypeStruct((2, BUOYS), f32),
+            near(2, ROWS, 2 * COLS),
+            near(2, 8, 2 * COLS),
+            near(2, 8, 2 * COLS),
         ],
+        (sums, left_table, table, right_table, col_hot, left_hot, right_hot),
+        (),
+        [near(2 * OWNERS, BUOYS), near(6 * ROWS, entries, dtype=bf16), near(48 * ROWS // SPAN, entries, dtype=bf16)],
     )
     above = from_behind(last, "gx", 1)
     below = from_behind(first, "gx", -1)
-    (coarse,) = call(adjoint_kernel, [(ROWS // 8, COLS // 8)], (adj, above, below, window, rates))
-    gradient = lax.psum(coarse, "member")
+    (coarse,) = call(adjoint_kernel, [near(ROWS // 8, COLS // 8)], (adj, above, below, window, rates))
+    gradient = jnp.sum(lax.all_gather(coarse, "member"), axis=0)
     return (misfit[None, None, None], gradient)
 
 

time: 92.5 us -> 70.7 us (0.76)
  the two profiles are of different devices: /device:TPU:56 before, /device:TPU:57 now
where the time goes in v2:
time: 70.7 us; the launch traced here: 70.3 us
  blocking collectives  28 us (40%)
  starting transfers between devices  19.7 us (28%)
  waiting for transfers between devices  12.4 us (18%)
  Pallas kernels  8.86 us (13%)
  between operations  0.74 us (1%)
    all_to_all x1, blocking collectives, per_device(): received = lax.all_to_all(packed, 'gy', 0, 0, tiled=True)  17.1 us
    ppermute x6, starting transfers between devices, from_behind(): return lax.ppermute(x, axis, pairs)  16.3 us
    ppermute x6, waiting for transfers between devices, from_behind(): return lax.ppermute(x, axis, pairs)  11.3 us
    all_gather x1, blocking collectives, per_device(): gradient = jnp.sum(lax.all_gather(coarse, 'member'), axis=0)  10.9 us
    pallas_call x7, Pallas kernels, call(): pl.pallas_call(kernel, out_shape=tuple(outs), in_specs=[near] * len(args)...  8.86 us
    all_to_all x1, starting transfers between devices, per_device(): sums = lax.all_to_all(sums, 'gy', 0, 0, tiled=True)  3.37 us
  transfers between devices with their start and end apart: 7, of which 4 were waited for; matrix products, arithmetic and copies ran while one was open for 0% of the time, Pallas kernels for 2%

profile of v2, /device:TPU:57, one launch (start us, length us, event | category | flops | bytes accessed | tf_op | source)
XLA Modules:
  0.0 70.3 jit_solution(4854838276824481086)
XLA Ops:
  0.6 1.1 %shard_map.86 = (f32[8,12,128]{2,1,0:T(8,128)S(1)}, f32[4,32,128]{2,1,0:T(8,128)S(1)}, s32[2,32,128]{2,1,0:T(8,128)S(1)}, f32[2,256]{1,0:T(2,128)S(1)}) custom-call(f32[2,32,128]{2,1,0:T(8,128)} %bitcast.8, f32[4,16]{1,0:T(4,128)} %strength_in.1, s32[32,128]{1,0:T(8,128)} %mask_in.1, s32[32,128]{1,0:T(8,128)} %bitcast.9, s32[32,128]{1,0:T(8,128)} %bitcast.10, ...), custom_call_target="tpu_custom_call" | custom-call | tf_op jit(solution)/shard_map/pallas_call | solution.py:340
  1.7 17.1 %all_to_all.10.received = f32[8,12,128]{2,1,0:T(8,128)S(1)} all-to-all(f32[8,12,128]{2,1,0:T(8,128)S(1)} %get-tuple-element.21), channel_id=1, replica_groups=mesh['member'=4,'gx'=16,'gy'=8] {'gy'}, dimensions={0} | all-to-all | bytes 98304 | tf_op jit(solution)/shard_map/all_to_all | solution.py:375
  18.8 0.1 shard_map.87
  18.9 3.9 %collective-permute-start = (f32[4,8,256]{2,1,0:T(8,128)S(1)}, f32[4,8,256]{2,1,0:T(8,128)S(1)}, u32[]{:S(2)}, u32[]{:S(2)}) collective-permute-start(f32[4,8,256]{2,1,0:T(8,128)S(1)} %get-tuple-element.24), channel_id=1, source_target_pairs={{0,8},{8,16},{16,24},{24,32},{32,40},{40,48},{48,56},{56,64},{64,7... | collective-permute-start | bytes 98312 | tf_op jit(solution)/shard_map/ppermute | solution.py:29
  22.8 1.9 %collective-permute-start.1 = (f32[4,8,256]{2,1,0:T(8,128)S(1)}, f32[4,8,256]{2,1,0:T(8,128)S(1)}, u32[]{:S(2)}, u32[]{:S(2)}) collective-permute-start(f32[4,8,256]{2,1,0:T(8,128)S(1)} %get-tuple-element.25), channel_id=1, source_target_pairs={{8,0},{16,8},{24,16},{32,24},{40,32},{48,40},{56,48},{64,56},{72,6... | collective-permute-start | bytes 98312 | tf_op jit(solution)/shard_map/ppermute | solution.py:29
  24.7 0.9 %shard_map.88 = (s32[3,32,128]{2,1,0:T(8,128)S(1)}, bf16[256,4096]{1,0:T(8,128)(2,1)S(1)}, bf16[128,4096]{1,0:T(8,128)(2,1)S(1)}) custom-call(f32[8,12,128]{2,1,0:T(8,128)S(1)} %all_to_all.10.received, s32[2,32,128]{2,1,0:T(8,128)S(1)} %get-tuple-element.26.table), custom_call_target="tpu_custom_call" | custom-call | flops 1000000000 | tf_op jit(solution)/shard_map/pallas_call | solution.py:340
  25.6 0.0 collective-permute-done.above
  25.6 5.4 %collective-permute-done.1.below = f32[4,8,256]{2,1,0:T(8,128)S(1)} collective-permute-done((f32[4,8,256]{2,1,0:T(8,128)S(1)}, f32[4,8,256]{2,1,0:T(8,128)S(1)}, u32[]{:S(2)}, u32[]{:S(2)}) %collective-permute-start.1) | collective-permute-done | bytes 32800 | tf_op jit(solution)/shard_map/ppermute | solution.py:29
  31.0 2.7 %shard_map.89 = (f32[8,16,256]{2,1,0:T(8,128)}, f32[7,3,32,128]{3,2,1,0:T(8,128)S(1)}, f32[2,48,256]{2,1,0:T(8,128)S(1)}) custom-call(f32[4,32,256]{2,1,0:T(8,128)S(1)} %get-tuple-element.23.ext, f32[4,8,256]{2,1,0:T(8,128)S(1)} %collective-permute-done.above, f32[4,8,256]{2,1,0:T(8,128)S(1)} %collective-permute-done.1.below, ...), custom_call_target="tpu_custom_call" | custom-call | tf_op jit(solution)/shard_map/pallas_call | solution.py:340
  33.7 3.4 %all-to-all-start.1 = ((f32[8,16,256]{2,1,0:T(8,128)}), f32[8,16,256]{2,1,0:T(8,128)S(1)}, u32[]{:S(2)}, u32[]{:S(2)}) async-start(f32[8,16,256]{2,1,0:T(8,128)} %get-tuple-element.30), calls=%async_computation.1 | async-start | bytes 262144 | tf_op jit(solution)/shard_map/all_to_all | solution.py:400
  37.1 1.3 %collective-permute-start.3 = (s32[3,32,128]{2,1,0:T(8,128)S(1)}, s32[3,32,128]{2,1,0:T(8,128)S(1)}, u32[]{:S(2)}, u32[]{:S(2)}) collective-permute-start(s32[3,32,128]{2,1,0:T(8,128)S(1)} %get-tuple-element.28.table.own_table), channel_id=1, source_target_pairs={{1,0},{2,1},{3,2},{4,3},{5,4},{6,5},{7,6},{9,8},{10,9},{11,10},{12... | collective-permute-start | bytes 147464 | tf_op jit(solution)/shard_map/ppermute | solution.py:29
  38.4 4.0 %collective-permute-start.2 = (s32[3,32,128]{2,1,0:T(8,128)S(1)}, s32[3,32,128]{2,1,0:T(8,128)S(1)}, u32[]{:S(2)}, u32[]{:S(2)}) collective-permute-start(s32[3,32,128]{2,1,0:T(8,128)S(1)} %get-tuple-element.28.table.own_table), channel_id=1, source_target_pairs={{0,1},{1,2},{2,3},{3,4},{4,5},{5,6},{6,7},{8,9},{9,10},{10,11},{11... | collective-permute-start | bytes 147464 | tf_op jit(solution)/shard_map/ppermute | solution.py:29
  42.4 0.0 collective-permute-done.3.right_table
  42.4 1.1 %collective-permute-done.2.left_table = s32[3,32,128]{2,1,0:T(8,128)S(1)} collective-permute-done((s32[3,32,128]{2,1,0:T(8,128)S(1)}, s32[3,32,128]{2,1,0:T(8,128)S(1)}, u32[]{:S(2)}, u32[]{:S(2)}) %collective-permute-start.2) | collective-permute-done | bytes 49184 | tf_op jit(solution)/shard_map/ppermute | solution.py:29
  43.6 0.3 shard_map.90
  43.9 1.1 %all-to-all-done.1.sums = f32[8,16,256]{2,1,0:T(8,128)S(1)} async-done(((f32[8,16,256]{2,1,0:T(8,128)}), f32[8,16,256]{2,1,0:T(8,128)S(1)}, u32[]{:S(2)}, u32[]{:S(2)}) %all-to-all-start.1) | async-done | bytes 131104 | tf_op jit(solution)/shard_map/all_to_all | solution.py:400
  44.9 2.5 %shard_map.91 = (f32[2,256]{1,0:T(2,128)}, f32[2,32,256]{2,1,0:T(8,128)S(1)}, f32[2,8,256]{2,1,0:T(8,128)S(1)}, f32[2,8,256]{2,1,0:T(8,128)S(1)}) custom-call(f32[8,16,256]{2,1,0:T(8,128)S(1)} %all-to-all-done.1.sums, s32[3,32,128]{2,1,0:T(8,128)S(1)} %collective-permute-done.2.left_table, s32[3,32,128]{2,1,0:T(8,128)S(1)} %get-tuple-element.28.table.own_table, ...), custom_call_target="tpu_custom_call" | custom-call | tf_op jit(solution)/shard_map/pallas_call | solution.py:340
  47.5 1.9 %collective-permute-start.4 = (f32[2,8,256]{2,1,0:T(8,128)S(1)}, f32[2,8,256]{2,1,0:T(8,128)S(1)}, u32[]{:S(2)}, u32[]{:S(2)}) collective-permute-start(f32[2,8,256]{2,1,0:T(8,128)S(1)} %get-tuple-element.36), channel_id=1, source_target_pairs={{0,8},{8,16},{16,24},{24,32},{32,40},{40,48},{48,56},{56,64},{64,7... | collective-permute-start | bytes 49160 | tf_op jit(solution)/shard_map/ppermute | solution.py:29
  49.4 3.4 %collective-permute-start.5 = (f32[2,8,256]{2,1,0:T(8,128)S(1)}, f32[2,8,256]{2,1,0:T(8,128)S(1)}, u32[]{:S(2)}, u32[]{:S(2)}) collective-permute-start(f32[2,8,256]{2,1,0:T(8,128)S(1)} %get-tuple-element.37), channel_id=1, source_target_pairs={{8,0},{16,8},{24,16},{32,24},{40,32},{48,40},{56,48},{64,56},{72,6... | collective-permute-start | bytes 49160 | tf_op jit(solution)/shard_map/ppermute | solution.py:29
  52.8 0.0 collective-permute-done.4.above
  52.8 4.7 %collective-permute-done.5.below = f32[2,8,256]{2,1,0:T(8,128)S(1)} collective-permute-done((f32[2,8,256]{2,1,0:T(8,128)S(1)}, f32[2,8,256]{2,1,0:T(8,128)S(1)}, u32[]{:S(2)}, u32[]{:S(2)}) %collective-permute-start.5) | collective-permute-done | bytes 16416 | tf_op jit(solution)/shard_map/ppermute | solution.py:29
  57.5 1.2 %shard_map.92 = f32[4,16]{1,0:T(4,128)S(1)} custom-call(f32[2,32,256]{2,1,0:T(8,128)S(1)} %get-tuple-element.35.adj, f32[2,8,256]{2,1,0:T(8,128)S(1)} %collective-permute-done.4.above, f32[2,8,256]{2,1,0:T(8,128)S(1)} %collective-permute-done.5.below, f32[2,48,256]{2,1,0:T(8,128)S(1)} %get-tuple-element.38.window, f32[7,3,32,128]{3,2,1,0:T(8,128)S(1)} %get-tuple-element.39.rates), custom_call_target="tpu_custom_call" | custom-call | tf_op jit(solution)/shard_map/pallas_call | solution.py:340
  58.7 10.9 %all-gather.1 = f32[4,4,16]{2,1,0:T(4,128)S(1)} all-gather(f32[1,4,16]{2,1,0:T(4,128)S(1)} %bitcast.7), channel_id=2, replica_groups=mesh['member'=4,'gx'=16,'gy'=8] {'member'}, dimensions={0}, use_global_device_ids=true | all-gather | bytes 1280 | tf_op jit(solution)/shard_map/all_gather | solution.py:424
  69.7 0.6 reduce_sum.9
Async XLA Ops:
  18.9 6.7 %collective-permute-start = (f32[4,8,256]{2,1,0:T(8,128)S(1)}, f32[4,8,256]{2,1,0:T(8,128)S(1)}, u32[]{:S(2)}, u32[]{:S(2)}) collective-permute-start(f32[4,8,256]{2,1,0:T(8,128)S(1)} %get-tuple-element.24), channel_id=1, source_target_pairs={{0,8},{8,16},{16,24},{24,32},{32,40},{40,48},{48,56},{56,64},{64,7... | collective-permute-start | bytes 98312 | tf_op jit(solution)/shard_map/ppermute | solution.py:29
  22.8 8.3 %collective-permute-start.1 = (f32[4,8,256]{2,1,0:T(8,128)S(1)}, f32[4,8,256]{2,1,0:T(8,128)S(1)}, u32[]{:S(2)}, u32[]{:S(2)}) collective-permute-start(f32[4,8,256]{2,1,0:T(8,128)S(1)} %get-tuple-element.25), channel_id=1, source_target_pairs={{8,0},{16,8},{24,16},{32,24},{40,32},{48,40},{56,48},{64,56},{72,6... | collective-permute-start | bytes 98312 | tf_op jit(solution)/shard_map/ppermute | solution.py:29
  33.7 11.2 %all-to-all-start.1 = ((f32[8,16,256]{2,1,0:T(8,128)}), f32[8,16,256]{2,1,0:T(8,128)S(1)}, u32[]{:S(2)}, u32[]{:S(2)}) async-start(f32[8,16,256]{2,1,0:T(8,128)} %get-tuple-element.30), calls=%async_computation.1 | async-start | bytes 262144 | tf_op jit(solution)/shard_map/all_to_all | solution.py:400
  37.1 5.3 %collective-permute-start.3 = (s32[3,32,128]{2,1,0:T(8,128)S(1)}, s32[3,32,128]{2,1,0:T(8,128)S(1)}, u32[]{:S(2)}, u32[]{:S(2)}) collective-permute-start(s32[3,32,128]{2,1,0:T(8,128)S(1)} %get-tuple-element.28.table.own_table), channel_id=1, source_target_pairs={{1,0},{2,1},{3,2},{4,3},{5,4},{6,5},{7,6},{9,8},{10,9},{11,10},{12... | collective-permute-start | bytes 147464 | tf_op jit(solution)/shard_map/ppermute | solution.py:29
  38.4 5.2 %collective-permute-start.2 = (s32[3,32,128]{2,1,0:T(8,128)S(1)}, s32[3,32,128]{2,1,0:T(8,128)S(1)}, u32[]{:S(2)}, u32[]{:S(2)}) collective-permute-start(s32[3,32,128]{2,1,0:T(8,128)S(1)} %get-tuple-element.28.table.own_table), channel_id=1, source_target_pairs={{0,1},{1,2},{2,3},{3,4},{4,5},{5,6},{6,7},{8,9},{9,10},{10,11},{11... | collective-permute-start | bytes 147464 | tf_op jit(solution)/shard_map/ppermute | solution.py:29
  47.5 5.3 %collective-permute-start.4 = (f32[2,8,256]{2,1,0:T(8,128)S(1)}, f32[2,8,256]{2,1,0:T(8,128)S(1)}, u32[]{:S(2)}, u32[]{:S(2)}) collective-permute-start(f32[2,8,256]{2,1,0:T(8,128)S(1)} %get-tuple-element.36), channel_id=1, source_target_pairs={{0,8},{8,16},{16,24},{24,32},{32,40},{40,48},{48,56},{56,64},{64,7... | collective-permute-start | bytes 49160 | tf_op jit(solution)/shard_map/ppermute | solution.py:29
  49.4 8.1 %collective-permute-start.5 = (f32[2,8,256]{2,1,0:T(8,128)S(1)}, f32[2,8,256]{2,1,0:T(8,128)S(1)}, u32[]{:S(2)}, u32[]{:S(2)}) collective-permute-start(f32[2,8,256]{2,1,0:T(8,128)S(1)} %get-tuple-element.37), channel_id=1, source_target_pairs={{8,0},{16,8},{24,16},{32,24},{40,32},{48,40},{56,48},{64,56},{72,6... | collective-permute-start | bytes 49160 | tf_op jit(solution)/shard_map/ppermute | solution.py:29

commit v3 on v2

--- a/solution.py
+++ b/solution.py
@@ -29,6 +29,28 @@
     return lax.ppermute(x, axis, pairs)
 
 
+def facing_rows(first, last):
+    even = lax.axis_index("gx") % 2 == 0
+    return jnp.where(even, last, first), jnp.where(even, first, last)
+
+
+def above_below(pair, other, f):
+    a = lax.axis_index("gx")
+    near = pair[1 - a % 2, f]
+    far = other[f]
+    even = a % 2 == 0
+    return jnp.where(even, far, near), jnp.where(even, near, far)
+
+
+def exchange_rows(to_pair, to_other):
+    count = lax.axis_size("gx")
+    swaps = [(i, i + 1) for i in range(1, count - 1, 2)]
+    other = lax.ppermute(to_other, "gx", swaps + [(j, i) for i, j in swaps])
+    groups = [[i, i + 1] for i in range(0, count, 2)]
+    pair = lax.all_gather(to_pair, "gx", axis_index_groups=groups)
+    return pair, other
+
+
 def iota(shape, dim):
     return lax.broadcasted_iota(jnp.int32, shape, dim)
 
@@ -42,6 +64,16 @@
 
 def contract_last(a, b):
     return lax.dot_general(a, b, (((1,), (1,)), ((), ())), preferred_element_type=f32)
+
+
+def keep_parts(ref, parts):
+    for p, part in enumerate(parts):
+        ref[ROWS * p : ROWS * p + ROWS, :] = part
+    ref[ROWS * len(parts) :, :] = jnp.zeros((ROWS * (8 - len(parts)), COLS), f32)
+
+
+def parts_of_row(ref, i):
+    return ref[pl.ds(i, 8, stride=ROWS), :]
 
 
 def tile_fields(forcing, strength, mask):
@@ -84,7 +116,7 @@
         out[d, 8:12, :] = slots[4 * d : 4 * d + 4]
 
 
-def widen_kernel(received, own, ext, first, last):
+def widen_kernel(received, own, ext, to_pair, to_other):
     b = lax.axis_index("gy")
     lane = iota((8, COLS), 1)
     from_left = received[jnp.maximum(b - 1, 0), 0:8, :] * (b > 0).astype(f32)
@@ -96,8 +128,7 @@
             low = pltpu.roll(from_right, (COLS - at) % COLS, 1) if at else from_right
             high = pltpu.roll(from_left, (120 - at) % COLS, 1)
             ext[f, 8 * g : 8 * g + 8, COLS:] = jnp.where(lane < 8, low, jnp.where(lane >= 120, high, 0.0))
-    first[...] = ext[:, 0:8, :]
-    last[...] = ext[:, ROWS - 8 : ROWS, :]
+    to_pair[...], to_other[...] = facing_rows(ext[:, 0:8, :], ext[:, ROWS - 8 : ROWS, :])
 
 
 def next_row(x):
@@ -132,11 +163,13 @@
         col_hot[:, at] = jnp.where(col_ids == col[i : i + 1, :], weight[i : i + 1, :], 0.0).astype(bf16)
 
 
-def forward_kernel(ext, above, below, hot, table, observed, sums, rates, window, vel):
+def forward_kernel(ext, pair, other, hot, table, observed, sums, rates, window, vel, kept):
     b = lax.axis_index("gy")
-    force_x, force_y, cover, visc = (
-        jnp.concatenate([above[f], ext[f], below[f]], axis=0) for f in range(4)
-    )
+    fields = []
+    for f in range(4):
+        above, below = above_below(pair, other, f)
+        fields.append(jnp.concatenate([above, ext[f], below], axis=0))
+    force_x, force_y, cover, visc = fields
     window[0] = cover
     window[1] = visc
     tau_x = step_size * cover * force_x
@@ -178,21 +211,14 @@
         got_u = jnp.where(hit, jnp.take_along_axis(line_u, col, axis=1), got_u)
         got_v = jnp.where(hit, jnp.take_along_axis(line_v, col, axis=1), got_v)
     weight = table[1].astype(f32) * (1.0 / 16.0)
-    parts = split3(got_u * weight) + split3(got_v * weight)
-    sub = iota((8, COLS), 0)
+    keep_parts(kept, split3(got_u * weight) + split3(got_v * weight))
     blocks = []
     for d in range(OWNERS):
-        base = 8 * (d // 2)
-        left = []
-        for i in range(4):
-            keep = sub == 4 * (d % 2) + i
-            left.append(
-                jnp.concatenate([jnp.where(keep, p[base : base + 8], 0.0) for p in parts], axis=0).astype(bf16)
-            )
-        prod = contract_last(jnp.concatenate(left, axis=1), hot[:, 4 * COLS * d : 4 * COLS * d + 4 * COLS])
+        left = jnp.concatenate([parts_of_row(kept, 4 * d + i) for i in range(4)], axis=1).astype(bf16)
+        prod = contract_last(left, hot[:, 4 * COLS * d : 4 * COLS * d + 4 * COLS])
         mine = (b == d).astype(f32)
-        blocks.append(jnp.sum(prod[0:24], axis=0, keepdims=True) - mine * observed[0:1, :])
-        blocks.append(jnp.sum(prod[24:48], axis=0, keepdims=True) - mine * observed[1:2, :])
+        blocks.append(jnp.sum(prod[0:3], axis=0, keepdims=True) - mine * observed[0:1, :])
+        blocks.append(jnp.sum(prod[3:6], axis=0, keepdims=True) - mine * observed[1:2, :])
     total = jnp.concatenate(blocks, axis=0)
     for d in range(OWNERS):
         sums[d] = total
@@ -212,8 +238,8 @@
 
 def scatter_kernel(
     sums, left_table, own_table, right_table, col_hot, left_hot, right_hot,
-    misfit, adj, first, last,
-    total, lhs, edge_lhs,
+    misfit, adj, to_pair, to_other,
+    total, kept, lhs, edge_lhs,
 ):
     b = lax.axis_index("gy")
     acc = sums[0]
@@ -270,16 +296,16 @@
                 at = 3 * ROWS * c
                 adj[c, :, 0:COLS] = prod[at : at + 32] + prod[at + 32 : at + 64] + prod[at + 64 : at + 96]
         else:
+            keep_parts(kept.at[k // 2], parts)
             group = row // SPAN
             for i in range(ROWS):
-                base = slice(8 * (i // 8), 8 * (i // 8) + 8)
-                keep = [(sub == i % 8) & (group[base] == g) for g in range(ROWS // SPAN)]
+                block = parts_of_row(kept.at[k // 2], i)
                 edge_lhs[:, COLS * i : COLS * i + COLS] = jnp.concatenate(
-                    [jnp.where(m, p[base], 0.0) for m in keep for p in parts], axis=0
+                    [jnp.where(group[i : i + 1, :] == g, block, 0.0) for g in range(ROWS // SPAN)], axis=0
                 ).astype(bf16)
             prod = contract_last(edge_lhs[...], (right_hot if k else left_hot)[...])
             halo[k] = [
-                [jnp.sum(prod[at : at + 24], axis=0, keepdims=True) for at in (48 * g, 48 * g + 24)]
+                [jnp.sum(prod[at : at + 3], axis=0, keepdims=True) for at in (8 * g, 8 * g + 3)]
                 for g in range(ROWS // SPAN)
             ]
     for c in range(2):
@@ -294,16 +320,19 @@
                     line = jnp.concatenate([line, line], axis=1)
                 sides.append(jnp.take_along_axis(jnp.broadcast_to(line, (8, COLS)), where, axis=1))
             adj[c, 8 * q : 8 * q + 8, COLS:] = jnp.where(lane < 8, sides[0], jnp.where(lane >= 120, sides[1], 0.0))
-    first[...] = adj[:, 0:8, :]
-    last[...] = adj[:, ROWS - 8 : ROWS, :]
-
-
-def adjoint_kernel(adj, above, below, window, rates, out):
+    to_pair[...], to_other[...] = facing_rows(adj[:, 0:8, :], adj[:, ROWS - 8 : ROWS, :])
+
+
+def adjoint_kernel(adj, pair, other, window, rates, out):
     cover = window[0]
     visc = window[1]
     scaled = step_size * cover
     third = 0.25 * visc
-    w0, w1 = (scaled * jnp.concatenate([above[c], adj[c], below[c]], axis=0) for c in range(2))
+    states = []
+    for c in range(2):
+        above, below = above_below(pair, other, c)
+        states.append(scaled * jnp.concatenate([above, adj[c], below], axis=0))
+    w0, w1 = states
     own = slice(HALO, HALO + ROWS)
     a = h = t = None
     grad = None
@@ -373,13 +402,12 @@
         ],
     )
     received = lax.all_to_all(packed, "gy", 0, 0, tiled=True)
-    ext, first, last = call(
+    ext, to_pair, to_other = call(
         widen_kernel,
         [near(4, ROWS, 2 * COLS), near(4, 8, 2 * COLS), near(4, 8, 2 * COLS)],
         (received, own),
     )
-    above = from_behind(last, "gx", 1)
-    below = from_behind(first, "gx", -1)
+    pair, other = exchange_rows(to_pair, to_other)
     table, slot_hot, col_hot = call(
         own_kernel,
         [
@@ -393,9 +421,9 @@
     sums, rates, window = call(
         forward_kernel,
         [near(OWNERS, 2 * OWNERS, BUOYS), near(SUBCYCLES - 1, 3, ROWS, COLS), near(2, WIN, 2 * COLS)],
-        (ext, above, below, slot_hot, table, observed),
+        (ext, pair, other, slot_hot, table, observed),
         (),
-        [near(2, ROWS, COLS)],
+        [near(2, ROWS, COLS), near(8 * ROWS, COLS)],
     )
     sums = lax.all_to_all(sums, "gy", 0, 0, tiled=True)
     left_table = from_behind(table, "gy", 1)
@@ -406,7 +434,7 @@
         (left_table, right_table),
         cost=10**9,
     )
-    misfit, adj, first, last = call(
+    misfit, adj, to_pair, to_other = call(
         scatter_kernel,
         [
             jax.ShapeDtypeStruct((2, BUOYS), f32),
@@ -416,11 +444,15 @@
         ],
         (sums, left_table, table, right_table, col_hot, left_hot, right_hot),
         (),
-        [near(2 * OWNERS, BUOYS), near(6 * ROWS, entries, dtype=bf16), near(48 * ROWS // SPAN, entries, dtype=bf16)],
-    )
-    above = from_behind(last, "gx", 1)
-    below = from_behind(first, "gx", -1)
-    (coarse,) = call(adjoint_kernel, [near(ROWS // 8, COLS // 8)], (adj, above, below, window, rates))
+        [
+            near(2 * OWNERS, BUOYS),
+            near(2, 8 * ROWS, COLS),
+            near(6 * ROWS, entries, dtype=bf16),
+            near(8 * ROWS // SPAN, entries, dtype=bf16),
+        ],
+    )
+    pair, other = exchange_rows(to_pair, to_other)
+    (coarse,) = call(adjoint_kernel, [near(ROWS // 8, COLS // 8)], (adj, pair, other, window, rates))
     gradient = jnp.sum(lax.all_gather(coarse, "member"), axis=0)
     return (misfit[None, None, None], gradient)
 

time: 70.7 us -> 65.9 us (0.932)
  the two profiles are of different devices: /device:TPU:57 before, /device:TPU:7 now
where the time goes in v3:
time: 65.9 us; the launch traced here: 65.5 us
  blocking collectives  34.5 us (52%)
  starting transfers between devices  18.2 us (28%)
  Pallas kernels  7.94 us (12%)
  waiting for transfers between devices  3.57 us (5%)
  between operations  0.71 us (1%)
    all_to_all x1, blocking collectives, per_device(): received = lax.all_to_all(packed, 'gy', 0, 0, tiled=True)  17.1 us
    all_gather x1, blocking collectives, per_device(): gradient = jnp.sum(lax.all_gather(coarse, 'member'), axis=0)  10.4 us
    ppermute x2, starting transfers between devices, exchange_rows(): other = lax.ppermute(to_other, 'gx', swaps + [(j, i) for i, j in swaps])  9.52 us
    pallas_call x7, Pallas kernels, call(): pl.pallas_call(kernel, out_shape=tuple(outs), in_specs=[near] * len(args)...  7.94 us
    all_gather x2, blocking collectives, exchange_rows(): pair = lax.all_gather(to_pair, 'gx', axis_index_groups=groups)  7 us
    ppermute x2, starting transfers between devices, from_behind(): return lax.ppermute(x, axis, pairs)  5.28 us
    all_to_all x1, starting transfers between devices, per_device(): sums = lax.all_to_all(sums, 'gy', 0, 0, tiled=True)  3.37 us
  transfers between devices with their start and end apart: 5, of which 3 were waited for; matrix products, arithmetic and copies ran while one was open for 0% of the time, Pallas kernels for 2%

profile of v3, /device:TPU:7, one launch (start us, length us, event | category | flops | bytes accessed | tf_op | source)
XLA Modules:
  0.0 65.5 jit_solution(18336189079515731267)
XLA Ops:
  0.6 1.1 %shard_map.86 = (f32[8,12,128]{2,1,0:T(8,128)S(1)}, f32[4,32,128]{2,1,0:T(8,128)S(1)}, s32[2,32,128]{2,1,0:T(8,128)S(1)}, f32[2,256]{1,0:T(2,128)S(1)}) custom-call(f32[2,32,128]{2,1,0:T(8,128)} %bitcast.12, f32[4,16]{1,0:T(4,128)} %strength_in.1, s32[32,128]{1,0:T(8,128)} %mask_in.1, s32[32,128]{1,0:T(8,128)} %bitcast.13, s32[32,128]{1,0:T(8,128)} %bitcast.14, ...), custom_call_target="tpu_custom_call" | custom-call | tf_op jit(solution)/shard_map/pallas_call | solution.py:369
  1.7 17.1 %all_to_all.10.received = f32[8,12,128]{2,1,0:T(8,128)S(1)} all-to-all(f32[8,12,128]{2,1,0:T(8,128)S(1)} %get-tuple-element.21), channel_id=1, replica_groups=mesh['member'=4,'gx'=16,'gy'=8] {'gy'}, dimensions={0} | all-to-all | bytes 98304 | tf_op jit(solution)/shard_map/all_to_all | solution.py:404
  18.8 0.1 shard_map.87
  18.9 5.9 %collective-permute-start = (f32[4,8,256]{2,1,0:T(8,128)S(1)}, f32[4,8,256]{2,1,0:T(8,128)S(1)}, u32[]{:S(2)}, u32[]{:S(2)}) collective-permute-start(f32[4,8,256]{2,1,0:T(8,128)S(1)} %get-tuple-element.25), channel_id=1, source_target_pairs={{8,16},{24,32},{40,48},{56,64},{72,80},{88,96},{104,112},{16,8},{3... | collective-permute-start | bytes 98312 | tf_op jit(solution)/shard_map/ppermute | solution.py:48
  24.8 0.9 %shard_map.88 = (s32[3,32,128]{2,1,0:T(8,128)S(1)}, bf16[256,4096]{1,0:T(8,128)(2,1)S(1)}, bf16[128,4096]{1,0:T(8,128)(2,1)S(1)}) custom-call(f32[8,12,128]{2,1,0:T(8,128)S(1)} %all_to_all.10.received, s32[2,32,128]{2,1,0:T(8,128)S(1)} %get-tuple-element.26.table), custom_call_target="tpu_custom_call" | custom-call | flops 1000000000 | tf_op jit(solution)/shard_map/pallas_call | solution.py:369
  25.8 3.7 %all-gather = f32[8,8,256]{2,1,0:T(8,128)S(1)} all-gather(f32[4,8,256]{2,1,0:T(8,128)S(1)} %get-tuple-element.24), channel_id=2, replica_groups={{0,8},{16,24},{32,40},{48,56},{64,72},{80,88},{96,104},{112,120},{1,9},..., dimensions={0}, use_global_device_ids=true | all-gather | bytes 98304 | tf_op jit(solution)/shard_map/all_gather | solution.py:50
  29.5 0.0 collective-permute-done.other
  29.5 2.7 %shard_map.89 = (f32[8,16,256]{2,1,0:T(8,128)}, f32[7,3,32,128]{3,2,1,0:T(8,128)S(1)}, f32[2,48,256]{2,1,0:T(8,128)S(1)}) custom-call(f32[4,32,256]{2,1,0:T(8,128)S(1)} %get-tuple-element.23.ext, f32[2,4,8,256]{3,2,1,0:T(8,128)S(1)} %bitcast.9, f32[4,8,256]{2,1,0:T(8,128)S(1)} %collective-permute-done.other, bf16[256,4096]{1,0:T(8,128)(2,1)S(1)} %get-tuple-element.27.hot, ...), custom_call_target="tpu_custom_call" | custom-call | tf_op jit(solution)/shard_map/pallas_call | solution.py:369
  32.2 3.4 %all-to-all-start.1 = ((f32[8,16,256]{2,1,0:T(8,128)}), f32[8,16,256]{2,1,0:T(8,128)S(1)}, u32[]{:S(2)}, u32[]{:S(2)}) async-start(f32[8,16,256]{2,1,0:T(8,128)} %get-tuple-element.30), calls=%async_computation.1 | async-start | bytes 262144 | tf_op jit(solution)/shard_map/all_to_all | solution.py:428
  35.6 1.3 %collective-permute-start.2 = (s32[3,32,128]{2,1,0:T(8,128)S(1)}, s32[3,32,128]{2,1,0:T(8,128)S(1)}, u32[]{:S(2)}, u32[]{:S(2)}) collective-permute-start(s32[3,32,128]{2,1,0:T(8,128)S(1)} %get-tuple-element.28.table.own_table), channel_id=1, source_target_pairs={{1,0},{2,1},{3,2},{4,3},{5,4},{6,5},{7,6},{9,8},{10,9},{11,10},{12... | collective-permute-start | bytes 147464 | tf_op jit(solution)/shard_map/ppermute | solution.py:29
  36.9 4.0 %collective-permute-start.1 = (s32[3,32,128]{2,1,0:T(8,128)S(1)}, s32[3,32,128]{2,1,0:T(8,128)S(1)}, u32[]{:S(2)}, u32[]{:S(2)}) collective-permute-start(s32[3,32,128]{2,1,0:T(8,128)S(1)} %get-tuple-element.28.table.own_table), channel_id=1, source_target_pairs={{0,1},{1,2},{2,3},{3,4},{4,5},{5,6},{6,7},{8,9},{9,10},{10,11},{11... | collective-permute-start | bytes 147464 | tf_op jit(solution)/shard_map/ppermute | solution.py:29
  40.9 0.0 collective-permute-done.2.right_table
  40.9 1.1 %collective-permute-done.1.left_table = s32[3,32,128]{2,1,0:T(8,128)S(1)} collective-permute-done((s32[3,32,128]{2,1,0:T(8,128)S(1)}, s32[3,32,128]{2,1,0:T(8,128)S(1)}, u32[]{:S(2)}, u32[]{:S(2)}) %collective-permute-start.1) | collective-permute-done | bytes 49184 | tf_op jit(solution)/shard_map/ppermute | solution.py:29
  42.0 0.3 shard_map.90
  42.3 1.2 %all-to-all-done.1.sums = f32[8,16,256]{2,1,0:T(8,128)S(1)} async-done(((f32[8,16,256]{2,1,0:T(8,128)}), f32[8,16,256]{2,1,0:T(8,128)S(1)}, u32[]{:S(2)}, u32[]{:S(2)}) %all-to-all-start.1) | async-done | bytes 131104 | tf_op jit(solution)/shard_map/all_to_all | solution.py:428
  43.5 1.6 %shard_map.91 = (f32[2,256]{1,0:T(2,128)}, f32[2,32,256]{2,1,0:T(8,128)S(1)}, f32[2,8,256]{2,1,0:T(8,128)S(1)}, f32[2,8,256]{2,1,0:T(8,128)S(1)}) custom-call(f32[8,16,256]{2,1,0:T(8,128)S(1)} %all-to-all-done.1.sums, s32[3,32,128]{2,1,0:T(8,128)S(1)} %collective-permute-done.1.left_table, s32[3,32,128]{2,1,0:T(8,128)S(1)} %get-tuple-element.28.table.own_table, ...), custom_call_target="tpu_custom_call" | custom-call | tf_op jit(solution)/shard_map/pallas_call | solution.py:369
  45.1 3.6 %collective-permute-start.3 = (f32[2,8,256]{2,1,0:T(8,128)S(1)}, f32[2,8,256]{2,1,0:T(8,128)S(1)}, u32[]{:S(2)}, u32[]{:S(2)}) collective-permute-start(f32[2,8,256]{2,1,0:T(8,128)S(1)} %get-tuple-element.37), channel_id=1, source_target_pairs={{8,16},{24,32},{40,48},{56,64},{72,80},{88,96},{104,112},{16,8},{3... | collective-permute-start | bytes 49160 | tf_op jit(solution)/shard_map/ppermute | solution.py:48
  48.7 3.3 %all-gather.1 = f32[4,8,256]{2,1,0:T(8,128)S(1)} all-gather(f32[2,8,256]{2,1,0:T(8,128)S(1)} %get-tuple-element.36), channel_id=3, replica_groups={{0,8},{16,24},{32,40},{48,56},{64,72},{80,88},{96,104},{112,120},{1,9},..., dimensions={0}, use_global_device_ids=true | all-gather | bytes 49152 | tf_op jit(solution)/shard_map/all_gather | solution.py:50
  52.0 1.2 %collective-permute-done.3.other = f32[2,8,256]{2,1,0:T(8,128)S(1)} collective-permute-done((f32[2,8,256]{2,1,0:T(8,128)S(1)}, f32[2,8,256]{2,1,0:T(8,128)S(1)}, u32[]{:S(2)}, u32[]{:S(2)}) %collective-permute-start.3) | collective-permute-done | bytes 16416 | tf_op jit(solution)/shard_map/ppermute | solution.py:48
  53.2 1.2 %shard_map.92 = f32[4,16]{1,0:T(4,128)S(1)} custom-call(f32[2,32,256]{2,1,0:T(8,128)S(1)} %get-tuple-element.35.adj, f32[2,2,8,256]{3,2,1,0:T(8,128)S(1)} %bitcast.10, f32[2,8,256]{2,1,0:T(8,128)S(1)} %collective-permute-done.3.other, f32[2,48,256]{2,1,0:T(8,128)S(1)} %get-tuple-element.38.window, f32[7,3,32,128]{3,2,1,0:T(8,128)S(1)} %get-tuple-element.39.rates), custom_call_target="tpu_custom_call" | custom-call | tf_op jit(solution)/shard_map/pallas_call | solution.py:369
  54.5 10.4 %all-gather.3 = f32[4,4,16]{2,1,0:T(4,128)S(1)} all-gather(f32[1,4,16]{2,1,0:T(4,128)S(1)} %bitcast.11), channel_id=4, replica_groups=mesh['member'=4,'gx'=16,'gy'=8] {'member'}, dimensions={0}, use_global_device_ids=true | all-gather | bytes 1280 | tf_op jit(solution)/shard_map/all_gather | solution.py:456
  64.9 0.6 reduce_sum.9
Async XLA Ops:
  18.9 10.6 %collective-permute-start = (f32[4,8,256]{2,1,0:T(8,128)S(1)}, f32[4,8,256]{2,1,0:T(8,128)S(1)}, u32[]{:S(2)}, u32[]{:S(2)}) collective-permute-start(f32[4,8,256]{2,1,0:T(8,128)S(1)} %get-tuple-element.25), channel_id=1, source_target_pairs={{8,16},{24,32},{40,48},{56,64},{72,80},{88,96},{104,112},{16,8},{3... | collective-permute-start | bytes 98312 | tf_op jit(solution)/shard_map/ppermute | solution.py:48
  32.2 11.3 %all-to-all-start.1 = ((f32[8,16,256]{2,1,0:T(8,128)}), f32[8,16,256]{2,1,0:T(8,128)S(1)}, u32[]{:S(2)}, u32[]{:S(2)}) async-start(f32[8,16,256]{2,1,0:T(8,128)} %get-tuple-element.30), calls=%async_computation.1 | async-start | bytes 262144 | tf_op jit(solution)/shard_map/all_to_all | solution.py:428
  35.6 5.3 %collective-permute-start.2 = (s32[3,32,128]{2,1,0:T(8,128)S(1)}, s32[3,32,128]{2,1,0:T(8,128)S(1)}, u32[]{:S(2)}, u32[]{:S(2)}) collective-permute-start(s32[3,32,128]{2,1,0:T(8,128)S(1)} %get-tuple-element.28.table.own_table), channel_id=1, source_target_pairs={{1,0},{2,1},{3,2},{4,3},{5,4},{6,5},{7,6},{9,8},{10,9},{11,10},{12... | collective-permute-start | bytes 147464 | tf_op jit(solution)/shard_map/ppermute | solution.py:29
  36.9 5.2 %collective-permute-start.1 = (s32[3,32,128]{2,1,0:T(8,128)S(1)}, s32[3,32,128]{2,1,0:T(8,128)S(1)}, u32[]{:S(2)}, u32[]{:S(2)}) collective-permute-start(s32[3,32,128]{2,1,0:T(8,128)S(1)} %get-tuple-element.28.table.own_table), channel_id=1, source_target_pairs={{0,1},{1,2},{2,3},{3,4},{4,5},{5,6},{6,7},{8,9},{9,10},{10,11},{11... | collective-permute-start | bytes 147464 | tf_op jit(solution)/shard_map/ppermute | solution.py:29
  45.1 8.1 %collective-permute-start.3 = (f32[2,8,256]{2,1,0:T(8,128)S(1)}, f32[2,8,256]{2,1,0:T(8,128)S(1)}, u32[]{:S(2)}, u32[]{:S(2)}) collective-permute-start(f32[2,8,256]{2,1,0:T(8,128)S(1)} %get-tuple-element.37), channel_id=1, source_target_pairs={{8,16},{24,32},{40,48},{56,64},{72,80},{88,96},{104,112},{16,8},{3... | collective-permute-start | bytes 49160 | tf_op jit(solution)/shard_map/ppermute | solution.py:48

commit v4 on v3

--- a/solution.py
+++ b/solution.py
@@ -147,24 +147,16 @@
     return pltpu.roll(x, 1, 1)
 
 
-def own_kernel(received, table, table_out, slot_hot, col_hot):
+def forward_kernel(ext, pair, other, received, table, observed, sums, rates, window, table_out, vel, kept, hot, total, sems):
+    b = lax.axis_index("gy")
     slot_ids = iota((BUOYS, COLS), 0)
-    col_ids = iota((COLS, COLS), 0)
     slots = jnp.concatenate([received[d, 8:12, :] for d in range(OWNERS)], axis=0).astype(jnp.int32)
-    cell = table[0]
-    weight = table[1].astype(f32) * (1.0 / 16.0)
-    col = cell % COLS
-    table_out[0] = cell
+    table_out[0] = table[0]
     table_out[1] = table[1]
     table_out[2] = slots
     for i in range(ROWS):
         at = slice(COLS * i, COLS * i + COLS)
-        slot_hot[:, at] = (slot_ids == slots[i : i + 1, :]).astype(f32).astype(bf16)
-        col_hot[:, at] = jnp.where(col_ids == col[i : i + 1, :], weight[i : i + 1, :], 0.0).astype(bf16)
-
-
-def forward_kernel(ext, pair, other, hot, table, observed, sums, rates, window, vel, kept):
-    b = lax.axis_index("gy")
+        hot[:, at] = (slot_ids == slots[i : i + 1, :]).astype(f32).astype(bf16)
     fields = []
     for f in range(4):
         above, below = above_below(pair, other, f)
@@ -219,21 +211,28 @@
         mine = (b == d).astype(f32)
         blocks.append(jnp.sum(prod[0:3], axis=0, keepdims=True) - mine * observed[0:1, :])
         blocks.append(jnp.sum(prod[3:6], axis=0, keepdims=True) - mine * observed[1:2, :])
-    total = jnp.concatenate(blocks, axis=0)
-    for d in range(OWNERS):
-        sums[d] = total
-
-
-def edge_kernel(left_table, right_table, left_hot, right_hot):
+    total[...] = jnp.concatenate(blocks, axis=0)
+    copies = [pltpu.make_async_copy(total, sums.at[d], sems.at[d]) for d in range(OWNERS)]
+    for copy in copies:
+        copy.start()
+    for copy in copies:
+        copy.wait()
+
+
+def edge_kernel(own_table, left_table, right_table, col_hot, left_hot, right_hot):
     edge_ids = iota((8 * SPAN, COLS), 0)
-    for table, hot, first_col in ((left_table, left_hot, COLS - 8), (right_table, right_hot, 0)):
+    col_ids = iota((COLS, COLS), 0)
+    for table, hot, first_col in ((own_table, col_hot, None), (left_table, left_hot, COLS - 8), (right_table, right_hot, 0)):
         cell = table[0]
         weight = table[1].astype(f32) * (1.0 / 16.0)
         row, col = cell // COLS, cell % COLS
-        place = jnp.where((col >= first_col) & (col < first_col + 8), row % SPAN * 8 + col % 8, -1)
+        ids, place = col_ids, col
+        if first_col is not None:
+            ids = edge_ids
+            place = jnp.where((col >= first_col) & (col < first_col + 8), row % SPAN * 8 + col % 8, -1)
         for i in range(ROWS):
             at = slice(COLS * i, COLS * i + COLS)
-            hot[:, at] = jnp.where(edge_ids == place[i : i + 1, :], weight[i : i + 1, :], 0.0).astype(bf16)
+            hot[:, at] = jnp.where(ids == place[i : i + 1, :], weight[i : i + 1, :], 0.0).astype(bf16)
 
 
 def scatter_kernel(
@@ -323,7 +322,9 @@
     to_pair[...], to_other[...] = facing_rows(adj[:, 0:8, :], adj[:, ROWS - 8 : ROWS, :])
 
 
-def adjoint_kernel(adj, pair, other, window, rates, out):
+def adjoint_kernel(adj, pair, other, window, rates, misfit, out, misfit_out, sem):
+    copy = pltpu.make_async_copy(misfit, misfit_out, sem.at[0])
+    copy.start()
     cover = window[0]
     visc = window[1]
     scaled = step_size * cover
@@ -361,6 +362,7 @@
     )
     gather = (iota((COLS, 16), 0) // 8 == iota((COLS, 16), 1)).astype(f32)
     out[...] = jnp.dot(rows, gather, precision=lax.Precision.HIGHEST, preferred_element_type=f32)
+    copy.wait()
 
 
 def call(kernel, outs, args, far=(), scratch=(), cost=0, limit=8):
@@ -370,7 +372,7 @@
         kernel,
         out_shape=tuple(outs),
         in_specs=[near] * len(args) + [pl.BlockSpec(memory_space=pltpu.HBM)] * len(far),
-        out_specs=(near,) * len(outs),
+        out_specs=tuple(pl.BlockSpec(memory_space=o.memory_space) for o in outs),
         scratch_shapes=list(scratch),
         cost_estimate=pl.CostEstimate(flops=cost, bytes_accessed=0, transcendentals=0) if cost else None,
         compiler_params=pltpu.CompilerParams(vmem_limit_bytes=limit * 1024 * 1024),
@@ -408,36 +410,37 @@
         (received, own),
     )
     pair, other = exchange_rows(to_pair, to_other)
-    table, slot_hot, col_hot = call(
-        own_kernel,
-        [
+    sums, rates, window, table = call(
+        forward_kernel,
+        [
+            pltpu.HBM((OWNERS, 2 * OWNERS, BUOYS), f32),
+            near(SUBCYCLES - 1, 3, ROWS, COLS),
+            near(2, WIN, 2 * COLS),
             near(3, ROWS, COLS, dtype=jnp.int32),
+        ],
+        (ext, pair, other, received, table, observed),
+        (),
+        [
+            near(2, ROWS, COLS),
+            near(8 * ROWS, COLS),
             near(BUOYS, entries, dtype=bf16),
-            near(COLS, entries, dtype=bf16),
+            near(2 * OWNERS, BUOYS),
+            pltpu.SemaphoreType.DMA((OWNERS,)),
         ],
-        (received, table),
-        cost=10**9,
-    )
-    sums, rates, window = call(
-        forward_kernel,
-        [near(OWNERS, 2 * OWNERS, BUOYS), near(SUBCYCLES - 1, 3, ROWS, COLS), near(2, WIN, 2 * COLS)],
-        (ext, pair, other, slot_hot, table, observed),
-        (),
-        [near(2, ROWS, COLS), near(8 * ROWS, COLS)],
     )
     sums = lax.all_to_all(sums, "gy", 0, 0, tiled=True)
     left_table = from_behind(table, "gy", 1)
     right_table = from_behind(table, "gy", -1)
-    left_hot, right_hot = call(
+    col_hot, left_hot, right_hot = call(
         edge_kernel,
-        [near(8 * SPAN, entries, dtype=bf16), near(8 * SPAN, entries, dtype=bf16)],
-        (left_table, right_table),
+        [near(COLS, entries, dtype=bf16), near(8 * SPAN, entries, dtype=bf16), near(8 * SPAN, entries, dtype=bf16)],
+        (table, left_table, right_table),
         cost=10**9,
     )
     misfit, adj, to_pair, to_other = call(
         scatter_kernel,
         [
-            jax.ShapeDtypeStruct((2, BUOYS), f32),
+            near(2, BUOYS),
             near(2, ROWS, 2 * COLS),
             near(2, 8, 2 * COLS),
             near(2, 8, 2 * COLS),
@@ -452,7 +455,13 @@
         ],
     )
     pair, other = exchange_rows(to_pair, to_other)
-    (coarse,) = call(adjoint_kernel, [near(ROWS // 8, COLS // 8)], (adj, pair, other, window, rates))
+    coarse, misfit = call(
+        adjoint_kernel,
+        [near(ROWS // 8, COLS // 8), pltpu.HBM((2, BUOYS), f32)],
+        (adj, pair, other, window, rates, misfit),
+        (),
+        [pltpu.SemaphoreType.DMA((1,))],
+    )
     gradient = jnp.sum(lax.all_gather(coarse, "member"), axis=0)
     return (misfit[None, None, None], gradient)
 

time: 65.9 us -> 64.9 us (0.985)
  waiting for transfers between devices: 3.57 us -> 2.37 us
  starting transfers between devices: 18.2 us -> 19.1 us
  Pallas kernels: 7.94 us -> 7.15 us
    ppermute x2, starting transfers between devices: 9.52 us -> 10.5 us  [exchange_rows(): other = lax.ppermute(to_other, 'gx', swaps + [(j, i) for i, j in swaps])]
    ppermute x2, waiting for transfers between devices: 1.24 us -> 0.31 us  [exchange_rows(): other = lax.ppermute(to_other, 'gx', swaps + [(j, i) for i, j in swaps])]
    pallas_call x7 -> x6, Pallas kernels: 7.94 us -> 7.15 us  [call(): pl.pallas_call(kernel, out_shape=tuple(outs), in_specs=[near] * len(args)...]
  transfers between devices with their start and end apart: 5 -> 5, of which waited for: 3 -> 3; matrix products, arithmetic and copies ran while one was open for 0% -> 0% of each run, Pallas kernels for 2% -> 1%
where the time goes in v4:
time: 64.9 us; the launch traced here: 64.5 us
  blocking collectives  34.5 us (53%)
  starting transfers between devices  19.1 us (29%)
  Pallas kernels  7.15 us (11%)
  waiting for transfers between devices  2.37 us (4%)
  between operations  0.73 us (1%)
    all_to_all x1, blocking collectives, per_device(): received = lax.all_to_all(packed, 'gy', 0, 0, tiled=True)  17.1 us
    ppermute x2, starting transfers between devices, exchange_rows(): other = lax.ppermute(to_other, 'gx', swaps + [(j, i) for i, j in swaps])  10.5 us
    all_gather x1, blocking collectives, per_device(): gradient = jnp.sum(lax.all_gather(coarse, 'member'), axis=0)  10.4 us
    pallas_call x6, Pallas kernels, call(): pl.pallas_call(kernel, out_shape=tuple(outs), in_specs=[near] * len(args)...  7.15 us
    all_gather x2, blocking collectives, exchange_rows(): pair = lax.all_gather(to_pair, 'gx', axis_index_groups=groups)  7 us
    ppermute x2, starting transfers between devices, from_behind(): return lax.ppermute(x, axis, pairs)  5.28 us
    all_to_all x1, starting transfers between devices, per_device(): sums = lax.all_to_all(sums, 'gy', 0, 0, tiled=True)  3.38 us
  transfers between devices with their start and end apart: 5, of which 3 were waited for; matrix products, arithmetic and copies ran while one was open for 0% of the time, Pallas kernels for 1%

profile of v4, /device:TPU:7, one launch (start us, length us, event | category | flops | bytes accessed | tf_op | source)
XLA Modules:
  0.0 64.5 jit_solution(2389858660199351550)
XLA Ops:
  0.6 1.1 %shard_map.86 = (f32[8,12,128]{2,1,0:T(8,128)S(1)}, f32[4,32,128]{2,1,0:T(8,128)S(1)}, s32[2,32,128]{2,1,0:T(8,128)S(1)}, f32[2,256]{1,0:T(2,128)S(1)}) custom-call(f32[2,32,128]{2,1,0:T(8,128)} %bitcast.12, f32[4,16]{1,0:T(4,128)} %strength_in.1, s32[32,128]{1,0:T(8,128)} %mask_in.1, s32[32,128]{1,0:T(8,128)} %bitcast.13, s32[32,128]{1,0:T(8,128)} %bitcast.14, ...), custom_call_target="tpu_custom_call" | custom-call | tf_op jit(solution)/shard_map/pallas_call | solution.py:371
  1.7 17.1 %all_to_all.10.received = f32[8,12,128]{2,1,0:T(8,128)S(1)} all-to-all(f32[8,12,128]{2,1,0:T(8,128)S(1)} %get-tuple-element.22), channel_id=1, replica_groups=mesh['member'=4,'gx'=16,'gy'=8] {'gy'}, dimensions={0} | all-to-all | bytes 98304 | tf_op jit(solution)/shard_map/all_to_all | solution.py:406
  18.8 0.1 shard_map.87
  18.9 5.9 %collective-permute-start = (f32[4,8,256]{2,1,0:T(8,128)S(1)}, f32[4,8,256]{2,1,0:T(8,128)S(1)}, u32[]{:S(2)}, u32[]{:S(2)}) collective-permute-start(f32[4,8,256]{2,1,0:T(8,128)S(1)} %get-tuple-element.26), channel_id=1, source_target_pairs={{8,16},{24,32},{40,48},{56,64},{72,80},{88,96},{104,112},{16,8},{3... | collective-permute-start | bytes 98312 | tf_op jit(solution)/shard_map/ppermute | solution.py:48
  24.8 3.7 %all-gather = f32[8,8,256]{2,1,0:T(8,128)S(1)} all-gather(f32[4,8,256]{2,1,0:T(8,128)S(1)} %get-tuple-element.25), channel_id=2, replica_groups={{0,8},{16,24},{32,40},{48,56},{64,72},{80,88},{96,104},{112,120},{1,9},..., dimensions={0}, use_global_device_ids=true | all-gather | bytes 98304 | tf_op jit(solution)/shard_map/all_gather | solution.py:50
  28.6 0.0 collective-permute-done.other
  28.6 3.0 %shard_map.88 = (f32[8,16,256]{2,1,0:T(8,128)}, f32[7,3,32,128]{3,2,1,0:T(8,128)S(1)}, f32[2,48,256]{2,1,0:T(8,128)S(1)}, s32[3,32,128]{2,1,0:T(8,128)S(1)}) custom-call(f32[4,32,256]{2,1,0:T(8,128)S(1)} %get-tuple-element.24.ext, f32[2,4,8,256]{3,2,1,0:T(8,128)S(1)} %bitcast.9, f32[4,8,256]{2,1,0:T(8,128)S(1)} %collective-permute-done.other, ...), custom_call_target="tpu_custom_call" | custom-call | tf_op jit(solution)/shard_map/pallas_call | solution.py:371
  31.6 3.4 %all-to-all-start.1 = ((f32[8,16,256]{2,1,0:T(8,128)}), f32[8,16,256]{2,1,0:T(8,128)S(1)}, u32[]{:S(2)}, u32[]{:S(2)}) async-start(f32[8,16,256]{2,1,0:T(8,128)} %get-tuple-element.29), calls=%async_computation.1 | async-start | bytes 262144 | tf_op jit(solution)/shard_map/all_to_all | solution.py:431
  35.0 1.3 %collective-permute-start.2 = (s32[3,32,128]{2,1,0:T(8,128)S(1)}, s32[3,32,128]{2,1,0:T(8,128)S(1)}, u32[]{:S(2)}, u32[]{:S(2)}) collective-permute-start(s32[3,32,128]{2,1,0:T(8,128)S(1)} %get-tuple-element.30.own_table), channel_id=1, source_target_pairs={{1,0},{2,1},{3,2},{4,3},{5,4},{6,5},{7,6},{9,8},{10,9},{11,10},{12... | collective-permute-start | bytes 147464 | tf_op jit(solution)/shard_map/ppermute | solution.py:29
  36.3 4.0 %collective-permute-start.1 = (s32[3,32,128]{2,1,0:T(8,128)S(1)}, s32[3,32,128]{2,1,0:T(8,128)S(1)}, u32[]{:S(2)}, u32[]{:S(2)}) collective-permute-start(s32[3,32,128]{2,1,0:T(8,128)S(1)} %get-tuple-element.30.own_table), channel_id=1, source_target_pairs={{0,1},{1,2},{2,3},{3,4},{4,5},{5,6},{6,7},{8,9},{9,10},{10,11},{11... | collective-permute-start | bytes 147464 | tf_op jit(solution)/shard_map/ppermute | solution.py:29
  40.3 0.0 collective-permute-done.2.right_table
  40.3 1.1 %collective-permute-done.1.left_table = s32[3,32,128]{2,1,0:T(8,128)S(1)} collective-permute-done((s32[3,32,128]{2,1,0:T(8,128)S(1)}, s32[3,32,128]{2,1,0:T(8,128)S(1)}, u32[]{:S(2)}, u32[]{:S(2)}) %collective-permute-start.1) | collective-permute-done | bytes 49184 | tf_op jit(solution)/shard_map/ppermute | solution.py:29
  41.4 0.6 shard_map.89
  42.0 0.9 %all-to-all-done.1.sums = f32[8,16,256]{2,1,0:T(8,128)S(1)} async-done(((f32[8,16,256]{2,1,0:T(8,128)}), f32[8,16,256]{2,1,0:T(8,128)S(1)}, u32[]{:S(2)}, u32[]{:S(2)}) %all-to-all-start.1) | async-done | bytes 131104 | tf_op jit(solution)/shard_map/all_to_all | solution.py:431
  42.9 1.2 %shard_map.90 = (f32[2,256]{1,0:T(2,128)S(1)}, f32[2,32,256]{2,1,0:T(8,128)S(1)}, f32[2,8,256]{2,1,0:T(8,128)S(1)}, f32[2,8,256]{2,1,0:T(8,128)S(1)}) custom-call(f32[8,16,256]{2,1,0:T(8,128)S(1)} %all-to-all-done.1.sums, s32[3,32,128]{2,1,0:T(8,128)S(1)} %collective-permute-done.1.left_table, s32[3,32,128]{2,1,0:T(8,128)S(1)} %get-tuple-element.30.own_table, ...), custom_call_target="tpu_custom_call" | custom-call | tf_op jit(solution)/shard_map/pallas_call | solution.py:371
  44.1 4.5 %collective-permute-start.3 = (f32[2,8,256]{2,1,0:T(8,128)S(1)}, f32[2,8,256]{2,1,0:T(8,128)S(1)}, u32[]{:S(2)}, u32[]{:S(2)}) collective-permute-start(f32[2,8,256]{2,1,0:T(8,128)S(1)} %get-tuple-element.36), channel_id=1, source_target_pairs={{8,16},{24,32},{40,48},{56,64},{72,80},{88,96},{104,112},{16,8},{3... | collective-permute-start | bytes 49160 | tf_op jit(solution)/shard_map/ppermute | solution.py:48
  48.6 3.3 %all-gather.1 = f32[4,8,256]{2,1,0:T(8,128)S(1)} all-gather(f32[2,8,256]{2,1,0:T(8,128)S(1)} %get-tuple-element.35), channel_id=3, replica_groups={{0,8},{16,24},{32,40},{48,56},{64,72},{80,88},{96,104},{112,120},{1,9},..., dimensions={0}, use_global_device_ids=true | all-gather | bytes 49152 | tf_op jit(solution)/shard_map/all_gather | solution.py:50
  51.9 0.3 collective-permute-done.3.other
  52.2 1.3 %shard_map.91 = (f32[4,16]{1,0:T(4,128)S(1)}, f32[2,256]{1,0:T(2,128)}) custom-call(f32[2,32,256]{2,1,0:T(8,128)S(1)} %get-tuple-element.34.adj, f32[2,2,8,256]{3,2,1,0:T(8,128)S(1)} %bitcast.10, f32[2,8,256]{2,1,0:T(8,128)S(1)} %collective-permute-done.3.other, f32[2,48,256]{2,1,0:T(8,128)S(1)} %get-tuple-element.37.window, ...), custom_call_target="tpu_custom_call" | custom-call | tf_op jit(solution)/shard_map/pallas_call | solution.py:371
  53.4 10.4 %all-gather.3 = f32[4,4,16]{2,1,0:T(4,128)S(1)} all-gather(f32[1,4,16]{2,1,0:T(4,128)S(1)} %bitcast.11), channel_id=4, replica_groups=mesh['member'=4,'gx'=16,'gy'=8] {'member'}, dimensions={0}, use_global_device_ids=true | all-gather | bytes 1280 | tf_op jit(solution)/shard_map/all_gather | solution.py:465
  63.9 0.6 reduce_sum.9
Async XLA Ops:
  18.9 9.7 %collective-permute-start = (f32[4,8,256]{2,1,0:T(8,128)S(1)}, f32[4,8,256]{2,1,0:T(8,128)S(1)}, u32[]{:S(2)}, u32[]{:S(2)}) collective-permute-start(f32[4,8,256]{2,1,0:T(8,128)S(1)} %get-tuple-element.26), channel_id=1, source_target_pairs={{8,16},{24,32},{40,48},{56,64},{72,80},{88,96},{104,112},{16,8},{3... | collective-permute-start | bytes 98312 | tf_op jit(solution)/shard_map/ppermute | solution.py:48
  31.6 11.3 %all-to-all-start.1 = ((f32[8,16,256]{2,1,0:T(8,128)}), f32[8,16,256]{2,1,0:T(8,128)S(1)}, u32[]{:S(2)}, u32[]{:S(2)}) async-start(f32[8,16,256]{2,1,0:T(8,128)} %get-tuple-element.29), calls=%async_computation.1 | async-start | bytes 262144 | tf_op jit(solution)/shard_map/all_to_all | solution.py:431
  35.0 5.3 %collective-permute-start.2 = (s32[3,32,128]{2,1,0:T(8,128)S(1)}, s32[3,32,128]{2,1,0:T(8,128)S(1)}, u32[]{:S(2)}, u32[]{:S(2)}) collective-permute-start(s32[3,32,128]{2,1,0:T(8,128)S(1)} %get-tuple-element.30.own_table), channel_id=1, source_target_pairs={{1,0},{2,1},{3,2},{4,3},{5,4},{6,5},{7,6},{9,8},{10,9},{11,10},{12... | collective-permute-start | bytes 147464 | tf_op jit(solution)/shard_map/ppermute | solution.py:29
  36.3 5.2 %collective-permute-start.1 = (s32[3,32,128]{2,1,0:T(8,128)S(1)}, s32[3,32,128]{2,1,0:T(8,128)S(1)}, u32[]{:S(2)}, u32[]{:S(2)}) collective-permute-start(s32[3,32,128]{2,1,0:T(8,128)S(1)} %get-tuple-element.30.own_table), channel_id=1, source_target_pairs={{0,1},{1,2},{2,3},{3,4},{4,5},{5,6},{6,7},{8,9},{9,10},{10,11},{11... | collective-permute-start | bytes 147464 | tf_op jit(solution)/shard_map/ppermute | solution.py:29
  44.1 8.1 %collective-permute-start.3 = (f32[2,8,256]{2,1,0:T(8,128)S(1)}, f32[2,8,256]{2,1,0:T(8,128)S(1)}, u32[]{:S(2)}, u32[]{:S(2)}) collective-permute-start(f32[2,8,256]{2,1,0:T(8,128)S(1)} %get-tuple-element.36), channel_id=1, source_target_pairs={{8,16},{24,32},{40,48},{56,64},{72,80},{88,96},{104,112},{16,8},{3... | collective-permute-start | bytes 49160 | tf_op jit(solution)/shard_map/ppermute | solution.py:48

commit v5 on v4

--- a/solution.py
+++ b/solution.py
@@ -62,6 +62,14 @@
     return hi, mid, rest - mid
 
 
+def interleave(parts_u, parts_v):
+    return [part for both in zip(parts_u, parts_v) for part in both]
+
+
+def sum_parts(x):
+    return x[0:2] + x[2:4] + x[4:6]
+
+
 def contract_last(a, b):
     return lax.dot_general(a, b, (((1,), (1,)), ((), ())), preferred_element_type=f32)
 
@@ -79,7 +87,9 @@
 def tile_fields(forcing, strength, mask):
     cover = mask.astype(f32)
     spread = (iota((16, COLS), 1) // 8 == iota((16, COLS), 0)).astype(f32)
-    wide = jnp.dot(strength, spread, precision=lax.Precision.HIGHEST, preferred_element_type=f32)
+    parts = jnp.concatenate(split3(strength), axis=0).astype(bf16)
+    wide = jnp.dot(parts, spread.astype(bf16), preferred_element_type=f32)
+    wide = (wide[0:4] + wide[4:8]) + wide[8:12]
     fine = jnp.concatenate([jnp.broadcast_to(wide[i : i + 1], (8, COLS)) for i in range(ROWS // 8)], axis=0)
     return forcing[0], forcing[1], cover, visc_scale * fine * cover
 
@@ -149,14 +159,14 @@
 
 def forward_kernel(ext, pair, other, received, table, observed, sums, rates, window, table_out, vel, kept, hot, total, sems):
     b = lax.axis_index("gy")
-    slot_ids = iota((BUOYS, COLS), 0)
+    slot_ids = iota((COLS, COLS), 0)
     slots = jnp.concatenate([received[d, 8:12, :] for d in range(OWNERS)], axis=0).astype(jnp.int32)
     table_out[0] = table[0]
     table_out[1] = table[1]
     table_out[2] = slots
     for i in range(ROWS):
         at = slice(COLS * i, COLS * i + COLS)
-        hot[:, at] = (slot_ids == slots[i : i + 1, :]).astype(f32).astype(bf16)
+        hot[:, at] = (slot_ids == slots[i : i + 1, :] % COLS).astype(f32).astype(bf16)
     fields = []
     for f in range(4):
         above, below = above_below(pair, other, f)
@@ -169,24 +179,33 @@
     big = (0.625 * step_size) * visc
     small = (0.375 * step_size) * visc
     quarter = (0.25 * step_size) * visc
+    big_p, small_p, quarter_p = prev_col(big), prev_col(small), prev_col(quarter)
     u, v = tau_x, tau_y
-    nx = ny = s3 = None
+    nx = ny = s3 = ny_p = s3_p = None
     own = slice(HALO, HALO + ROWS)
     for step in range(SUBCYCLES - 1):
+        u_p, v_p = prev_col(u), prev_col(v)
         ex = next_row(u) - u
         ey = next_col(v) - v
         sh = (next_col(u) - u) + (next_row(v) - v)
+        ex_p = next_row(u_p) - u_p
+        ey_p = v - v_p
+        sh_p = (u - u_p) + (next_row(v_p) - v_p)
         rates[step, 0] = ex[own, :COLS]
         rates[step, 1] = ey[own, :COLS]
         rates[step, 2] = sh[own, :COLS]
         dx = big * ex + small * ey
         dy = small * ex + big * ey
         ds = quarter * sh
+        dy_p = small_p * ex_p + big_p * ey_p
+        ds_p = quarter_p * sh_p
         nx = dx if nx is None else relax * nx + dx
         ny = dy if ny is None else relax * ny + dy
         s3 = ds if s3 is None else relax * s3 + ds
-        fx = (nx - prev_row(nx)) + (s3 - prev_col(s3))
-        fy = (ny - prev_col(ny)) + (s3 - prev_row(s3))
+        ny_p = dy_p if ny_p is None else relax * ny_p + dy_p
+        s3_p = ds_p if s3_p is None else relax * s3_p + ds_p
+        fx = (nx - prev_row(nx)) + (s3 - s3_p)
+        fy = (ny - ny_p) + (s3 - prev_row(s3))
         u = damping * u + cover * fx + tau_x
         v = damping * v + cover * fy + tau_y
     vel[0] = u[own, :COLS]
@@ -203,15 +222,19 @@
         got_u = jnp.where(hit, jnp.take_along_axis(line_u, col, axis=1), got_u)
         got_v = jnp.where(hit, jnp.take_along_axis(line_v, col, axis=1), got_v)
     weight = table[1].astype(f32) * (1.0 / 16.0)
-    keep_parts(kept, split3(got_u * weight) + split3(got_v * weight))
-    blocks = []
+    keep_parts(kept, interleave(split3(got_u * weight), split3(got_v * weight)))
     for d in range(OWNERS):
-        left = jnp.concatenate([parts_of_row(kept, 4 * d + i) for i in range(4)], axis=1).astype(bf16)
+        left = []
+        for i in range(4 * d, 4 * d + 4):
+            block = parts_of_row(kept, i)
+            low = slots[i : i + 1, :] < COLS
+            left.append(jnp.concatenate([jnp.where(low, block, 0.0), jnp.where(low, 0.0, block)], axis=0))
+        left = jnp.concatenate(left, axis=1).astype(bf16)
         prod = contract_last(left, hot[:, 4 * COLS * d : 4 * COLS * d + 4 * COLS])
         mine = (b == d).astype(f32)
-        blocks.append(jnp.sum(prod[0:3], axis=0, keepdims=True) - mine * observed[0:1, :])
-        blocks.append(jnp.sum(prod[3:6], axis=0, keepdims=True) - mine * observed[1:2, :])
-    total[...] = jnp.concatenate(blocks, axis=0)
+        for h in range(2):
+            at = slice(COLS * h, COLS * h + COLS)
+            total[2 * d : 2 * d + 2, at] = sum_parts(prod[8 * h : 8 * h + 8]) - mine * observed[:, at]
     copies = [pltpu.make_async_copy(total, sums.at[d], sems.at[d]) for d in range(OWNERS)]
     for copy in copies:
         copy.start()
@@ -281,9 +304,7 @@
                         jnp.take_along_axis(tables[q][c][1], near, axis=1),
                     )
                 )
-        parts = []
-        for c in range(2):
-            parts += split3(jnp.concatenate(values[c], axis=0))
+        parts = interleave(*(split3(jnp.concatenate(values[c], axis=0)) for c in range(2)))
         if k == 1:
             for i in range(ROWS):
                 at = slice(COLS * i, COLS * i + COLS)
@@ -292,8 +313,7 @@
                     lhs[ROWS * p : ROWS * p + ROWS, at] = jnp.where(hit, part[i : i + 1, :], 0.0).astype(bf16)
             prod = contract_last(lhs[...], col_hot[...])
             for c in range(2):
-                at = 3 * ROWS * c
-                adj[c, :, 0:COLS] = prod[at : at + 32] + prod[at + 32 : at + 64] + prod[at + 64 : at + 96]
+                adj[c, :, 0:COLS] = sum(prod[ROWS * p : ROWS * p + ROWS] for p in (c, c + 2, c + 4))
         else:
             keep_parts(kept.at[k // 2], parts)
             group = row // SPAN
@@ -303,17 +323,14 @@
                     [jnp.where(group[i : i + 1, :] == g, block, 0.0) for g in range(ROWS // SPAN)], axis=0
                 ).astype(bf16)
             prod = contract_last(edge_lhs[...], (right_hot if k else left_hot)[...])
-            halo[k] = [
-                [jnp.sum(prod[at : at + 3], axis=0, keepdims=True) for at in (8 * g, 8 * g + 3)]
-                for g in range(ROWS // SPAN)
-            ]
+            halo[k] = [sum_parts(prod[8 * g : 8 * g + 8]) for g in range(ROWS // SPAN)]
     for c in range(2):
         for q in range(4):
             first_row = 8 * q % SPAN
             where = ((first_row % 16 + sub) * 8 + lane % 8) % COLS
             sides = []
             for k in (2, 0):
-                line = halo[k][8 * q // SPAN][c]
+                line = halo[k][8 * q // SPAN][c : c + 1]
                 line = line[:, 8 * (first_row - first_row % 16) :][:, :COLS]
                 if line.shape[1] < COLS:
                     line = jnp.concatenate([line, line], axis=1)
@@ -329,23 +346,31 @@
     visc = window[1]
     scaled = step_size * cover
     third = 0.25 * visc
+    visc_p, third_p = prev_col(visc), prev_col(third)
     states = []
     for c in range(2):
         above, below = above_below(pair, other, c)
         states.append(scaled * jnp.concatenate([above, adj[c], below], axis=0))
     w0, w1 = states
     own = slice(HALO, HALO + ROWS)
-    a = h = t = None
+    a = h = t = h_p = t_p = None
     grad = None
     for step in range(SUBCYCLES - 2, -1, -1):
+        w0_p, w1_p = prev_col(w0), prev_col(w1)
         ax = w0 - next_row(w0)
         ay = w1 - next_col(w1)
         at = (w0 - next_col(w0)) + (w1 - next_row(w1))
+        ax_p = w0_p - next_row(w0_p)
+        ay_p = w1_p - w1
+        at_p = (w0_p - w0) + (w1_p - next_row(w1_p))
         da = 0.625 * ax + 0.375 * ay
         dh = 0.375 * ax + 0.625 * ay
+        dh_p = 0.375 * ax_p + 0.625 * ay_p
         a = da if a is None else relax * a + da
         h = dh if h is None else relax * h + dh
         t = at if t is None else relax * t + at
+        h_p = dh_p if h_p is None else relax * h_p + dh_p
+        t_p = at_p if t_p is None else relax * t_p + at_p
         term = (
             a[own, :COLS] * rates[step, 0]
             + h[own, :COLS] * rates[step, 1]
@@ -354,14 +379,16 @@
         grad = term if grad is None else grad + term
         if step:
             ra, rh, rt = visc * a, visc * h, third * t
-            w0 = damping * w0 + scaled * ((prev_row(ra) - ra) + (prev_col(rt) - rt))
-            w1 = damping * w1 + scaled * ((prev_col(rh) - rh) + (prev_row(rt) - rt))
+            w0 = damping * w0 + scaled * ((prev_row(ra) - ra) + (third_p * t_p - rt))
+            w1 = damping * w1 + scaled * ((visc_p * h_p - rh) + (prev_row(rt) - rt))
     grad = visc_scale * cover[own, :COLS] * grad
     rows = jnp.concatenate(
         [jnp.sum(grad[8 * i : 8 * i + 8], axis=0, keepdims=True) for i in range(ROWS // 8)], axis=0
     )
     gather = (iota((COLS, 16), 0) // 8 == iota((COLS, 16), 1)).astype(f32)
-    out[...] = jnp.dot(rows, gather, precision=lax.Precision.HIGHEST, preferred_element_type=f32)
+    parts = jnp.concatenate(split3(rows), axis=0).astype(bf16)
+    sums = jnp.dot(parts, gather.astype(bf16), preferred_element_type=f32)
+    out[...] = sums[0:4] + sums[4:8] + sums[8:12]
     copy.wait()
 
 
@@ -423,7 +450,7 @@
         [
             near(2, ROWS, COLS),
             near(8 * ROWS, COLS),
-            near(BUOYS, entries, dtype=bf16),
+            near(COLS, entries, dtype=bf16),
             near(2 * OWNERS, BUOYS),
             pltpu.SemaphoreType.DMA((OWNERS,)),
         ],

time: 64.9 us -> 64.6 us (level)
  no operation moved by 1% of the time
where the time goes in v5:
time: 64.6 us; the launch traced here: 64.2 us
  blocking collectives  34.5 us (53%)
  starting transfers between devices  19.1 us (30%)
  Pallas kernels  6.87 us (11%)
  waiting for transfers between devices  2.37 us (4%)
  between operations  0.72 us (1%)
    all_to_all x1, blocking collectives, per_device(): received = lax.all_to_all(packed, 'gy', 0, 0, tiled=True)  17.1 us
    ppermute x2, starting transfers between devices, exchange_rows(): other = lax.ppermute(to_other, 'gx', swaps + [(j, i) for i, j in swaps])  10.5 us
    all_gather x1, blocking collectives, per_device(): gradient = jnp.sum(lax.all_gather(coarse, 'member'), axis=0)  10.4 us
    all_gather x2, blocking collectives, exchange_rows(): pair = lax.all_gather(to_pair, 'gx', axis_index_groups=groups)  7 us
    pallas_call x6, Pallas kernels, call(): pl.pallas_call(kernel, out_shape=tuple(outs), in_specs=[near] * len(args)...  6.87 us
    ppermute x2, starting transfers between devices, from_behind(): return lax.ppermute(x, axis, pairs)  5.28 us
    all_to_all x1, starting transfers between devices, per_device(): sums = lax.all_to_all(sums, 'gy', 0, 0, tiled=True)  3.38 us
  transfers between devices with their start and end apart: 5, of which 3 were waited for; matrix products, arithmetic and copies ran while one was open for 0% of the time, Pallas kernels for 1%

profile of v5, /device:TPU:7, one launch (start us, length us, event | category | flops | bytes accessed | tf_op | source)
XLA Modules:
  0.0 64.2 jit_solution(16431356481837918563)
XLA Ops:
  0.6 1.1 %shard_map.86 = (f32[8,12,128]{2,1,0:T(8,128)S(1)}, f32[4,32,128]{2,1,0:T(8,128)S(1)}, s32[2,32,128]{2,1,0:T(8,128)S(1)}, f32[2,256]{1,0:T(2,128)S(1)}) custom-call(f32[2,32,128]{2,1,0:T(8,128)} %bitcast.12, f32[4,16]{1,0:T(4,128)} %strength_in.1, s32[32,128]{1,0:T(8,128)} %mask_in.1, s32[32,128]{1,0:T(8,128)} %bitcast.13, s32[32,128]{1,0:T(8,128)} %bitcast.14, ...), custom_call_target="tpu_custom_call" | custom-call | tf_op jit(solution)/shard_map/pallas_call | solution.py:398
  1.7 17.1 %all_to_all.10.received = f32[8,12,128]{2,1,0:T(8,128)S(1)} all-to-all(f32[8,12,128]{2,1,0:T(8,128)S(1)} %get-tuple-element.22), channel_id=1, replica_groups=mesh['member'=4,'gx'=16,'gy'=8] {'gy'}, dimensions={0} | all-to-all | bytes 98304 | tf_op jit(solution)/shard_map/all_to_all | solution.py:433
  18.8 0.1 shard_map.87
  18.9 5.9 %collective-permute-start = (f32[4,8,256]{2,1,0:T(8,128)S(1)}, f32[4,8,256]{2,1,0:T(8,128)S(1)}, u32[]{:S(2)}, u32[]{:S(2)}) collective-permute-start(f32[4,8,256]{2,1,0:T(8,128)S(1)} %get-tuple-element.26), channel_id=1, source_target_pairs={{8,16},{24,32},{40,48},{56,64},{72,80},{88,96},{104,112},{16,8},{3... | collective-permute-start | bytes 98312 | tf_op jit(solution)/shard_map/ppermute | solution.py:48
  24.8 3.7 %all-gather = f32[8,8,256]{2,1,0:T(8,128)S(1)} all-gather(f32[4,8,256]{2,1,0:T(8,128)S(1)} %get-tuple-element.25), channel_id=2, replica_groups={{0,8},{16,24},{32,40},{48,56},{64,72},{80,88},{96,104},{112,120},{1,9},..., dimensions={0}, use_global_device_ids=true | all-gather | bytes 98304 | tf_op jit(solution)/shard_map/all_gather | solution.py:50
  28.6 0.0 collective-permute-done.other
  28.6 2.8 %shard_map.88 = (f32[8,16,256]{2,1,0:T(8,128)}, f32[7,3,32,128]{3,2,1,0:T(8,128)S(1)}, f32[2,48,256]{2,1,0:T(8,128)S(1)}, s32[3,32,128]{2,1,0:T(8,128)S(1)}) custom-call(f32[4,32,256]{2,1,0:T(8,128)S(1)} %get-tuple-element.24.ext, f32[2,4,8,256]{3,2,1,0:T(8,128)S(1)} %bitcast.9, f32[4,8,256]{2,1,0:T(8,128)S(1)} %collective-permute-done.other, ...), custom_call_target="tpu_custom_call" | custom-call | tf_op jit(solution)/shard_map/pallas_call | solution.py:398
  31.4 3.4 %all-to-all-start.1 = ((f32[8,16,256]{2,1,0:T(8,128)}), f32[8,16,256]{2,1,0:T(8,128)S(1)}, u32[]{:S(2)}, u32[]{:S(2)}) async-start(f32[8,16,256]{2,1,0:T(8,128)} %get-tuple-element.29), calls=%async_computation.1 | async-start | bytes 262144 | tf_op jit(solution)/shard_map/all_to_all | solution.py:458
  34.8 1.3 %collective-permute-start.2 = (s32[3,32,128]{2,1,0:T(8,128)S(1)}, s32[3,32,128]{2,1,0:T(8,128)S(1)}, u32[]{:S(2)}, u32[]{:S(2)}) collective-permute-start(s32[3,32,128]{2,1,0:T(8,128)S(1)} %get-tuple-element.30.own_table), channel_id=1, source_target_pairs={{1,0},{2,1},{3,2},{4,3},{5,4},{6,5},{7,6},{9,8},{10,9},{11,10},{12... | collective-permute-start | bytes 147464 | tf_op jit(solution)/shard_map/ppermute | solution.py:29
  36.1 4.0 %collective-permute-start.1 = (s32[3,32,128]{2,1,0:T(8,128)S(1)}, s32[3,32,128]{2,1,0:T(8,128)S(1)}, u32[]{:S(2)}, u32[]{:S(2)}) collective-permute-start(s32[3,32,128]{2,1,0:T(8,128)S(1)} %get-tuple-element.30.own_table), channel_id=1, source_target_pairs={{0,1},{1,2},{2,3},{3,4},{4,5},{5,6},{6,7},{8,9},{9,10},{10,11},{11... | collective-permute-start | bytes 147464 | tf_op jit(solution)/shard_map/ppermute | solution.py:29
  40.1 0.0 collective-permute-done.2.right_table
  40.1 1.1 %collective-permute-done.1.left_table = s32[3,32,128]{2,1,0:T(8,128)S(1)} collective-permute-done((s32[3,32,128]{2,1,0:T(8,128)S(1)}, s32[3,32,128]{2,1,0:T(8,128)S(1)}, u32[]{:S(2)}, u32[]{:S(2)}) %collective-permute-start.1) | collective-permute-done | bytes 49184 | tf_op jit(solution)/shard_map/ppermute | solution.py:29
  41.2 0.6 shard_map.89
  41.8 0.9 %all-to-all-done.1.sums = f32[8,16,256]{2,1,0:T(8,128)S(1)} async-done(((f32[8,16,256]{2,1,0:T(8,128)}), f32[8,16,256]{2,1,0:T(8,128)S(1)}, u32[]{:S(2)}, u32[]{:S(2)}) %all-to-all-start.1) | async-done | bytes 131104 | tf_op jit(solution)/shard_map/all_to_all | solution.py:458
  42.7 1.1 %shard_map.90 = (f32[2,256]{1,0:T(2,128)S(1)}, f32[2,32,256]{2,1,0:T(8,128)S(1)}, f32[2,8,256]{2,1,0:T(8,128)S(1)}, f32[2,8,256]{2,1,0:T(8,128)S(1)}) custom-call(f32[8,16,256]{2,1,0:T(8,128)S(1)} %all-to-all-done.1.sums, s32[3,32,128]{2,1,0:T(8,128)S(1)} %collective-permute-done.1.left_table, s32[3,32,128]{2,1,0:T(8,128)S(1)} %get-tuple-element.30.own_table, ...), custom_call_target="tpu_custom_call" | custom-call | tf_op jit(solution)/shard_map/pallas_call | solution.py:398
  43.9 4.5 %collective-permute-start.3 = (f32[2,8,256]{2,1,0:T(8,128)S(1)}, f32[2,8,256]{2,1,0:T(8,128)S(1)}, u32[]{:S(2)}, u32[]{:S(2)}) collective-permute-start(f32[2,8,256]{2,1,0:T(8,128)S(1)} %get-tuple-element.36), channel_id=1, source_target_pairs={{8,16},{24,32},{40,48},{56,64},{72,80},{88,96},{104,112},{16,8},{3... | collective-permute-start | bytes 49160 | tf_op jit(solution)/shard_map/ppermute | solution.py:48
  48.4 3.3 %all-gather.1 = f32[4,8,256]{2,1,0:T(8,128)S(1)} all-gather(f32[2,8,256]{2,1,0:T(8,128)S(1)} %get-tuple-element.35), channel_id=3, replica_groups={{0,8},{16,24},{32,40},{48,56},{64,72},{80,88},{96,104},{112,120},{1,9},..., dimensions={0}, use_global_device_ids=true | all-gather | bytes 49152 | tf_op jit(solution)/shard_map/all_gather | solution.py:50
  51.7 0.3 collective-permute-done.3.other
  52.0 1.2 %shard_map.91 = (f32[4,16]{1,0:T(4,128)S(1)}, f32[2,256]{1,0:T(2,128)}) custom-call(f32[2,32,256]{2,1,0:T(8,128)S(1)} %get-tuple-element.34.adj, f32[2,2,8,256]{3,2,1,0:T(8,128)S(1)} %bitcast.10, f32[2,8,256]{2,1,0:T(8,128)S(1)} %collective-permute-done.3.other, f32[2,48,256]{2,1,0:T(8,128)S(1)} %get-tuple-element.37.window, ...), custom_call_target="tpu_custom_call" | custom-call | tf_op jit(solution)/shard_map/pallas_call | solution.py:398
  53.2 10.4 %all-gather.3 = f32[4,4,16]{2,1,0:T(4,128)S(1)} all-gather(f32[1,4,16]{2,1,0:T(4,128)S(1)} %bitcast.11), channel_id=4, replica_groups=mesh['member'=4,'gx'=16,'gy'=8] {'member'}, dimensions={0}, use_global_device_ids=true | all-gather | bytes 1280 | tf_op jit(solution)/shard_map/all_gather | solution.py:492
  63.6 0.6 reduce_sum.9
Async XLA Ops:
  18.9 9.7 %collective-permute-start = (f32[4,8,256]{2,1,0:T(8,128)S(1)}, f32[4,8,256]{2,1,0:T(8,128)S(1)}, u32[]{:S(2)}, u32[]{:S(2)}) collective-permute-start(f32[4,8,256]{2,1,0:T(8,128)S(1)} %get-tuple-element.26), channel_id=1, source_target_pairs={{8,16},{24,32},{40,48},{56,64},{72,80},{88,96},{104,112},{16,8},{3... | collective-permute-start | bytes 98312 | tf_op jit(solution)/shard_map/ppermute | solution.py:48
  31.4 11.3 %all-to-all-start.1 = ((f32[8,16,256]{2,1,0:T(8,128)}), f32[8,16,256]{2,1,0:T(8,128)S(1)}, u32[]{:S(2)}, u32[]{:S(2)}) async-start(f32[8,16,256]{2,1,0:T(8,128)} %get-tuple-element.29), calls=%async_computation.1 | async-start | bytes 262144 | tf_op jit(solution)/shard_map/all_to_all | solution.py:458
  34.8 5.3 %collective-permute-start.2 = (s32[3,32,128]{2,1,0:T(8,128)S(1)}, s32[3,32,128]{2,1,0:T(8,128)S(1)}, u32[]{:S(2)}, u32[]{:S(2)}) collective-permute-start(s32[3,32,128]{2,1,0:T(8,128)S(1)} %get-tuple-element.30.own_table), channel_id=1, source_target_pairs={{1,0},{2,1},{3,2},{4,3},{5,4},{6,5},{7,6},{9,8},{10,9},{11,10},{12... | collective-permute-start | bytes 147464 | tf_op jit(solution)/shard_map/ppermute | solution.py:29
  36.1 5.2 %collective-permute-start.1 = (s32[3,32,128]{2,1,0:T(8,128)S(1)}, s32[3,32,128]{2,1,0:T(8,128)S(1)}, u32[]{:S(2)}, u32[]{:S(2)}) collective-permute-start(s32[3,32,128]{2,1,0:T(8,128)S(1)} %get-tuple-element.30.own_table), channel_id=1, source_target_pairs={{0,1},{1,2},{2,3},{3,4},{4,5},{5,6},{6,7},{8,9},{9,10},{10,11},{11... | collective-permute-start | bytes 147464 | tf_op jit(solution)/shard_map/ppermute | solution.py:29
  43.9 8.1 %collective-permute-start.3 = (f32[2,8,256]{2,1,0:T(8,128)S(1)}, f32[2,8,256]{2,1,0:T(8,128)S(1)}, u32[]{:S(2)}, u32[]{:S(2)}) collective-permute-start(f32[2,8,256]{2,1,0:T(8,128)S(1)} %get-tuple-element.36), channel_id=1, source_target_pairs={{8,16},{24,32},{40,48},{56,64},{72,80},{88,96},{104,112},{16,8},{3... | collective-permute-start | bytes 49160 | tf_op jit(solution)/shard_map/ppermute | solution.py:48

commit v6 on v5

--- a/solution.py
+++ b/solution.py
@@ -122,15 +122,18 @@
             right = jnp.where(here, pltpu.roll(piece, at + 8, 1), right)
     slots = recv[...].astype(f32)
     for d in range(OWNERS):
-        out[d, 0:8, :] = jnp.where(d < b, left, right)
-        out[d, 8:12, :] = slots[4 * d : 4 * d + 4]
+        strip = jnp.where(d < b, left, right)
+        out[d, 0] = strip[0:4]
+        out[d, 1] = strip[4:8]
+        out[d, 2] = slots[4 * d : 4 * d + 4]
 
 
 def widen_kernel(received, own, ext, to_pair, to_other):
     b = lax.axis_index("gy")
     lane = iota((8, COLS), 1)
-    from_left = received[jnp.maximum(b - 1, 0), 0:8, :] * (b > 0).astype(f32)
-    from_right = received[jnp.minimum(b + 1, OWNERS - 1), 0:8, :] * (b < OWNERS - 1).astype(f32)
+    left, right = jnp.maximum(b - 1, 0), jnp.minimum(b + 1, OWNERS - 1)
+    from_left = jnp.concatenate([received[left, n] for n in range(2)], axis=0) * (b > 0).astype(f32)
+    from_right = jnp.concatenate([received[right, n] for n in range(2)], axis=0) * (b < OWNERS - 1).astype(f32)
     for f in range(4):
         ext[f, :, 0:COLS] = own[f]
         for g in range(4):
@@ -160,7 +163,7 @@
 def forward_kernel(ext, pair, other, received, table, observed, sums, rates, window, table_out, vel, kept, hot, total, sems):
     b = lax.axis_index("gy")
     slot_ids = iota((COLS, COLS), 0)
-    slots = jnp.concatenate([received[d, 8:12, :] for d in range(OWNERS)], axis=0).astype(jnp.int32)
+    slots = jnp.concatenate([received[d, 2] for d in range(OWNERS)], axis=0).astype(jnp.int32)
     table_out[0] = table[0]
     table_out[1] = table[1]
     table_out[2] = slots
@@ -179,7 +182,8 @@
     big = (0.625 * step_size) * visc
     small = (0.375 * step_size) * visc
     quarter = (0.25 * step_size) * visc
-    big_p, small_p, quarter_p = prev_col(big), prev_col(small), prev_col(quarter)
+    visc_p = prev_col(visc)
+    big_p, small_p, quarter_p = ((c * step_size) * visc_p for c in (0.625, 0.375, 0.25))
     u, v = tau_x, tau_y
     nx = ny = s3 = ny_p = s3_p = None
     own = slice(HALO, HALO + ROWS)
@@ -346,7 +350,8 @@
     visc = window[1]
     scaled = step_size * cover
     third = 0.25 * visc
-    visc_p, third_p = prev_col(visc), prev_col(third)
+    visc_p = prev_col(visc)
+    third_p = 0.25 * visc_p
     states = []
     for c in range(2):
         above, below = above_below(pair, other, c)
@@ -419,7 +424,7 @@
     entries = ROWS * COLS
     packed, own, table, observed = call(
         pack_kernel,
-        [near(OWNERS, 12, COLS), near(4, ROWS, COLS), near(2, ROWS, COLS, dtype=jnp.int32), near(2, BUOYS)],
+        [near(OWNERS, 3, 4, COLS), near(4, ROWS, COLS), near(2, ROWS, COLS, dtype=jnp.int32), near(2, BUOYS)],
         (),
         (forcing, strength, mask, recv, cells, codes, observed),
         [

time: 64.6 us -> 64.4 us (level)
  no operation moved by 1% of the time
where the time goes in v6:
time: 64.4 us; the launch traced here: 64 us
  blocking collectives  34.3 us (53%)
  starting transfers between devices  19.1 us (30%)
  Pallas kernels  6.87 us (11%)
  waiting for transfers between devices  2.37 us (4%)
  between operations  0.72 us (1%)
    all_to_all x1, blocking collectives, per_device(): received = lax.all_to_all(packed, 'gy', 0, 0, tiled=True)  16.9 us
    ppermute x2, starting transfers between devices, exchange_rows(): other = lax.ppermute(to_other, 'gx', swaps + [(j, i) for i, j in swaps])  10.5 us
    all_gather x1, blocking collectives, per_device(): gradient = jnp.sum(lax.all_gather(coarse, 'member'), axis=0)  10.4 us
    all_gather x2, blocking collectives, exchange_rows(): pair = lax.all_gather(to_pair, 'gx', axis_index_groups=groups)  7 us
    pallas_call x6, Pallas kernels, call(): pl.pallas_call(kernel, out_shape=tuple(outs), in_specs=[near] * len(args)...  6.87 us
    ppermute x2, starting transfers between devices, from_behind(): return lax.ppermute(x, axis, pairs)  5.28 us
    all_to_all x1, starting transfers between devices, per_device(): sums = lax.all_to_all(sums, 'gy', 0, 0, tiled=True)  3.38 us
  transfers between devices with their start and end apart: 5, of which 3 were waited for; matrix products, arithmetic and copies ran while one was open for 0% of the time, Pallas kernels for 1%

profile of v6, /device:TPU:7, one launch (start us, length us, event | category | flops | bytes accessed | tf_op | source)
XLA Modules:
  0.0 64.0 jit_solution(2713580362115881861)
XLA Ops:
  0.6 1.1 %shard_map.86 = (f32[8,3,4,128]{3,2,1,0:T(4,128)S(1)}, f32[4,32,128]{2,1,0:T(8,128)S(1)}, s32[2,32,128]{2,1,0:T(8,128)S(1)}, f32[2,256]{1,0:T(2,128)S(1)}) custom-call(f32[2,32,128]{2,1,0:T(8,128)} %bitcast.12, f32[4,16]{1,0:T(4,128)} %strength_in.1, s32[32,128]{1,0:T(8,128)} %mask_in.1, s32[32,128]{1,0:T(8,128)} %bitcast.13, s32[32,128]{1,0:T(8,128)} %bitcast.14, ...), custom_call_target="tpu_custom_call" | custom-call | tf_op jit(solution)/shard_map/pallas_call | solution.py:403
  1.7 16.9 %all_to_all.10.received = f32[8,3,4,128]{3,2,1,0:T(4,128)S(1)} all-to-all(f32[8,3,4,128]{3,2,1,0:T(4,128)S(1)} %get-tuple-element.22), channel_id=1, replica_groups=mesh['member'=4,'gx'=16,'gy'=8] {'gy'}, dimensions={0} | all-to-all | bytes 98304 | tf_op jit(solution)/shard_map/all_to_all | solution.py:438
  18.6 0.1 shard_map.87
  18.7 5.9 %collective-permute-start = (f32[4,8,256]{2,1,0:T(8,128)S(1)}, f32[4,8,256]{2,1,0:T(8,128)S(1)}, u32[]{:S(2)}, u32[]{:S(2)}) collective-permute-start(f32[4,8,256]{2,1,0:T(8,128)S(1)} %get-tuple-element.26), channel_id=1, source_target_pairs={{8,16},{24,32},{40,48},{56,64},{72,80},{88,96},{104,112},{16,8},{3... | collective-permute-start | bytes 98312 | tf_op jit(solution)/shard_map/ppermute | solution.py:48
  24.6 3.7 %all-gather = f32[8,8,256]{2,1,0:T(8,128)S(1)} all-gather(f32[4,8,256]{2,1,0:T(8,128)S(1)} %get-tuple-element.25), channel_id=2, replica_groups={{0,8},{16,24},{32,40},{48,56},{64,72},{80,88},{96,104},{112,120},{1,9},..., dimensions={0}, use_global_device_ids=true | all-gather | bytes 98304 | tf_op jit(solution)/shard_map/all_gather | solution.py:50
  28.4 0.0 collective-permute-done.other
  28.4 2.8 %shard_map.88 = (f32[8,16,256]{2,1,0:T(8,128)}, f32[7,3,32,128]{3,2,1,0:T(8,128)S(1)}, f32[2,48,256]{2,1,0:T(8,128)S(1)}, s32[3,32,128]{2,1,0:T(8,128)S(1)}) custom-call(f32[4,32,256]{2,1,0:T(8,128)S(1)} %get-tuple-element.24.ext, f32[2,4,8,256]{3,2,1,0:T(8,128)S(1)} %bitcast.9, f32[4,8,256]{2,1,0:T(8,128)S(1)} %collective-permute-done.other, ...), custom_call_target="tpu_custom_call" | custom-call | tf_op jit(solution)/shard_map/pallas_call | solution.py:403
  31.2 3.4 %all-to-all-start.1 = ((f32[8,16,256]{2,1,0:T(8,128)}), f32[8,16,256]{2,1,0:T(8,128)S(1)}, u32[]{:S(2)}, u32[]{:S(2)}) async-start(f32[8,16,256]{2,1,0:T(8,128)} %get-tuple-element.29), calls=%async_computation.1 | async-start | bytes 262144 | tf_op jit(solution)/shard_map/all_to_all | solution.py:463
  34.6 1.3 %collective-permute-start.2 = (s32[3,32,128]{2,1,0:T(8,128)S(1)}, s32[3,32,128]{2,1,0:T(8,128)S(1)}, u32[]{:S(2)}, u32[]{:S(2)}) collective-permute-start(s32[3,32,128]{2,1,0:T(8,128)S(1)} %get-tuple-element.30.own_table), channel_id=1, source_target_pairs={{1,0},{2,1},{3,2},{4,3},{5,4},{6,5},{7,6},{9,8},{10,9},{11,10},{12... | collective-permute-start | bytes 147464 | tf_op jit(solution)/shard_map/ppermute | solution.py:29
  35.9 4.0 %collective-permute-start.1 = (s32[3,32,128]{2,1,0:T(8,128)S(1)}, s32[3,32,128]{2,1,0:T(8,128)S(1)}, u32[]{:S(2)}, u32[]{:S(2)}) collective-permute-start(s32[3,32,128]{2,1,0:T(8,128)S(1)} %get-tuple-element.30.own_table), channel_id=1, source_target_pairs={{0,1},{1,2},{2,3},{3,4},{4,5},{5,6},{6,7},{8,9},{9,10},{10,11},{11... | collective-permute-start | bytes 147464 | tf_op jit(solution)/shard_map/ppermute | solution.py:29
  39.9 0.0 collective-permute-done.2.right_table
  39.9 1.1 %collective-permute-done.1.left_table = s32[3,32,128]{2,1,0:T(8,128)S(1)} collective-permute-done((s32[3,32,128]{2,1,0:T(8,128)S(1)}, s32[3,32,128]{2,1,0:T(8,128)S(1)}, u32[]{:S(2)}, u32[]{:S(2)}) %collective-permute-start.1) | collective-permute-done | bytes 49184 | tf_op jit(solution)/shard_map/ppermute | solution.py:29
  41.0 0.6 shard_map.89
  41.6 0.9 %all-to-all-done.1.sums = f32[8,16,256]{2,1,0:T(8,128)S(1)} async-done(((f32[8,16,256]{2,1,0:T(8,128)}), f32[8,16,256]{2,1,0:T(8,128)S(1)}, u32[]{:S(2)}, u32[]{:S(2)}) %all-to-all-start.1) | async-done | bytes 131104 | tf_op jit(solution)/shard_map/all_to_all | solution.py:463
  42.5 1.1 %shard_map.90 = (f32[2,256]{1,0:T(2,128)S(1)}, f32[2,32,256]{2,1,0:T(8,128)S(1)}, f32[2,8,256]{2,1,0:T(8,128)S(1)}, f32[2,8,256]{2,1,0:T(8,128)S(1)}) custom-call(f32[8,16,256]{2,1,0:T(8,128)S(1)} %all-to-all-done.1.sums, s32[3,32,128]{2,1,0:T(8,128)S(1)} %collective-permute-done.1.left_table, s32[3,32,128]{2,1,0:T(8,128)S(1)} %get-tuple-element.30.own_table, ...), custom_call_target="tpu_custom_call" | custom-call | tf_op jit(solution)/shard_map/pallas_call | solution.py:403
  43.7 4.5 %collective-permute-start.3 = (f32[2,8,256]{2,1,0:T(8,128)S(1)}, f32[2,8,256]{2,1,0:T(8,128)S(1)}, u32[]{:S(2)}, u32[]{:S(2)}) collective-permute-start(f32[2,8,256]{2,1,0:T(8,128)S(1)} %get-tuple-element.36), channel_id=1, source_target_pairs={{8,16},{24,32},{40,48},{56,64},{72,80},{88,96},{104,112},{16,8},{3... | collective-permute-start | bytes 49160 | tf_op jit(solution)/shard_map/ppermute | solution.py:48
  48.2 3.3 %all-gather.1 = f32[4,8,256]{2,1,0:T(8,128)S(1)} all-gather(f32[2,8,256]{2,1,0:T(8,128)S(1)} %get-tuple-element.35), channel_id=3, replica_groups={{0,8},{16,24},{32,40},{48,56},{64,72},{80,88},{96,104},{112,120},{1,9},..., dimensions={0}, use_global_device_ids=true | all-gather | bytes 49152 | tf_op jit(solution)/shard_map/all_gather | solution.py:50
  51.5 0.3 collective-permute-done.3.other
  51.8 1.2 %shard_map.91 = (f32[4,16]{1,0:T(4,128)S(1)}, f32[2,256]{1,0:T(2,128)}) custom-call(f32[2,32,256]{2,1,0:T(8,128)S(1)} %get-tuple-element.34.adj, f32[2,2,8,256]{3,2,1,0:T(8,128)S(1)} %bitcast.10, f32[2,8,256]{2,1,0:T(8,128)S(1)} %collective-permute-done.3.other, f32[2,48,256]{2,1,0:T(8,128)S(1)} %get-tuple-element.37.window, ...), custom_call_target="tpu_custom_call" | custom-call | tf_op jit(solution)/shard_map/pallas_call | solution.py:403
  53.0 10.4 %all-gather.3 = f32[4,4,16]{2,1,0:T(4,128)S(1)} all-gather(f32[1,4,16]{2,1,0:T(4,128)S(1)} %bitcast.11), channel_id=4, replica_groups=mesh['member'=4,'gx'=16,'gy'=8] {'member'}, dimensions={0}, use_global_device_ids=true | all-gather | bytes 1280 | tf_op jit(solution)/shard_map/all_gather | solution.py:497
  63.4 0.6 reduce_sum.9
Async XLA Ops:
  18.7 9.7 %collective-permute-start = (f32[4,8,256]{2,1,0:T(8,128)S(1)}, f32[4,8,256]{2,1,0:T(8,128)S(1)}, u32[]{:S(2)}, u32[]{:S(2)}) collective-permute-start(f32[4,8,256]{2,1,0:T(8,128)S(1)} %get-tuple-element.26), channel_id=1, source_target_pairs={{8,16},{24,32},{40,48},{56,64},{72,80},{88,96},{104,112},{16,8},{3... | collective-permute-start | bytes 98312 | tf_op jit(solution)/shard_map/ppermute | solution.py:48
  31.2 11.3 %all-to-all-start.1 = ((f32[8,16,256]{2,1,0:T(8,128)}), f32[8,16,256]{2,1,0:T(8,128)S(1)}, u32[]{:S(2)}, u32[]{:S(2)}) async-start(f32[8,16,256]{2,1,0:T(8,128)} %get-tuple-element.29), calls=%async_computation.1 | async-start | bytes 262144 | tf_op jit(solution)/shard_map/all_to_all | solution.py:463
  34.6 5.3 %collective-permute-start.2 = (s32[3,32,128]{2,1,0:T(8,128)S(1)}, s32[3,32,128]{2,1,0:T(8,128)S(1)}, u32[]{:S(2)}, u32[]{:S(2)}) collective-permute-start(s32[3,32,128]{2,1,0:T(8,128)S(1)} %get-tuple-element.30.own_table), channel_id=1, source_target_pairs={{1,0},{2,1},{3,2},{4,3},{5,4},{6,5},{7,6},{9,8},{10,9},{11,10},{12... | collective-permute-start | bytes 147464 | tf_op jit(solution)/shard_map/ppermute | solution.py:29
  35.9 5.2 %collective-permute-start.1 = (s32[3,32,128]{2,1,0:T(8,128)S(1)}, s32[3,32,128]{2,1,0:T(8,128)S(1)}, u32[]{:S(2)}, u32[]{:S(2)}) collective-permute-start(s32[3,32,128]{2,1,0:T(8,128)S(1)} %get-tuple-element.30.own_table), channel_id=1, source_target_pairs={{0,1},{1,2},{2,3},{3,4},{4,5},{5,6},{6,7},{8,9},{9,10},{10,11},{11... | collective-permute-start | bytes 147464 | tf_op jit(solution)/shard_map/ppermute | solution.py:29
  43.7 8.1 %collective-permute-start.3 = (f32[2,8,256]{2,1,0:T(8,128)S(1)}, f32[2,8,256]{2,1,0:T(8,128)S(1)}, u32[]{:S(2)}, u32[]{:S(2)}) collective-permute-start(f32[2,8,256]{2,1,0:T(8,128)S(1)} %get-tuple-element.36), channel_id=1, source_target_pairs={{8,16},{24,32},{40,48},{56,64},{72,80},{88,96},{104,112},{16,8},{3... | collective-permute-start | bytes 49160 | tf_op jit(solution)/shard_map/ppermute | solution.py:48

commit v7 on v6

--- a/solution.py
+++ b/solution.py
@@ -86,10 +86,10 @@
 
 def tile_fields(forcing, strength, mask):
     cover = mask.astype(f32)
-    spread = (iota((16, COLS), 1) // 8 == iota((16, COLS), 0)).astype(f32)
-    parts = jnp.concatenate(split3(strength), axis=0).astype(bf16)
-    wide = jnp.dot(parts, spread.astype(bf16), preferred_element_type=f32)
-    wide = (wide[0:4] + wide[4:8]) + wide[8:12]
+    cells_y = COLS // 8
+    padded = jnp.concatenate([strength, jnp.zeros((ROWS // 8, COLS - cells_y), f32)], axis=1)
+    padded = jnp.concatenate([padded, padded], axis=0)
+    wide = jnp.take_along_axis(padded, iota((8, COLS), 1) // 8, axis=1)
     fine = jnp.concatenate([jnp.broadcast_to(wide[i : i + 1], (8, COLS)) for i in range(ROWS // 8)], axis=0)
     return forcing[0], forcing[1], cover, visc_scale * fine * cover
 
@@ -105,7 +105,7 @@
     copies = [pltpu.make_async_copy(a, t, sems.at[i]) for i, (a, t) in enumerate(zip(sources, targets))]
     for copy in copies:
         copy.start()
-    for copy in copies:
+    for copy in copies[:3]:
         copy.wait()
     fields = tile_fields(forcing[...], strength[...], mask[...])
     for f in range(4):
@@ -120,6 +120,8 @@
             here = (lane >= at) & (lane < at + 8)
             left = jnp.where(here, pltpu.roll(piece, at, 1) if at else piece, left)
             right = jnp.where(here, pltpu.roll(piece, at + 8, 1), right)
+    for copy in copies[3:]:
+        copy.wait()
     slots = recv[...].astype(f32)
     for d in range(OWNERS):
         strip = jnp.where(d < b, left, right)

time: 64.4 us -> 64.3 us (level)
  no operation moved by 1% of the time
where the time goes in v7:
time: 64.3 us; the launch traced here: 63.9 us
  blocking collectives  34.3 us (53%)
  starting transfers between devices  19.1 us (30%)
  Pallas kernels  6.8 us (11%)
  waiting for transfers between devices  2.37 us (4%)
  between operations  0.72 us (1%)
    all_to_all x1, blocking collectives, per_device(): received = lax.all_to_all(packed, 'gy', 0, 0, tiled=True)  16.9 us
    ppermute x2, starting transfers between devices, exchange_rows(): other = lax.ppermute(to_other, 'gx', swaps + [(j, i) for i, j in swaps])  10.5 us
    all_gather x1, blocking collectives, per_device(): gradient = jnp.sum(lax.all_gather(coarse, 'member'), axis=0)  10.4 us
    all_gather x2, blocking collectives, exchange_rows(): pair = lax.all_gather(to_pair, 'gx', axis_index_groups=groups)  7 us
    pallas_call x6, Pallas kernels, call(): pl.pallas_call(kernel, out_shape=tuple(outs), in_specs=[near] * len(args)...  6.8 us
    ppermute x2, starting transfers between devices, from_behind(): return lax.ppermute(x, axis, pairs)  5.28 us
    all_to_all x1, starting transfers between devices, per_device(): sums = lax.all_to_all(sums, 'gy', 0, 0, tiled=True)  3.38 us
  transfers between devices with their start and end apart: 5, of which 3 were waited for; matrix products, arithmetic and copies ran while one was open for 0% of the time, Pallas kernels for 1%

profile of v7, /device:TPU:7, one launch (start us, length us, event | category | flops | bytes accessed | tf_op | source)
XLA Modules:
  0.0 63.9 jit_solution(12743917058923058912)
XLA Ops:
  0.6 1.0 %shard_map.86 = (f32[8,3,4,128]{3,2,1,0:T(4,128)S(1)}, f32[4,32,128]{2,1,0:T(8,128)S(1)}, s32[2,32,128]{2,1,0:T(8,128)S(1)}, f32[2,256]{1,0:T(2,128)S(1)}) custom-call(f32[2,32,128]{2,1,0:T(8,128)} %bitcast.12, f32[4,16]{1,0:T(4,128)} %strength_in.1, s32[32,128]{1,0:T(8,128)} %mask_in.1, s32[32,128]{1,0:T(8,128)} %bitcast.13, s32[32,128]{1,0:T(8,128)} %bitcast.14, ...), custom_call_target="tpu_custom_call" | custom-call | tf_op jit(solution)/shard_map/pallas_call | solution.py:405
  1.6 16.9 %all_to_all.10.received = f32[8,3,4,128]{3,2,1,0:T(4,128)S(1)} all-to-all(f32[8,3,4,128]{3,2,1,0:T(4,128)S(1)} %get-tuple-element.22), channel_id=1, replica_groups=mesh['member'=4,'gx'=16,'gy'=8] {'gy'}, dimensions={0} | all-to-all | bytes 98304 | tf_op jit(solution)/shard_map/all_to_all | solution.py:440
  18.5 0.1 shard_map.87
  18.6 5.9 %collective-permute-start = (f32[4,8,256]{2,1,0:T(8,128)S(1)}, f32[4,8,256]{2,1,0:T(8,128)S(1)}, u32[]{:S(2)}, u32[]{:S(2)}) collective-permute-start(f32[4,8,256]{2,1,0:T(8,128)S(1)} %get-tuple-element.26), channel_id=1, source_target_pairs={{8,16},{24,32},{40,48},{56,64},{72,80},{88,96},{104,112},{16,8},{3... | collective-permute-start | bytes 98312 | tf_op jit(solution)/shard_map/ppermute | solution.py:48
  24.6 3.7 %all-gather = f32[8,8,256]{2,1,0:T(8,128)S(1)} all-gather(f32[4,8,256]{2,1,0:T(8,128)S(1)} %get-tuple-element.25), channel_id=2, replica_groups={{0,8},{16,24},{32,40},{48,56},{64,72},{80,88},{96,104},{112,120},{1,9},..., dimensions={0}, use_global_device_ids=true | all-gather | bytes 98304 | tf_op jit(solution)/shard_map/all_gather | solution.py:50
  28.3 0.0 collective-permute-done.other
  28.3 2.8 %shard_map.88 = (f32[8,16,256]{2,1,0:T(8,128)}, f32[7,3,32,128]{3,2,1,0:T(8,128)S(1)}, f32[2,48,256]{2,1,0:T(8,128)S(1)}, s32[3,32,128]{2,1,0:T(8,128)S(1)}) custom-call(f32[4,32,256]{2,1,0:T(8,128)S(1)} %get-tuple-element.24.ext, f32[2,4,8,256]{3,2,1,0:T(8,128)S(1)} %bitcast.9, f32[4,8,256]{2,1,0:T(8,128)S(1)} %collective-permute-done.other, ...), custom_call_target="tpu_custom_call" | custom-call | tf_op jit(solution)/shard_map/pallas_call | solution.py:405
  31.1 3.4 %all-to-all-start.1 = ((f32[8,16,256]{2,1,0:T(8,128)}), f32[8,16,256]{2,1,0:T(8,128)S(1)}, u32[]{:S(2)}, u32[]{:S(2)}) async-start(f32[8,16,256]{2,1,0:T(8,128)} %get-tuple-element.29), calls=%async_computation.1 | async-start | bytes 262144 | tf_op jit(solution)/shard_map/all_to_all | solution.py:465
  34.5 1.3 %collective-permute-start.2 = (s32[3,32,128]{2,1,0:T(8,128)S(1)}, s32[3,32,128]{2,1,0:T(8,128)S(1)}, u32[]{:S(2)}, u32[]{:S(2)}) collective-permute-start(s32[3,32,128]{2,1,0:T(8,128)S(1)} %get-tuple-element.30.own_table), channel_id=1, source_target_pairs={{1,0},{2,1},{3,2},{4,3},{5,4},{6,5},{7,6},{9,8},{10,9},{11,10},{12... | collective-permute-start | bytes 147464 | tf_op jit(solution)/shard_map/ppermute | solution.py:29
  35.8 4.0 %collective-permute-start.1 = (s32[3,32,128]{2,1,0:T(8,128)S(1)}, s32[3,32,128]{2,1,0:T(8,128)S(1)}, u32[]{:S(2)}, u32[]{:S(2)}) collective-permute-start(s32[3,32,128]{2,1,0:T(8,128)S(1)} %get-tuple-element.30.own_table), channel_id=1, source_target_pairs={{0,1},{1,2},{2,3},{3,4},{4,5},{5,6},{6,7},{8,9},{9,10},{10,11},{11... | collective-permute-start | bytes 147464 | tf_op jit(solution)/shard_map/ppermute | solution.py:29
  39.8 0.0 collective-permute-done.2.right_table
  39.8 1.1 %collective-permute-done.1.left_table = s32[3,32,128]{2,1,0:T(8,128)S(1)} collective-permute-done((s32[3,32,128]{2,1,0:T(8,128)S(1)}, s32[3,32,128]{2,1,0:T(8,128)S(1)}, u32[]{:S(2)}, u32[]{:S(2)}) %collective-permute-start.1) | collective-permute-done | bytes 49184 | tf_op jit(solution)/shard_map/ppermute | solution.py:29
  41.0 0.6 shard_map.89
  41.5 0.9 %all-to-all-done.1.sums = f32[8,16,256]{2,1,0:T(8,128)S(1)} async-done(((f32[8,16,256]{2,1,0:T(8,128)}), f32[8,16,256]{2,1,0:T(8,128)S(1)}, u32[]{:S(2)}, u32[]{:S(2)}) %all-to-all-start.1) | async-done | bytes 131104 | tf_op jit(solution)/shard_map/all_to_all | solution.py:465
  42.5 1.1 %shard_map.90 = (f32[2,256]{1,0:T(2,128)S(1)}, f32[2,32,256]{2,1,0:T(8,128)S(1)}, f32[2,8,256]{2,1,0:T(8,128)S(1)}, f32[2,8,256]{2,1,0:T(8,128)S(1)}) custom-call(f32[8,16,256]{2,1,0:T(8,128)S(1)} %all-to-all-done.1.sums, s32[3,32,128]{2,1,0:T(8,128)S(1)} %collective-permute-done.1.left_table, s32[3,32,128]{2,1,0:T(8,128)S(1)} %get-tuple-element.30.own_table, ...), custom_call_target="tpu_custom_call" | custom-call | tf_op jit(solution)/shard_map/pallas_call | solution.py:405
  43.6 4.5 %collective-permute-start.3 = (f32[2,8,256]{2,1,0:T(8,128)S(1)}, f32[2,8,256]{2,1,0:T(8,128)S(1)}, u32[]{:S(2)}, u32[]{:S(2)}) collective-permute-start(f32[2,8,256]{2,1,0:T(8,128)S(1)} %get-tuple-element.36), channel_id=1, source_target_pairs={{8,16},{24,32},{40,48},{56,64},{72,80},{88,96},{104,112},{16,8},{3... | collective-permute-start | bytes 49160 | tf_op jit(solution)/shard_map/ppermute | solution.py:48
  48.1 3.3 %all-gather.1 = f32[4,8,256]{2,1,0:T(8,128)S(1)} all-gather(f32[2,8,256]{2,1,0:T(8,128)S(1)} %get-tuple-element.35), channel_id=3, replica_groups={{0,8},{16,24},{32,40},{48,56},{64,72},{80,88},{96,104},{112,120},{1,9},..., dimensions={0}, use_global_device_ids=true | all-gather | bytes 49152 | tf_op jit(solution)/shard_map/all_gather | solution.py:50
  51.4 0.3 collective-permute-done.3.other
  51.7 1.2 %shard_map.91 = (f32[4,16]{1,0:T(4,128)S(1)}, f32[2,256]{1,0:T(2,128)}) custom-call(f32[2,32,256]{2,1,0:T(8,128)S(1)} %get-tuple-element.34.adj, f32[2,2,8,256]{3,2,1,0:T(8,128)S(1)} %bitcast.10, f32[2,8,256]{2,1,0:T(8,128)S(1)} %collective-permute-done.3.other, f32[2,48,256]{2,1,0:T(8,128)S(1)} %get-tuple-element.37.window, ...), custom_call_target="tpu_custom_call" | custom-call | tf_op jit(solution)/shard_map/pallas_call | solution.py:405
  52.9 10.4 %all-gather.3 = f32[4,4,16]{2,1,0:T(4,128)S(1)} all-gather(f32[1,4,16]{2,1,0:T(4,128)S(1)} %bitcast.11), channel_id=4, replica_groups=mesh['member'=4,'gx'=16,'gy'=8] {'member'}, dimensions={0}, use_global_device_ids=true | all-gather | bytes 1280 | tf_op jit(solution)/shard_map/all_gather | solution.py:499
  63.3 0.6 reduce_sum.9
Async XLA Ops:
  18.6 9.7 %collective-permute-start = (f32[4,8,256]{2,1,0:T(8,128)S(1)}, f32[4,8,256]{2,1,0:T(8,128)S(1)}, u32[]{:S(2)}, u32[]{:S(2)}) collective-permute-start(f32[4,8,256]{2,1,0:T(8,128)S(1)} %get-tuple-element.26), channel_id=1, source_target_pairs={{8,16},{24,32},{40,48},{56,64},{72,80},{88,96},{104,112},{16,8},{3... | collective-permute-start | bytes 98312 | tf_op jit(solution)/shard_map/ppermute | solution.py:48
  31.1 11.3 %all-to-all-start.1 = ((f32[8,16,256]{2,1,0:T(8,128)}), f32[8,16,256]{2,1,0:T(8,128)S(1)}, u32[]{:S(2)}, u32[]{:S(2)}) async-start(f32[8,16,256]{2,1,0:T(8,128)} %get-tuple-element.29), calls=%async_computation.1 | async-start | bytes 262144 | tf_op jit(solution)/shard_map/all_to_all | solution.py:465
  34.5 5.3 %collective-permute-start.2 = (s32[3,32,128]{2,1,0:T(8,128)S(1)}, s32[3,32,128]{2,1,0:T(8,128)S(1)}, u32[]{:S(2)}, u32[]{:S(2)}) collective-permute-start(s32[3,32,128]{2,1,0:T(8,128)S(1)} %get-tuple-element.30.own_table), channel_id=1, source_target_pairs={{1,0},{2,1},{3,2},{4,3},{5,4},{6,5},{7,6},{9,8},{10,9},{11,10},{12... | collective-permute-start | bytes 147464 | tf_op jit(solution)/shard_map/ppermute | solution.py:29
  35.8 5.2 %collective-permute-start.1 = (s32[3,32,128]{2,1,0:T(8,128)S(1)}, s32[3,32,128]{2,1,0:T(8,128)S(1)}, u32[]{:S(2)}, u32[]{:S(2)}) collective-permute-start(s32[3,32,128]{2,1,0:T(8,128)S(1)} %get-tuple-element.30.own_table), channel_id=1, source_target_pairs={{0,1},{1,2},{2,3},{3,4},{4,5},{5,6},{6,7},{8,9},{9,10},{10,11},{11... | collective-permute-start | bytes 147464 | tf_op jit(solution)/shard_map/ppermute | solution.py:29
  43.6 8.1 %collective-permute-start.3 = (f32[2,8,256]{2,1,0:T(8,128)S(1)}, f32[2,8,256]{2,1,0:T(8,128)S(1)}, u32[]{:S(2)}, u32[]{:S(2)}) collective-permute-start(f32[2,8,256]{2,1,0:T(8,128)S(1)} %get-tuple-element.36), channel_id=1, source_target_pairs={{8,16},{24,32},{40,48},{56,64},{72,80},{88,96},{104,112},{16,8},{3... | collective-permute-start | bytes 49160 | tf_op jit(solution)/shard_map/ppermute | solution.py:48

commit v8 on v6

--- a/solution.py
+++ b/solution.py
@@ -494,7 +494,7 @@
         (),
         [pltpu.SemaphoreType.DMA((1,))],
     )
-    gradient = jnp.sum(lax.all_gather(coarse, "member"), axis=0)
+    gradient = lax.psum(coarse, "member")
     return (misfit[None, None, None], gradient)
 
 

time: 64.4 us -> 64.5 us (level)
  blocking collectives: 34.3 us -> 35 us
    psum x0 -> x1, blocking collectives: none -> 11.1 us  [per_device(): gradient = lax.psum(coarse, 'member')]
    all_gather x1 -> x0, blocking collectives: 10.4 us -> none  [per_device(): gradient = jnp.sum(lax.all_gather(coarse, 'member'), axis=0)]
where the time goes in v8:
time: 64.5 us; the launch traced here: 64 us
  blocking collectives  35 us (54%)
  starting transfers between devices  19.1 us (30%)
  Pallas kernels  6.87 us (11%)
  waiting for transfers between devices  2.37 us (4%)
  between operations  0.72 us (1%)
    all_to_all x1, blocking collectives, per_device(): received = lax.all_to_all(packed, 'gy', 0, 0, tiled=True)  16.9 us
    psum x1, blocking collectives, per_device(): gradient = lax.psum(coarse, 'member')  11.1 us
    ppermute x2, starting transfers between devices, exchange_rows(): other = lax.ppermute(to_other, 'gx', swaps + [(j, i) for i, j in swaps])  10.5 us
    all_gather x2, blocking collectives, exchange_rows(): pair = lax.all_gather(to_pair, 'gx', axis_index_groups=groups)  7 us
    pallas_call x6, Pallas kernels, call(): pl.pallas_call(kernel, out_shape=tuple(outs), in_specs=[near] * len(args)...  6.87 us
    ppermute x2, starting transfers between devices, from_behind(): return lax.ppermute(x, axis, pairs)  5.28 us
    all_to_all x1, starting transfers between devices, per_device(): sums = lax.all_to_all(sums, 'gy', 0, 0, tiled=True)  3.38 us
  transfers between devices with their start and end apart: 5, of which 3 were waited for; matrix products, arithmetic and copies ran while one was open for 0% of the time, Pallas kernels for 1%

profile of v8, /device:TPU:7, one launch (start us, length us, event | category | flops | bytes accessed | tf_op | source)
XLA Modules:
  0.0 64.0 jit_solution(11171003052013616486)
XLA Ops:
  0.6 1.1 %shard_map.86 = (f32[8,3,4,128]{3,2,1,0:T(4,128)S(1)}, f32[4,32,128]{2,1,0:T(8,128)S(1)}, s32[2,32,128]{2,1,0:T(8,128)S(1)}, f32[2,256]{1,0:T(2,128)S(1)}) custom-call(f32[2,32,128]{2,1,0:T(8,128)} %bitcast.10, f32[4,16]{1,0:T(4,128)} %strength_in.1, s32[32,128]{1,0:T(8,128)} %mask_in.1, s32[32,128]{1,0:T(8,128)} %bitcast.11, s32[32,128]{1,0:T(8,128)} %bitcast.12, ...), custom_call_target="tpu_custom_call" | custom-call | tf_op jit(solution)/shard_map/pallas_call | solution.py:403
  1.7 16.9 %all_to_all.10.received = f32[8,3,4,128]{3,2,1,0:T(4,128)S(1)} all-to-all(f32[8,3,4,128]{3,2,1,0:T(4,128)S(1)} %get-tuple-element.22), channel_id=1, replica_groups=mesh['member'=4,'gx'=16,'gy'=8] {'gy'}, dimensions={0} | all-to-all | bytes 98304 | tf_op jit(solution)/shard_map/all_to_all | solution.py:438
  18.6 0.1 shard_map.87
  18.7 5.9 %collective-permute-start = (f32[4,8,256]{2,1,0:T(8,128)S(1)}, f32[4,8,256]{2,1,0:T(8,128)S(1)}, u32[]{:S(2)}, u32[]{:S(2)}) collective-permute-start(f32[4,8,256]{2,1,0:T(8,128)S(1)} %get-tuple-element.26), channel_id=1, source_target_pairs={{8,16},{24,32},{40,48},{56,64},{72,80},{88,96},{104,112},{16,8},{3... | collective-permute-start | bytes 98312 | tf_op jit(solution)/shard_map/ppermute | solution.py:48
  24.6 3.7 %all-gather = f32[8,8,256]{2,1,0:T(8,128)S(1)} all-gather(f32[4,8,256]{2,1,0:T(8,128)S(1)} %get-tuple-element.25), channel_id=2, replica_groups={{0,8},{16,24},{32,40},{48,56},{64,72},{80,88},{96,104},{112,120},{1,9},..., dimensions={0}, use_global_device_ids=true | all-gather | bytes 98304 | tf_op jit(solution)/shard_map/all_gather | solution.py:50
  28.4 0.0 collective-permute-done.other
  28.4 2.8 %shard_map.88 = (f32[8,16,256]{2,1,0:T(8,128)}, f32[7,3,32,128]{3,2,1,0:T(8,128)S(1)}, f32[2,48,256]{2,1,0:T(8,128)S(1)}, s32[3,32,128]{2,1,0:T(8,128)S(1)}) custom-call(f32[4,32,256]{2,1,0:T(8,128)S(1)} %get-tuple-element.24.ext, f32[2,4,8,256]{3,2,1,0:T(8,128)S(1)} %bitcast.8, f32[4,8,256]{2,1,0:T(8,128)S(1)} %collective-permute-done.other, ...), custom_call_target="tpu_custom_call" | custom-call | tf_op jit(solution)/shard_map/pallas_call | solution.py:403
  31.2 3.4 %all-to-all-start.1 = ((f32[8,16,256]{2,1,0:T(8,128)}), f32[8,16,256]{2,1,0:T(8,128)S(1)}, u32[]{:S(2)}, u32[]{:S(2)}) async-start(f32[8,16,256]{2,1,0:T(8,128)} %get-tuple-element.29), calls=%async_computation.1 | async-start | bytes 262144 | tf_op jit(solution)/shard_map/all_to_all | solution.py:463
  34.6 1.3 %collective-permute-start.2 = (s32[3,32,128]{2,1,0:T(8,128)S(1)}, s32[3,32,128]{2,1,0:T(8,128)S(1)}, u32[]{:S(2)}, u32[]{:S(2)}) collective-permute-start(s32[3,32,128]{2,1,0:T(8,128)S(1)} %get-tuple-element.30.own_table), channel_id=1, source_target_pairs={{1,0},{2,1},{3,2},{4,3},{5,4},{6,5},{7,6},{9,8},{10,9},{11,10},{12... | collective-permute-start | bytes 147464 | tf_op jit(solution)/shard_map/ppermute | solution.py:29
  35.9 4.0 %collective-permute-start.1 = (s32[3,32,128]{2,1,0:T(8,128)S(1)}, s32[3,32,128]{2,1,0:T(8,128)S(1)}, u32[]{:S(2)}, u32[]{:S(2)}) collective-permute-start(s32[3,32,128]{2,1,0:T(8,128)S(1)} %get-tuple-element.30.own_table), channel_id=1, source_target_pairs={{0,1},{1,2},{2,3},{3,4},{4,5},{5,6},{6,7},{8,9},{9,10},{10,11},{11... | collective-permute-start | bytes 147464 | tf_op jit(solution)/shard_map/ppermute | solution.py:29
  39.9 0.0 collective-permute-done.2.right_table
  39.9 1.1 %collective-permute-done.1.left_table = s32[3,32,128]{2,1,0:T(8,128)S(1)} collective-permute-done((s32[3,32,128]{2,1,0:T(8,128)S(1)}, s32[3,32,128]{2,1,0:T(8,128)S(1)}, u32[]{:S(2)}, u32[]{:S(2)}) %collective-permute-start.1) | collective-permute-done | bytes 49184 | tf_op jit(solution)/shard_map/ppermute | solution.py:29
  41.0 0.6 shard_map.89
  41.6 0.9 %all-to-all-done.1.sums = f32[8,16,256]{2,1,0:T(8,128)S(1)} async-done(((f32[8,16,256]{2,1,0:T(8,128)}), f32[8,16,256]{2,1,0:T(8,128)S(1)}, u32[]{:S(2)}, u32[]{:S(2)}) %all-to-all-start.1) | async-done | bytes 131104 | tf_op jit(solution)/shard_map/all_to_all | solution.py:463
  42.5 1.1 %shard_map.90 = (f32[2,256]{1,0:T(2,128)S(1)}, f32[2,32,256]{2,1,0:T(8,128)S(1)}, f32[2,8,256]{2,1,0:T(8,128)S(1)}, f32[2,8,256]{2,1,0:T(8,128)S(1)}) custom-call(f32[8,16,256]{2,1,0:T(8,128)S(1)} %all-to-all-done.1.sums, s32[3,32,128]{2,1,0:T(8,128)S(1)} %collective-permute-done.1.left_table, s32[3,32,128]{2,1,0:T(8,128)S(1)} %get-tuple-element.30.own_table, ...), custom_call_target="tpu_custom_call" | custom-call | tf_op jit(solution)/shard_map/pallas_call | solution.py:403
  43.7 4.5 %collective-permute-start.3 = (f32[2,8,256]{2,1,0:T(8,128)S(1)}, f32[2,8,256]{2,1,0:T(8,128)S(1)}, u32[]{:S(2)}, u32[]{:S(2)}) collective-permute-start(f32[2,8,256]{2,1,0:T(8,128)S(1)} %get-tuple-element.36), channel_id=1, source_target_pairs={{8,16},{24,32},{40,48},{56,64},{72,80},{88,96},{104,112},{16,8},{3... | collective-permute-start | bytes 49160 | tf_op jit(solution)/shard_map/ppermute | solution.py:48
  48.2 3.3 %all-gather.1 = f32[4,8,256]{2,1,0:T(8,128)S(1)} all-gather(f32[2,8,256]{2,1,0:T(8,128)S(1)} %get-tuple-element.35), channel_id=3, replica_groups={{0,8},{16,24},{32,40},{48,56},{64,72},{80,88},{96,104},{112,120},{1,9},..., dimensions={0}, use_global_device_ids=true | all-gather | bytes 49152 | tf_op jit(solution)/shard_map/all_gather | solution.py:50
  51.5 0.3 collective-permute-done.3.other
  51.8 1.2 %shard_map.91 = (f32[4,16]{1,0:T(4,128)S(1)}, f32[2,256]{1,0:T(2,128)}) custom-call(f32[2,32,256]{2,1,0:T(8,128)S(1)} %get-tuple-element.34.adj, f32[2,2,8,256]{3,2,1,0:T(8,128)S(1)} %bitcast.9, f32[2,8,256]{2,1,0:T(8,128)S(1)} %collective-permute-done.3.other, f32[2,48,256]{2,1,0:T(8,128)S(1)} %get-tuple-element.37.window, ...), custom_call_target="tpu_custom_call" | custom-call | tf_op jit(solution)/shard_map/pallas_call | solution.py:403
  53.0 11.1 %psum.7 = f32[4,16]{1,0:T(4,128)} all-reduce(f32[4,16]{1,0:T(4,128)S(1)} %get-tuple-element.41), channel_id=1, replica_groups=mesh['member'=4,'gx'=16,'gy'=8] {'member'}, use_global_device_ids=true, to_apply=%region_0.0 | all-reduce | flops 64 | bytes 512 | tf_op jit(solution)/shard_map/psum | solution.py:497
Async XLA Ops:
  18.7 9.7 %collective-permute-start = (f32[4,8,256]{2,1,0:T(8,128)S(1)}, f32[4,8,256]{2,1,0:T(8,128)S(1)}, u32[]{:S(2)}, u32[]{:S(2)}) collective-permute-start(f32[4,8,256]{2,1,0:T(8,128)S(1)} %get-tuple-element.26), channel_id=1, source_target_pairs={{8,16},{24,32},{40,48},{56,64},{72,80},{88,96},{104,112},{16,8},{3... | collective-permute-start | bytes 98312 | tf_op jit(solution)/shard_map/ppermute | solution.py:48
  31.2 11.3 %all-to-all-start.1 = ((f32[8,16,256]{2,1,0:T(8,128)}), f32[8,16,256]{2,1,0:T(8,128)S(1)}, u32[]{:S(2)}, u32[]{:S(2)}) async-start(f32[8,16,256]{2,1,0:T(8,128)} %get-tuple-element.29), calls=%async_computation.1 | async-start | bytes 262144 | tf_op jit(solution)/shard_map/all_to_all | solution.py:463
  34.6 5.3 %collective-permute-start.2 = (s32[3,32,128]{2,1,0:T(8,128)S(1)}, s32[3,32,128]{2,1,0:T(8,128)S(1)}, u32[]{:S(2)}, u32[]{:S(2)}) collective-permute-start(s32[3,32,128]{2,1,0:T(8,128)S(1)} %get-tuple-element.30.own_table), channel_id=1, source_target_pairs={{1,0},{2,1},{3,2},{4,3},{5,4},{6,5},{7,6},{9,8},{10,9},{11,10},{12... | collective-permute-start | bytes 147464 | tf_op jit(solution)/shard_map/ppermute | solution.py:29
  35.9 5.2 %collective-permute-start.1 = (s32[3,32,128]{2,1,0:T(8,128)S(1)}, s32[3,32,128]{2,1,0:T(8,128)S(1)}, u32[]{:S(2)}, u32[]{:S(2)}) collective-permute-start(s32[3,32,128]{2,1,0:T(8,128)S(1)} %get-tuple-element.30.own_table), channel_id=1, source_target_pairs={{0,1},{1,2},{2,3},{3,4},{4,5},{5,6},{6,7},{8,9},{9,10},{10,11},{11... | collective-permute-start | bytes 147464 | tf_op jit(solution)/shard_map/ppermute | solution.py:29
  43.7 8.1 %collective-permute-start.3 = (f32[2,8,256]{2,1,0:T(8,128)S(1)}, f32[2,8,256]{2,1,0:T(8,128)S(1)}, u32[]{:S(2)}, u32[]{:S(2)}) collective-permute-start(f32[2,8,256]{2,1,0:T(8,128)S(1)} %get-tuple-element.36), channel_id=1, source_target_pairs={{8,16},{24,32},{40,48},{56,64},{72,80},{88,96},{104,112},{16,8},{3... | collective-permute-start | bytes 49160 | tf_op jit(solution)/shard_map/ppermute | solution.py:48

commit v9 on v7

--- a/solution.py
+++ b/solution.py
@@ -162,8 +162,7 @@
     return pltpu.roll(x, 1, 1)
 
 
-def forward_kernel(ext, pair, other, received, table, observed, sums, rates, window, table_out, vel, kept, hot, total, sems):
-    b = lax.axis_index("gy")
+def slot_kernel(received, table, table_out, hot):
     slot_ids = iota((COLS, COLS), 0)
     slots = jnp.concatenate([received[d, 2] for d in range(OWNERS)], axis=0).astype(jnp.int32)
     table_out[0] = table[0]
@@ -172,6 +171,10 @@
     for i in range(ROWS):
         at = slice(COLS * i, COLS * i + COLS)
         hot[:, at] = (slot_ids == slots[i : i + 1, :] % COLS).astype(f32).astype(bf16)
+
+
+def forward_kernel(ext, pair, other, table, hot, observed, sums, rates, window, vel, kept, total, sems):
+    b = lax.axis_index("gy")
     fields = []
     for f in range(4):
         above, below = above_below(pair, other, f)
@@ -218,6 +221,7 @@
     vel[1] = v[own, :COLS]
 
     cell = table[0]
+    slots = table[2]
     row, col = cell // COLS, cell % COLS
     got_u = jnp.zeros((ROWS, COLS), f32)
     got_v = jnp.zeros((ROWS, COLS), f32)
@@ -444,23 +448,22 @@
         (received, own),
     )
     pair, other = exchange_rows(to_pair, to_other)
-    sums, rates, window, table = call(
+    table, slot_hot = call(
+        slot_kernel,
+        [near(3, ROWS, COLS, dtype=jnp.int32), near(COLS, entries, dtype=bf16)],
+        (received, table),
+        cost=10**9,
+    )
+    sums, rates, window = call(
         forward_kernel,
         [
             pltpu.HBM((OWNERS, 2 * OWNERS, BUOYS), f32),
             near(SUBCYCLES - 1, 3, ROWS, COLS),
             near(2, WIN, 2 * COLS),
-            near(3, ROWS, COLS, dtype=jnp.int32),
         ],
-        (ext, pair, other, received, table, observed),
+        (ext, pair, other, table, slot_hot, observed),
         (),
-        [
-            near(2, ROWS, COLS),
-            near(8 * ROWS, COLS),
-            near(COLS, entries, dtype=bf16),
-            near(2 * OWNERS, BUOYS),
-            pltpu.SemaphoreType.DMA((OWNERS,)),
-        ],
+        [near(2, ROWS, COLS), near(8 * ROWS, COLS), near(2 * OWNERS, BUOYS), pltpu.SemaphoreType.DMA((OWNERS,))],
     )
     sums = lax.all_to_all(sums, "gy", 0, 0, tiled=True)
     left_table = from_behind(table, "gy", 1)

time: 64.3 us -> 64.5 us (level)
    pallas_call x6 -> x7, Pallas kernels: 6.8 us -> 6.92 us  [call(): pl.pallas_call(kernel, out_shape=tuple(outs), in_specs=[near] * len(args)...]
where the time goes in v9:
time: 64.5 us; the launch traced here: 64.1 us
  blocking collectives  34.3 us (53%)
  starting transfers between devices  18.8 us (29%)
  Pallas kernels  6.92 us (11%)
  waiting for transfers between devices  2.64 us (4%)
  between operations  0.73 us (1%)
    all_to_all x1, blocking collectives, per_device(): received = lax.all_to_all(packed, 'gy', 0, 0, tiled=True)  16.9 us
    all_gather x1, blocking collectives, per_device(): gradient = jnp.sum(lax.all_gather(coarse, 'member'), axis=0)  10.4 us
    ppermute x2, starting transfers between devices, exchange_rows(): other = lax.ppermute(to_other, 'gx', swaps + [(j, i) for i, j in swaps])  10.2 us
    all_gather x2, blocking collectives, exchange_rows(): pair = lax.all_gather(to_pair, 'gx', axis_index_groups=groups)  7 us
    pallas_call x7, Pallas kernels, call(): pl.pallas_call(kernel, out_shape=tuple(outs), in_specs=[near] * len(args)...  6.92 us
    ppermute x2, starting transfers between devices, from_behind(): return lax.ppermute(x, axis, pairs)  5.28 us
    all_to_all x1, starting transfers between devices, per_device(): sums = lax.all_to_all(sums, 'gy', 0, 0, tiled=True)  3.38 us
  transfers between devices with their start and end apart: 5, of which 3 were waited for; matrix products, arithmetic and copies ran while one was open for 0% of the time, Pallas kernels for 1%

profile of v9, /device:TPU:7, one launch (start us, length us, event | category | flops | bytes accessed | tf_op | source)
XLA Modules:
  0.0 64.1 jit_solution(13750443752769239063)
XLA Ops:
  0.6 1.0 %shard_map.86 = (f32[8,3,4,128]{3,2,1,0:T(4,128)S(1)}, f32[4,32,128]{2,1,0:T(8,128)S(1)}, s32[2,32,128]{2,1,0:T(8,128)S(1)}, f32[2,256]{1,0:T(2,128)S(1)}) custom-call(f32[2,32,128]{2,1,0:T(8,128)} %bitcast.12, f32[4,16]{1,0:T(4,128)} %strength_in.1, s32[32,128]{1,0:T(8,128)} %mask_in.1, s32[32,128]{1,0:T(8,128)} %bitcast.13, s32[32,128]{1,0:T(8,128)} %bitcast.14, ...), custom_call_target="tpu_custom_call" | custom-call | tf_op jit(solution)/shard_map/pallas_call | solution.py:409
  1.6 16.9 %all_to_all.10.received = f32[8,3,4,128]{3,2,1,0:T(4,128)S(1)} all-to-all(f32[8,3,4,128]{3,2,1,0:T(4,128)S(1)} %get-tuple-element.23), channel_id=1, replica_groups=mesh['member'=4,'gx'=16,'gy'=8] {'gy'}, dimensions={0} | all-to-all | bytes 98304 | tf_op jit(solution)/shard_map/all_to_all | solution.py:444
  18.5 0.1 shard_map.87
  18.6 5.9 %collective-permute-start = (f32[4,8,256]{2,1,0:T(8,128)S(1)}, f32[4,8,256]{2,1,0:T(8,128)S(1)}, u32[]{:S(2)}, u32[]{:S(2)}) collective-permute-start(f32[4,8,256]{2,1,0:T(8,128)S(1)} %get-tuple-element.27), channel_id=1, source_target_pairs={{8,16},{24,32},{40,48},{56,64},{72,80},{88,96},{104,112},{16,8},{3... | collective-permute-start | bytes 98312 | tf_op jit(solution)/shard_map/ppermute | solution.py:48
  24.6 0.3 shard_map.88
  24.8 3.7 %all-gather = f32[8,8,256]{2,1,0:T(8,128)S(1)} all-gather(f32[4,8,256]{2,1,0:T(8,128)S(1)} %get-tuple-element.26), channel_id=2, replica_groups={{0,8},{16,24},{32,40},{48,56},{64,72},{80,88},{96,104},{112,120},{1,9},..., dimensions={0}, use_global_device_ids=true | all-gather | bytes 98304 | tf_op jit(solution)/shard_map/all_gather | solution.py:50
  28.6 0.0 collective-permute-done.other
  28.6 2.7 %shard_map.89 = (f32[8,16,256]{2,1,0:T(8,128)}, f32[7,3,32,128]{3,2,1,0:T(8,128)S(1)}, f32[2,48,256]{2,1,0:T(8,128)S(1)}) custom-call(f32[4,32,256]{2,1,0:T(8,128)S(1)} %get-tuple-element.25.ext, f32[2,4,8,256]{3,2,1,0:T(8,128)S(1)} %bitcast.9, f32[4,8,256]{2,1,0:T(8,128)S(1)} %collective-permute-done.other, ...), custom_call_target="tpu_custom_call" | custom-call | tf_op jit(solution)/shard_map/pallas_call | solution.py:409
  31.3 3.4 %all-to-all-start.1 = ((f32[8,16,256]{2,1,0:T(8,128)}), f32[8,16,256]{2,1,0:T(8,128)S(1)}, u32[]{:S(2)}, u32[]{:S(2)}) async-start(f32[8,16,256]{2,1,0:T(8,128)} %get-tuple-element.32), calls=%async_computation.1 | async-start | bytes 262144 | tf_op jit(solution)/shard_map/all_to_all | solution.py:468
  34.6 1.3 %collective-permute-start.2 = (s32[3,32,128]{2,1,0:T(8,128)S(1)}, s32[3,32,128]{2,1,0:T(8,128)S(1)}, u32[]{:S(2)}, u32[]{:S(2)}) collective-permute-start(s32[3,32,128]{2,1,0:T(8,128)S(1)} %get-tuple-element.29.table.own_table), channel_id=1, source_target_pairs={{1,0},{2,1},{3,2},{4,3},{5,4},{6,5},{7,6},{9,8},{10,9},{11,10},{12... | collective-permute-start | bytes 147464 | tf_op jit(solution)/shard_map/ppermute | solution.py:29
  35.9 4.0 %collective-permute-start.1 = (s32[3,32,128]{2,1,0:T(8,128)S(1)}, s32[3,32,128]{2,1,0:T(8,128)S(1)}, u32[]{:S(2)}, u32[]{:S(2)}) collective-permute-start(s32[3,32,128]{2,1,0:T(8,128)S(1)} %get-tuple-element.29.table.own_table), channel_id=1, source_target_pairs={{0,1},{1,2},{2,3},{3,4},{4,5},{5,6},{6,7},{8,9},{9,10},{10,11},{11... | collective-permute-start | bytes 147464 | tf_op jit(solution)/shard_map/ppermute | solution.py:29
  39.9 0.0 collective-permute-done.2.right_table
  40.0 1.1 %collective-permute-done.1.left_table = s32[3,32,128]{2,1,0:T(8,128)S(1)} collective-permute-done((s32[3,32,128]{2,1,0:T(8,128)S(1)}, s32[3,32,128]{2,1,0:T(8,128)S(1)}, u32[]{:S(2)}, u32[]{:S(2)}) %collective-permute-start.1) | collective-permute-done | bytes 49184 | tf_op jit(solution)/shard_map/ppermute | solution.py:29
  41.1 0.6 shard_map.90
  41.7 0.9 %all-to-all-done.1.sums = f32[8,16,256]{2,1,0:T(8,128)S(1)} async-done(((f32[8,16,256]{2,1,0:T(8,128)}), f32[8,16,256]{2,1,0:T(8,128)S(1)}, u32[]{:S(2)}, u32[]{:S(2)}) %all-to-all-start.1) | async-done | bytes 131104 | tf_op jit(solution)/shard_map/all_to_all | solution.py:468
  42.6 1.1 %shard_map.91 = (f32[2,256]{1,0:T(2,128)S(1)}, f32[2,32,256]{2,1,0:T(8,128)S(1)}, f32[2,8,256]{2,1,0:T(8,128)S(1)}, f32[2,8,256]{2,1,0:T(8,128)S(1)}) custom-call(f32[8,16,256]{2,1,0:T(8,128)S(1)} %all-to-all-done.1.sums, s32[3,32,128]{2,1,0:T(8,128)S(1)} %collective-permute-done.1.left_table, s32[3,32,128]{2,1,0:T(8,128)S(1)} %get-tuple-element.29.table.own_table, ...), custom_call_target="tpu_custom_call" | custom-call | tf_op jit(solution)/shard_map/pallas_call | solution.py:409
  43.7 4.2 %collective-permute-start.3 = (f32[2,8,256]{2,1,0:T(8,128)S(1)}, f32[2,8,256]{2,1,0:T(8,128)S(1)}, u32[]{:S(2)}, u32[]{:S(2)}) collective-permute-start(f32[2,8,256]{2,1,0:T(8,128)S(1)} %get-tuple-element.38), channel_id=1, source_target_pairs={{8,16},{24,32},{40,48},{56,64},{72,80},{88,96},{104,112},{16,8},{3... | collective-permute-start | bytes 49160 | tf_op jit(solution)/shard_map/ppermute | solution.py:48
  48.0 3.3 %all-gather.1 = f32[4,8,256]{2,1,0:T(8,128)S(1)} all-gather(f32[2,8,256]{2,1,0:T(8,128)S(1)} %get-tuple-element.37), channel_id=3, replica_groups={{0,8},{16,24},{32,40},{48,56},{64,72},{80,88},{96,104},{112,120},{1,9},..., dimensions={0}, use_global_device_ids=true | all-gather | bytes 49152 | tf_op jit(solution)/shard_map/all_gather | solution.py:50
  51.2 0.6 collective-permute-done.3.other
  51.8 1.2 %shard_map.92 = (f32[4,16]{1,0:T(4,128)S(1)}, f32[2,256]{1,0:T(2,128)}) custom-call(f32[2,32,256]{2,1,0:T(8,128)S(1)} %get-tuple-element.36.adj, f32[2,2,8,256]{3,2,1,0:T(8,128)S(1)} %bitcast.10, f32[2,8,256]{2,1,0:T(8,128)S(1)} %collective-permute-done.3.other, f32[2,48,256]{2,1,0:T(8,128)S(1)} %get-tuple-element.39.window, ...), custom_call_target="tpu_custom_call" | custom-call | tf_op jit(solution)/shard_map/pallas_call | solution.py:409
  53.0 10.4 %all-gather.3 = f32[4,4,16]{2,1,0:T(4,128)S(1)} all-gather(f32[1,4,16]{2,1,0:T(4,128)S(1)} %bitcast.11), channel_id=4, replica_groups=mesh['member'=4,'gx'=16,'gy'=8] {'member'}, dimensions={0}, use_global_device_ids=true | all-gather | bytes 1280 | tf_op jit(solution)/shard_map/all_gather | solution.py:502
  63.5 0.6 reduce_sum.9
Async XLA Ops:
  18.6 10.0 %collective-permute-start = (f32[4,8,256]{2,1,0:T(8,128)S(1)}, f32[4,8,256]{2,1,0:T(8,128)S(1)}, u32[]{:S(2)}, u32[]{:S(2)}) collective-permute-start(f32[4,8,256]{2,1,0:T(8,128)S(1)} %get-tuple-element.27), channel_id=1, source_target_pairs={{8,16},{24,32},{40,48},{56,64},{72,80},{88,96},{104,112},{16,8},{3... | collective-permute-start | bytes 98312 | tf_op jit(solution)/shard_map/ppermute | solution.py:48
  31.3 11.3 %all-to-all-start.1 = ((f32[8,16,256]{2,1,0:T(8,128)}), f32[8,16,256]{2,1,0:T(8,128)S(1)}, u32[]{:S(2)}, u32[]{:S(2)}) async-start(f32[8,16,256]{2,1,0:T(8,128)} %get-tuple-element.32), calls=%async_computation.1 | async-start | bytes 262144 | tf_op jit(solution)/shard_map/all_to_all | solution.py:468
  34.6 5.3 %collective-permute-start.2 = (s32[3,32,128]{2,1,0:T(8,128)S(1)}, s32[3,32,128]{2,1,0:T(8,128)S(1)}, u32[]{:S(2)}, u32[]{:S(2)}) collective-permute-start(s32[3,32,128]{2,1,0:T(8,128)S(1)} %get-tuple-element.29.table.own_table), channel_id=1, source_target_pairs={{1,0},{2,1},{3,2},{4,3},{5,4},{6,5},{7,6},{9,8},{10,9},{11,10},{12... | collective-permute-start | bytes 147464 | tf_op jit(solution)/shard_map/ppermute | solution.py:29
  35.9 5.2 %collective-permute-start.1 = (s32[3,32,128]{2,1,0:T(8,128)S(1)}, s32[3,32,128]{2,1,0:T(8,128)S(1)}, u32[]{:S(2)}, u32[]{:S(2)}) collective-permute-start(s32[3,32,128]{2,1,0:T(8,128)S(1)} %get-tuple-element.29.table.own_table), channel_id=1, source_target_pairs={{0,1},{1,2},{2,3},{3,4},{4,5},{5,6},{6,7},{8,9},{9,10},{10,11},{11... | collective-permute-start | bytes 147464 | tf_op jit(solution)/shard_map/ppermute | solution.py:29
  43.7 8.1 %collective-permute-start.3 = (f32[2,8,256]{2,1,0:T(8,128)S(1)}, f32[2,8,256]{2,1,0:T(8,128)S(1)}, u32[]{:S(2)}, u32[]{:S(2)}) collective-permute-start(f32[2,8,256]{2,1,0:T(8,128)S(1)} %get-tuple-element.38), channel_id=1, source_target_pairs={{8,16},{24,32},{40,48},{56,64},{72,80},{88,96},{104,112},{16,8},{3... | collective-permute-start | bytes 49160 | tf_op jit(solution)/shard_map/ppermute | solution.py:48
